TPU v7x, 32 devices: a whole 2x2x4 slice. The times are simulated.
32 devices in a mesh: grp: 2 (over y), shot: 4 (over z), sub: 4 (over x, core).
Axes of the slice: x: 2, y: 2, z: 4, core: 2. Of those that a mesh axis runs over, the one named last changes fastest.
Arguments:
- velocity: float32 [64, 64, 256], P(('grp', 'shot'), 'sub'), parts along dimension 0, may hold values from 1.5 to 4.5
- anchors: int32 [8], P(('grp', 'shot')), parts along dimension 0, may hold values from 0 to 3, as said below
- source_cells: int32 [8, 3], P(('grp', 'shot')), parts along dimension 0, may hold values from 0 to 255, as said below
- receiver_cells: int32 [8, 3, 256], P(('grp', 'shot')), parts along dimension 0, may hold values from 0 to 255, as said below
- wavelet: float32 [8, 2], P(('grp', 'shot')), parts along dimension 0, may hold values from -6 to 6
- residuals: float32 [8, 2, 256], P(('grp', 'shot')), parts along dimension 0, may hold values from -6 to 6
- forward_pair: float32 [8, 2, 32, 64, 256], P(('grp', 'shot'), None, None, 'sub'), parts along dimension 0, may hold values from -6 to 6
- adjoint_pair: float32 [8, 2, 32, 64, 256], P(('grp', 'shot'), None, None, 'sub'), parts along dimension 0, may hold values from -6 to 6
Outputs:
- gradient: float32 [64, 64, 256], P(('grp', 'shot'), 'sub'), parts along dimension 0
- forward_out: float32 [8, 2, 32, 64, 256], P(('grp', 'shot'), None, None, 'sub'), parts along dimension 0
- adjoint_out: float32 [8, 2, 32, 64, 256], P(('grp', 'shot'), None, None, 'sub'), parts along dimension 0
There are 2 independent parts, one for each index of `grp`. A program takes and returns all parts, laid end to end along the dimension named above; each array names one. Nothing has to cross between parts.
Inputs may be any that keep to these rules, and one draw needn't show every extreme that they name: anchors[s] = (s - k) mod 4 for some k between 0 and 3. `source_cells`: entries are an aperture first index below 32, a depth below 64 and a y index below 256. `receiver_cells`: entries are an aperture first index below 32, a depth below 16 and a y index below 256; cells may repeat.
All inputs are finite; a program needn't handle non-finite values.
Results may differ from a plain program's by a relative error of at most 0.0003.
Values sent between devices are 32-bit elements; how exact they have to be, the bound alone decides.
No kernel may reach another device: no remote copies, remote signals or barrier semaphores. Data moves between devices by JAX's collectives and lax.ppermute only.
A program may use at most 64 MiB of HBM per device.

v0:
```python
import jax
import jax.numpy as jnp
from jax import lax
from jax.sharding import PartitionSpec as P

APT = 4
STEPS = 2


STENCIL_COEFS = (-205.0 / 72.0, 8.0 / 5.0, -1.0 / 5.0, 8.0 / 315.0, -1.0 / 560.0)
SPACING_RATIO = 0.1


def extended(block, sides, width):
    for axis, dim in sides:
        count = lax.axis_size(axis)
        forward = [(i, i + 1) for i in range(count - 1)]
        backward = [(target, source) for source, target in forward]
        low = lax.ppermute(
            lax.slice_in_dim(block, block.shape[dim] - width, None, axis=dim), axis, forward
        )
        high = lax.ppermute(lax.slice_in_dim(block, 0, width, axis=dim), axis, backward)
        block = jnp.concatenate([low, block, high], axis=dim)
    return block


def passed_along(value, axis, steps):
    count = lax.axis_size(axis)
    pairs = [(source, (source + steps) % count) for source in range(count)]
    return lax.ppermute(value, axis, pairs)


def stencil(padded, field):
    rows_x, rows_z, rows_y = field.shape[-3:]
    total = 3.0 * STENCIL_COEFS[0] * field
    for offset in range(1, 5):
        along_x = (
            padded[..., 4 + offset : 4 + offset + rows_x, 4 : 4 + rows_z, 4 : 4 + rows_y]
            + padded[..., 4 - offset : 4 - offset + rows_x, 4 : 4 + rows_z, 4 : 4 + rows_y]
        )
        along_z = (
            padded[..., 4 : 4 + rows_x, 4 + offset : 4 + offset + rows_z, 4 : 4 + rows_y]
            + padded[..., 4 : 4 + rows_x, 4 - offset : 4 - offset + rows_z, 4 : 4 + rows_y]
        )
        along_y = (
            padded[..., 4 : 4 + rows_x, 4 : 4 + rows_z, 4 + offset : 4 + offset + rows_y]
            + padded[..., 4 : 4 + rows_x, 4 : 4 + rows_z, 4 - offset : 4 - offset + rows_y]
        )
        total = total + STENCIL_COEFS[offset] * (along_x + along_z + along_y)
    return total


def inject(field, first, depth, side, amount, depth_start):
    layers = field.shape[1]
    local_depth = depth - depth_start
    inside = (local_depth >= 0) & (local_depth < layers)
    local_depth = jnp.clip(local_depth, 0, layers - 1)
    return field.at[first, local_depth, side].add(jnp.where(inside, amount, 0.0))


def on_device(
    velocity, anchors, source_cells, receiver_cells, wavelet, residuals, forward_pair, adjoint_pair
):
    tile_rows = velocity.shape[0]
    reach_tiles = APT - 1
    aperture = APT * tile_rows
    shot_count = lax.axis_size("shot")
    shot_index = lax.axis_index("shot")
    anchor_tile = anchors[0]
    behind = (shot_index - anchor_tile + shot_count) % shot_count
    relative = 0 - behind
    frame_start = (relative + reach_tiles) * tile_rows
    whole = lax.all_gather(velocity, "shot", axis=0, tiled=True)
    model_rows = tile_rows * shot_count
    rows = (anchor_tile * tile_rows + jnp.arange(aperture, dtype=jnp.int32)) % model_rows
    local_velocity = jnp.take(whole, rows, axis=0)
    courant = (SPACING_RATIO * local_velocity) ** 2
    slab_depth = forward_pair.shape[3]
    depth_start = lax.axis_index("sub") * slab_depth
    source = source_cells[0]
    receivers = receiver_cells[0]
    later_p, now_p = (forward_pair[0, 0], forward_pair[0, 1])
    later_q, now_q = (adjoint_pair[0, 0], adjoint_pair[0, 1])
    image = jnp.zeros_like(now_p)
    for step_index in range(STEPS):
        both = jnp.stack([now_p, now_q])
        rims = extended(both, (("sub", 2),), 4)
        padded = jnp.pad(rims, ((0, 0), (4, 4), (0, 0), (4, 4)))
        laplace = stencil(padded, both)
        prev_p = 2.0 * now_p - later_p + courant * laplace[0]
        prev_p = inject(
            prev_p, source[0], source[1], source[2], wavelet[0, step_index], depth_start
        )
        prev_q = 2.0 * now_q - later_q + courant * laplace[1]
        prev_q = inject(
            prev_q, receivers[0], receivers[1], receivers[2], residuals[0, step_index], depth_start
        )
        image = image + now_q * (later_p - 2.0 * now_p + prev_p)
        later_p, now_p = (now_p, prev_p)
        later_q, now_q = (now_q, prev_q)
    frame = jnp.zeros(((2 * reach_tiles + 1) * tile_rows,) + image.shape[1:], jnp.float32)
    frame = lax.dynamic_update_slice_in_dim(frame, image, frame_start, 0)
    summed = frame[reach_tiles * tile_rows : (reach_tiles + 1) * tile_rows]
    for offset in range(-reach_tiles, reach_tiles + 1):
        if offset != 0:
            outgoing = frame[
                (offset + reach_tiles) * tile_rows : (offset + reach_tiles + 1) * tile_rows
            ]
            summed = summed + passed_along(outgoing, "shot", offset)
    gradient = -(2.0 / velocity) * summed
    forward_out = jnp.stack([later_p, now_p])[None]
    adjoint_out = jnp.stack([later_q, now_q])[None]
    return (gradient, forward_out, adjoint_out)


def solution(mesh):
    return jax.shard_map(
        on_device,
        mesh=mesh,
        in_specs=(
            P(("grp", "shot"), "sub", None),
            P(("grp", "shot")),
            P(("grp", "shot"), None),
            P(("grp", "shot"), None, None),
            P(("grp", "shot"), None),
            P(("grp", "shot"), None, None),
            P(("grp", "shot"), None, None, "sub", None),
            P(("grp", "shot"), None, None, "sub", None),
        ),
        out_specs=(
            P(("grp", "shot"), "sub", None),
            P(("grp", "shot"), None, None, "sub", None),
            P(("grp", "shot"), None, None, "sub", None),
        ),
        check_vma=False,
    )
```

profile of v0, /device:TPU:1, one launch (start us, length us, event | category | flops | bytes accessed | tf_op | source)
XLA Modules:
  0.0 128.9 jit_solution(9356056296718530971)
XLA Ops:
  0.6 0.0 copy-start.10
  0.6 0.0 copy-start.4
  0.7 0.0 copy-start.7
  0.7 0.0 copy-start.8
  0.7 0.0 copy-start.6
  0.7 0.0 copy-start.9
  0.7 1.3 %slice_bitcast_fusion.4 = (f32[1,32,16,256]{3,2,1,0:T(8,128)S(1)}, f32[1,32,16,256]{3,2,1,0:T(8,128)S(1)}) fusion(f32[1,2,32,16,256]{4,3,2,1,0:T(8,128)} %param.18, f32[1,2,32,16,256]{4,3,2,1,0:T(8,128)} %param.19), kind=kLoop, calls=%fused_computation.118 | loop fusion | bytes 2097152 | tf_op jit(solution)/shard_map/stack;squeeze | solution.py:86
  2.0 0.0 copy-start
  2.0 0.1 fusion.54
  2.2 4.5 %collective-permute-start = (f32[2,32,4,256]{3,2,1,0:T(4,128)S(1)}, f32[2,32,4,256]{3,2,1,0:T(4,128)S(1)}, u32[]{:S(2)}, u32[]{:S(2)}) collective-permute-start(f32[2,32,4,256]{3,2,1,0:T(4,128)S(1)} %get-tuple-element.37), channel_id=1, source_target_pairs={{0,1},{1,2},{2,3},{4,5},{5,6},{6,7},{8,9},{9,10},{10,11},{12,13},{... | collective-permute-start | bytes 786440 | tf_op jit(solution)/shard_map/ppermute | solution.py:19
  6.7 1.9 %collective-permute-start.1 = (f32[2,32,4,256]{3,2,1,0:T(4,128)S(1)}, f32[2,32,4,256]{3,2,1,0:T(4,128)}, u32[]{:S(2)}, u32[]{:S(2)}) collective-permute-start(f32[2,32,4,256]{3,2,1,0:T(4,128)S(1)} %get-tuple-element.38), channel_id=1, source_target_pairs={{1,0},{2,1},{3,2},{5,4},{6,5},{7,6},{9,8},{10,9},{11,10},{13,12},{... | collective-permute-start | bytes 786440 | tf_op jit(solution)/shard_map/ppermute | solution.py:22
  9.3 0.0 copy-done.4
  9.3 14.5 %all_gather.3 = f32[32,16,256]{2,1,0:T(8,128)S(1)} all-gather(f32[8,16,256]{2,1,0:T(8,128)S(1)} %copy-done.4), channel_id=1, replica_groups=mesh['grp'=2,'shot'=4,'sub'=4] {'shot'}, dimensions={0}, use_global_device_ids=true | all-gather | bytes 655360 | tf_op jit(solution)/shard_map/all_gather | solution.py:73
  23.8 0.0 copy-done.7
  23.8 0.6 fusion.69
  27.6 0.0 copy-done.8
  27.6 0.6 fusion.68
  28.3 0.0 copy-done.6
  29.6 0.0 copy-done.10
  29.6 0.8 and_reduce_fusion
  30.4 1.4 %gather_fusion = f32[32,16,256]{2,1,0:T(8,128)} fusion(f32[32,16,256]{2,1,0:T(8,128)S(1)} %all_gather.3, s32[1024]{0:T(1024)S(1)} %pad_clamp_fusion), kind=kCustom, calls=%fused_computation | custom fusion | bytes 1048704 | tf_op jit(solution)/shard_map/jit(_take)/gather | solution.py:76
  32.4 0.0 collective-permute-done
  32.4 0.0 copy-start.3
  32.4 0.0 collective-permute-done.1
  32.4 0.0 copy-done
  32.4 0.7 copy-done.3
  33.1 2.4 %pad_maximum_fusion.2 = (f32[2,32,20,256]{3,2,1,0:T(8,128)S(1)}, f32[2,32,20,256]{3,2,1,0:T(8,128)}) fusion(f32[2,32,4,256]{3,2,1,0:T(4,128)} %collective-permute-done.1, f32[1,32,16,256]{3,2,1,0:T(8,128)S(1)} %get-tuple-element.53, f32[1,32,16,256]{3,2,1,0:T(8,128)S(1)} %get-tuple-element.52, f32[2,32,4,256]{3,2,1,0:T(4,128)S(1)} %collective-permute-done), kind=kLoop, calls=%fused_computation.20 | loop fusion | flops 1310720 | bytes 4194304 | tf_op jit(solution)/shard_map/concatenate | solution.py:23
  35.5 3.6 %select_maximum_fusion.3 = f32[2,40,24,264]{3,2,1,0:T(8,128)S(1)} fusion(f32[2,32,4,256]{3,2,1,0:T(4,128)} %collective-permute-done.1, f32[2,32,4,256]{3,2,1,0:T(4,128)} %copy-done.3, f32[1,32,16,256]{3,2,1,0:T(8,128)} %copy-done, f32[1,32,16,256]{3,2,1,0:T(8,128)S(1)} %get-tuple-element.52), kind=kLoop, calls=%fused_computation.10 | loop fusion | flops 9123840 | bytes 3600384 | tf_op jit(solution)/shard_map/concatenate | solution.py:23
  39.2 7.6 %fusion.7 = f32[2,32,16,256]{3,2,1,0:T(8,128)} fusion(f32[1,32,16,256]{3,2,1,0:T(8,128)} %copy-done, f32[1,32,16,256]{3,2,1,0:T(8,128)S(1)} %get-tuple-element.52, f32[2,40,24,264]{3,2,1,0:T(8,128)S(1)} %select_maximum_fusion.3, f32[2,32,20,256]{3,2,1,0:T(8,128)} %get-tuple-element.36, f32[2,32,20,256]{3,2,1,0:T(8,128)S(1)} %get-tuple-element.35), kind=kLoop, calls=%fused_computation.35 | loop fusion | flops 7864320 | bytes 27262976 | tf_op jit(solution)/shard_map/add | solution.py:49
  46.8 2.2 %fusion.45 = (f32[32,16,256]{2,1,0:T(8,128)S(1)}, f32[32,16,256]{2,1,0:T(8,128)S(1)}) fusion(f32[2,32,16,256]{3,2,1,0:T(8,128)} %fusion.7, f32[1,2,32,16,256]{4,3,2,1,0:T(8,128)} %param.18, f32[32,16,256]{2,1,0:T(8,128)} %gather_fusion, pred[32]{0:T(512)(128)(4,1)S(1)} %compare_and_fusion.1, f32[1,2,32,16,256]{4,3,2,1,0:T(8,128)} %param.19), kind=kLoop, calls=%fused_computation.102 | loop fusion | flops 1441792 | bytes 4718624 | tf_op jit(solution)/shard_map/add | solution.py:90
  49.0 0.6 dynamic-slice.17
  51.6 0.1 scatter-add.24
  51.7 15.7 %scatter_fusion = f32[32,16,256]{2,1,0:T(8,128)S(1)} fusion(f32[32,16,256]{2,1,0:T(8,128)S(1)} %get-tuple-element.30, s32[256]{0:T(256)S(1)} %bitcast.112, f32[256]{0:T(256)S(1)} %bitcast.127), kind=kCustom, calls=%fused_computation.1 | custom fusion | flops 256 | bytes 6144 | tf_op jit(solution)/shard_map/scatter-add | solution.py:58
  67.5 0.1 fusion.52
  67.6 4.8 %collective-permute-start.2 = (f32[2,32,4,256]{3,2,1,0:T(4,128)S(1)}, f32[2,32,4,256]{3,2,1,0:T(4,128)S(1)}, u32[]{:S(2)}, u32[]{:S(2)}) collective-permute-start(f32[2,32,4,256]{3,2,1,0:T(4,128)S(1)} %get-tuple-element.33), channel_id=1, source_target_pairs={{0,1},{1,2},{2,3},{4,5},{5,6},{6,7},{8,9},{9,10},{10,11},{12,13},{... | collective-permute-start | bytes 786440 | tf_op jit(solution)/shard_map/ppermute | solution.py:19
  72.4 1.9 %collective-permute-start.3 = (f32[2,32,4,256]{3,2,1,0:T(4,128)S(1)}, f32[2,32,4,256]{3,2,1,0:T(4,128)S(1)}, u32[]{:S(2)}, u32[]{:S(2)}) collective-permute-start(f32[2,32,4,256]{3,2,1,0:T(4,128)S(1)} %get-tuple-element.34), channel_id=1, source_target_pairs={{1,0},{2,1},{3,2},{5,4},{6,5},{7,6},{9,8},{10,9},{11,10},{13,12},{... | collective-permute-start | bytes 786440 | tf_op jit(solution)/shard_map/ppermute | solution.py:22
  75.0 0.7 collective-permute-done.2
  75.7 4.4 %collective-permute-done.3 = f32[2,32,4,256]{3,2,1,0:T(4,128)S(1)} collective-permute-done((f32[2,32,4,256]{3,2,1,0:T(4,128)S(1)}, f32[2,32,4,256]{3,2,1,0:T(4,128)S(1)}, u32[]{:S(2)}, u32[]{:S(2)}) %collective-permute-start.3) | collective-permute-done | bytes 262176 | tf_op jit(solution)/shard_map/ppermute | solution.py:22
  80.1 1.9 %pad_maximum_fusion.3 = (f32[2,32,20,256]{3,2,1,0:T(8,128)}, f32[2,32,20,256]{3,2,1,0:T(8,128)}) fusion(f32[2,32,4,256]{3,2,1,0:T(4,128)S(1)} %collective-permute-done.3, f32[1,32,16,256]{3,2,1,0:T(8,128)S(1)} %bitcast.115, f32[1,32,16,256]{3,2,1,0:T(8,128)S(1)} %bitcast.120, f32[2,32,4,256]{3,2,1,0:T(4,128)S(1)} %collective-permute-done.2), kind=kLoop, calls=%fused_computation.22 | loop fusion | flops 1310720 | bytes 4194304 | tf_op jit(solution)/shard_map/concatenate | solution.py:23
  82.0 2.6 %select_maximum_fusion = f32[2,40,24,264]{3,2,1,0:T(8,128)S(1)} fusion(f32[2,32,4,256]{3,2,1,0:T(4,128)S(1)} %collective-permute-done.3, f32[2,32,4,256]{3,2,1,0:T(4,128)S(1)} %collective-permute-done.2, f32[1,32,16,256]{3,2,1,0:T(8,128)S(1)} %bitcast.116, f32[1,32,16,256]{3,2,1,0:T(8,128)S(1)} %bitcast.121), kind=kLoop, calls=%fused_computation.7 | loop fusion | flops 9123840 | bytes 3600384 | tf_op jit(solution)/shard_map/concatenate | solution.py:23
  84.6 0.0 copy-start.1
  84.6 8.9 %fusion.12 = f32[2,32,16,256]{3,2,1,0:T(8,128)} fusion(f32[1,32,16,256]{3,2,1,0:T(8,128)S(1)} %bitcast.117, f32[1,32,16,256]{3,2,1,0:T(8,128)S(1)} %bitcast.122, f32[2,40,24,264]{3,2,1,0:T(8,128)S(1)} %select_maximum_fusion, f32[2,32,20,256]{3,2,1,0:T(8,128)} %get-tuple-element.32, f32[2,32,20,256]{3,2,1,0:T(8,128)} %get-tuple-element.31), kind=kLoop, calls=%fused_computation.40 | loop fusion | flops 7864320 | bytes 27262976 | tf_op jit(solution)/shard_map/add | solution.py:49
  93.5 1.8 %fusion.39 = (f32[32,16,256]{2,1,0:T(8,128)S(1)}, f32[32,16,256]{2,1,0:T(8,128)S(1)}) fusion(f32[2,32,16,256]{3,2,1,0:T(8,128)} %fusion.12, f32[32,16,256]{2,1,0:T(8,128)S(1)} %scatter_fusion, f32[1,2,32,16,256]{4,3,2,1,0:T(8,128)} %param.19, f32[32,16,256]{2,1,0:T(8,128)} %gather_fusion, pred[32]{0:T(512)(128)(4,1)S(1)} %compare_and_fusion.1, ...), kind=kLoop, calls=%fused_computation.93 | loop fusion | flops 1441792 | bytes 4718624 | tf_op jit(solution)/shard_map/add | solution.py:94
  95.3 0.6 dynamic-slice.18
  97.8 0.1 scatter-add.26
  98.0 0.1 broadcast_in_dim.42
  98.1 1.4 %fusion.49 = f32[56,16,256]{2,1,0:T(8,128)S(1)} fusion(f32[56,16,256]{2,1,0:T(8,128)S(1)} %broadcast_in_dim.42, s32[]{:T(128)S(6)} %select_n.125, f32[32,16,256]{2,1,0:T(8,128)S(1)} %scatter_fusion, f32[32,16,256]{2,1,0:T(8,128)S(1)} %scatter-add.26, f32[32,16,256]{2,1,0:T(8,128)S(1)} %scatter-add.24, f32[1,2,32,16,256]{4,3,2,1,0:T(8,128)S(1)} %copy-done.1, ...), kind=kLoop, calls=%fused_computation.110 | loop fusion | flops 1179648 | bytes 3670020 | tf_op jit(solution)/shard_map/dynamic_update_slice | solution.py:102
  99.5 0.9 fusion.67
  100.4 1.9 %collective-permute-start.4 = (f32[8,16,256]{2,1,0:T(8,128)}, f32[8,16,256]{2,1,0:T(8,128)S(1)}, u32[]{:S(2)}, u32[]{:S(2)}) collective-permute-start(f32[8,16,256]{2,1,0:T(8,128)} %get-tuple-element.39), channel_id=1, source_target_pairs={{0,4},{4,8},{8,12},{12,0},{1,5},{5,9},{9,13},{13,1},{2,6},{6,10},{... | collective-permute-start | bytes 393224 | tf_op jit(solution)/shard_map/ppermute | solution.py:30
  102.3 2.3 %collective-permute-start.5 = (f32[8,16,256]{2,1,0:T(8,128)}, f32[8,16,256]{2,1,0:T(8,128)S(1)}, u32[]{:S(2)}, u32[]{:S(2)}) collective-permute-start(f32[8,16,256]{2,1,0:T(8,128)} %get-tuple-element.44), channel_id=1, source_target_pairs={{0,8},{4,12},{8,0},{12,4},{1,9},{5,13},{9,1},{13,5},{2,10},{6,14},... | collective-permute-start | bytes 393224 | tf_op jit(solution)/shard_map/ppermute | solution.py:30
  104.5 0.0 collective-permute-start.6
  104.5 1.5 %collective-permute-start.7 = (f32[8,16,256]{2,1,0:T(8,128)S(1)}, f32[8,16,256]{2,1,0:T(8,128)S(1)}, u32[]{:S(2)}, u32[]{:S(2)}) collective-permute-start(f32[8,16,256]{2,1,0:T(8,128)S(1)} %get-tuple-element.42), channel_id=1, source_target_pairs={{0,4},{4,8},{8,12},{12,0},{1,5},{5,9},{9,13},{13,1},{2,6},{6,10},{... | collective-permute-start | bytes 393224 | tf_op jit(solution)/shard_map/ppermute | solution.py:30
  106.0 0.1 collective-permute-start.8
  106.1 15.7 %scatter_fusion.1 = f32[32,16,256]{2,1,0:T(8,128)S(1)} fusion(f32[32,16,256]{2,1,0:T(8,128)S(1)} %get-tuple-element.27, s32[256]{0:T(256)S(1)} %bitcast.113, f32[256]{0:T(256)S(1)} %bitcast.126), kind=kCustom, calls=%fused_computation.2 | custom fusion | flops 256 | bytes 6144 | tf_op jit(solution)/shard_map/scatter-add | solution.py:58
  121.8 1.1 maximum_bitcast_fusion
  122.9 0.0 collective-permute-done.4
  122.9 2.0 %collective-permute-start.9 = (f32[8,16,256]{2,1,0:T(8,128)S(1)}, f32[8,16,256]{2,1,0:T(8,128)S(1)}, u32[]{:S(2)}, u32[]{:S(2)}) collective-permute-start(f32[8,16,256]{2,1,0:T(8,128)S(1)} %get-tuple-element.40), channel_id=1, source_target_pairs={{0,12},{4,0},{8,4},{12,8},{1,13},{5,1},{9,5},{13,9},{2,14},{6,2},{... | collective-permute-start | bytes 393224 | tf_op jit(solution)/shard_map/ppermute | solution.py:30
  124.9 1.1 fusion.13
  126.0 0.0 collective-permute-done.5
  126.0 0.0 collective-permute-done.6
  126.0 0.0 collective-permute-done.7
  126.0 0.0 collective-permute-done.8
  126.0 1.2 collective-permute-done.9
  127.3 1.7 %fusion.61 = f32[8,16,256]{2,1,0:T(8,128)} fusion(f32[8,16,256]{2,1,0:T(8,128)S(1)} %collective-permute-done.9, f32[8,16,256]{2,1,0:T(8,128)S(1)} %collective-permute-done.8, f32[8,16,256]{2,1,0:T(8,128)S(1)} %collective-permute-done.7, f32[8,16,256]{2,1,0:T(8,128)S(1)} %collective-permute-done.6, f32[8,16,256]{2,1,0:T(8,128)S(1)} %collective-permute-done.5, ...), kind=kLoop, calls=%fused_computation.130 | loop fusion | flops 294912 | bytes 1179648 | tf_op jit(solution)/shard_map/mul | solution.py:110
  (11 shorter events, 0.1 us)
Async XLA Ops:
  0.6 28.9 %copy-start.10 = (s32[3]{0:T(128)S(1)}, s32[3]{0:T(128)}, u32[]{:S(2)}) copy-start(s32[3]{0:T(128)} %constant.117.clone.1) | copy-start | bytes 40
  0.6 8.6 %copy-start.4 = (f32[8,16,256]{2,1,0:T(8,128)S(1)}, f32[8,16,256]{2,1,0:T(8,128)}, u32[]{:S(2)}) copy-start(f32[8,16,256]{2,1,0:T(8,128)} %param.12) | copy-start | bytes 393220
  0.7 23.1 %copy-start.7 = (s32[1,3]{1,0:T(1,128)S(1)}, s32[1,3]{1,0:T(1,128)}, u32[]{:S(2)}) copy-start(s32[1,3]{1,0:T(1,128)} %param.14) | copy-start | bytes 40
  0.7 26.9 %copy-start.8 = (f32[1,2]{1,0:T(1,128)S(1)}, f32[1,2]{1,0:T(1,128)}, u32[]{:S(2)}) copy-start(f32[1,2]{1,0:T(1,128)} %param.16) | copy-start | bytes 28
  0.7 27.6 %copy-start.6 = (s32[1,3,256]{2,0,1:T(1,128)S(1)}, s32[1,3,256]{2,0,1:T(1,128)}, u32[]{:S(2)}) copy-start(s32[1,3,256]{2,0,1:T(1,128)} %param.15) | copy-start | bytes 9220
  0.7 31.7 %copy-start.9 = (f32[1,2,256]{2,1,0:T(2,128)S(1)}, f32[1,2,256]{2,1,0:T(2,128)}, u32[]{:S(2)}) copy-start(f32[1,2,256]{2,1,0:T(2,128)} %param.17) | copy-start | bytes 6148
  2.0 30.4 %copy-start = (f32[1,32,16,256]{3,2,1,0:T(8,128)}, f32[1,32,16,256]{3,2,1,0:T(8,128)S(1)}, u32[]{:S(2)}) copy-start(f32[1,32,16,256]{3,2,1,0:T(8,128)S(1)} %get-tuple-element.53) | copy-start | bytes 1572868
  2.2 30.2 %collective-permute-start = (f32[2,32,4,256]{3,2,1,0:T(4,128)S(1)}, f32[2,32,4,256]{3,2,1,0:T(4,128)S(1)}, u32[]{:S(2)}, u32[]{:S(2)}) collective-permute-start(f32[2,32,4,256]{3,2,1,0:T(4,128)S(1)} %get-tuple-element.37), channel_id=1, source_target_pairs={{0,1},{1,2},{2,3},{4,5},{5,6},{6,7},{8,9},{9,10},{10,11},{12,13},{... | collective-permute-start | bytes 786440 | tf_op jit(solution)/shard_map/ppermute | solution.py:19
  6.7 25.7 %collective-permute-start.1 = (f32[2,32,4,256]{3,2,1,0:T(4,128)S(1)}, f32[2,32,4,256]{3,2,1,0:T(4,128)}, u32[]{:S(2)}, u32[]{:S(2)}) collective-permute-start(f32[2,32,4,256]{3,2,1,0:T(4,128)S(1)} %get-tuple-element.38), channel_id=1, source_target_pairs={{1,0},{2,1},{3,2},{5,4},{6,5},{7,6},{9,8},{10,9},{11,10},{13,12},{... | collective-permute-start | bytes 786440 | tf_op jit(solution)/shard_map/ppermute | solution.py:22
  32.4 0.7 copy-start.3
  67.6 8.1 %collective-permute-start.2 = (f32[2,32,4,256]{3,2,1,0:T(4,128)S(1)}, f32[2,32,4,256]{3,2,1,0:T(4,128)S(1)}, u32[]{:S(2)}, u32[]{:S(2)}) collective-permute-start(f32[2,32,4,256]{3,2,1,0:T(4,128)S(1)} %get-tuple-element.33), channel_id=1, source_target_pairs={{0,1},{1,2},{2,3},{4,5},{5,6},{6,7},{8,9},{9,10},{10,11},{12,13},{... | collective-permute-start | bytes 786440 | tf_op jit(solution)/shard_map/ppermute | solution.py:19
  72.4 7.7 %collective-permute-start.3 = (f32[2,32,4,256]{3,2,1,0:T(4,128)S(1)}, f32[2,32,4,256]{3,2,1,0:T(4,128)S(1)}, u32[]{:S(2)}, u32[]{:S(2)}) collective-permute-start(f32[2,32,4,256]{3,2,1,0:T(4,128)S(1)} %get-tuple-element.34), channel_id=1, source_target_pairs={{1,0},{2,1},{3,2},{5,4},{6,5},{7,6},{9,8},{10,9},{11,10},{13,12},{... | collective-permute-start | bytes 786440 | tf_op jit(solution)/shard_map/ppermute | solution.py:22
  84.6 8.9 %copy-start.1 = (f32[1,2,32,16,256]{4,3,2,1,0:T(8,128)S(1)}, f32[1,2,32,16,256]{4,3,2,1,0:T(8,128)}, u32[]{:S(2)}) copy-start(f32[1,2,32,16,256]{4,3,2,1,0:T(8,128)} %param.18) | copy-start | bytes 3145732
  99.5 6.6 %copy-start.2 = (f32[56,16,256]{2,1,0:T(8,128)}, f32[56,16,256]{2,1,0:T(8,128)S(1)}, u32[]{:S(2)}) copy-start(f32[56,16,256]{2,1,0:T(8,128)S(1)} %fusion.49) | copy-start | bytes 2752516
  100.4 22.5 %collective-permute-start.4 = (f32[8,16,256]{2,1,0:T(8,128)}, f32[8,16,256]{2,1,0:T(8,128)S(1)}, u32[]{:S(2)}, u32[]{:S(2)}) collective-permute-start(f32[8,16,256]{2,1,0:T(8,128)} %get-tuple-element.39), channel_id=1, source_target_pairs={{0,4},{4,8},{8,12},{12,0},{1,5},{5,9},{9,13},{13,1},{2,6},{6,10},{... | collective-permute-start | bytes 393224 | tf_op jit(solution)/shard_map/ppermute | solution.py:30
  102.3 23.8 %collective-permute-start.5 = (f32[8,16,256]{2,1,0:T(8,128)}, f32[8,16,256]{2,1,0:T(8,128)S(1)}, u32[]{:S(2)}, u32[]{:S(2)}) collective-permute-start(f32[8,16,256]{2,1,0:T(8,128)} %get-tuple-element.44), channel_id=1, source_target_pairs={{0,8},{4,12},{8,0},{12,4},{1,9},{5,13},{9,1},{13,5},{2,10},{6,14},... | collective-permute-start | bytes 393224 | tf_op jit(solution)/shard_map/ppermute | solution.py:30
  104.5 21.5 %collective-permute-start.6 = (f32[8,16,256]{2,1,0:T(8,128)S(1)}, f32[8,16,256]{2,1,0:T(8,128)S(1)}, u32[]{:S(2)}, u32[]{:S(2)}) collective-permute-start(f32[8,16,256]{2,1,0:T(8,128)S(1)} %get-tuple-element.43), channel_id=1, source_target_pairs={{0,12},{4,0},{8,4},{12,8},{1,13},{5,1},{9,5},{13,9},{2,14},{6,2},{... | collective-permute-start | bytes 393224 | tf_op jit(solution)/shard_map/ppermute | solution.py:30
  104.5 21.5 %collective-permute-start.7 = (f32[8,16,256]{2,1,0:T(8,128)S(1)}, f32[8,16,256]{2,1,0:T(8,128)S(1)}, u32[]{:S(2)}, u32[]{:S(2)}) collective-permute-start(f32[8,16,256]{2,1,0:T(8,128)S(1)} %get-tuple-element.42), channel_id=1, source_target_pairs={{0,4},{4,8},{8,12},{12,0},{1,5},{5,9},{9,13},{13,1},{2,6},{6,10},{... | collective-permute-start | bytes 393224 | tf_op jit(solution)/shard_map/ppermute | solution.py:30
  106.0 20.0 %collective-permute-start.8 = (f32[8,16,256]{2,1,0:T(8,128)S(1)}, f32[8,16,256]{2,1,0:T(8,128)S(1)}, u32[]{:S(2)}, u32[]{:S(2)}) collective-permute-start(f32[8,16,256]{2,1,0:T(8,128)S(1)} %get-tuple-element.41), channel_id=1, source_target_pairs={{0,8},{4,12},{8,0},{12,4},{1,9},{5,13},{9,1},{13,5},{2,10},{6,14},... | collective-permute-start | bytes 393224 | tf_op jit(solution)/shard_map/ppermute | solution.py:30
  106.1 21.2 %copy-start.5 = (f32[8,16,256]{2,1,0:T(8,128)S(1)}, f32[8,16,256]{2,1,0:T(8,128)}, u32[]{:S(2)}) copy-start(f32[8,16,256]{2,1,0:T(8,128)} %param.12) | copy-start | bytes 393220
  122.9 4.3 %collective-permute-start.9 = (f32[8,16,256]{2,1,0:T(8,128)S(1)}, f32[8,16,256]{2,1,0:T(8,128)S(1)}, u32[]{:S(2)}, u32[]{:S(2)}) collective-permute-start(f32[8,16,256]{2,1,0:T(8,128)S(1)} %get-tuple-element.40), channel_id=1, source_target_pairs={{0,12},{4,0},{8,4},{12,8},{1,13},{5,1},{9,5},{13,9},{2,14},{6,2},{... | collective-permute-start | bytes 393224 | tf_op jit(solution)/shard_map/ppermute | solution.py:30
where the time goes:
time: 129 us
  other arithmetic  68.8 us (53%)
  starting transfers between devices  20.8 us (16%)
  blocking collectives  14.5 us (11%)
  between operations  11.3 us (9%)
  local copies, waits for them, and re-layouts  7.15 us (6%)
  waiting for transfers between devices  6.29 us (5%)
    scatter-add x2, other arithmetic, inject(): field.at[first, local_depth, side].add(jnp.where(inside, amount, 0.0))  31.4 us
    add x2, other arithmetic, stencil(): total = total + STENCIL_COEFS[offset] * (along_x + along_z + along_y)  16.5 us
    all_gather x1, blocking collectives, on_device(): whole = lax.all_gather(velocity, 'shot', axis=0, tiled=True)  14.5 us
    concatenate x4, other arithmetic, extended(): block = jnp.concatenate([low, block, high], axis=dim)  10.5 us
    ppermute x2, starting transfers between devices, extended(): lax.ppermute(lax.slice_in_dim(block, block.shape[dim] - width, None, axis...  9.32 us
    ppermute x6, starting transfers between devices, passed_along(): return lax.ppermute(value, axis, pairs)  7.67 us
    ppermute x2, waiting for transfers between devices, extended(): lax.ppermute(lax.slice_in_dim(block, 0, width, axis=dim), axis, backward)  4.4 us
    ppermute x2, starting transfers between devices, extended(): lax.ppermute(lax.slice_in_dim(block, 0, width, axis=dim), axis, backward)  3.84 us
  transfers between devices with their start and end apart: 10, of which 3 were waited for; matrix products, arithmetic and copies ran while one was open for 17% of the time, Pallas kernels for 0%

commit v1 on v0

v1 whole, which is shorter than its diff:
```python
import functools

import jax
import jax.numpy as jnp
from jax import lax
from jax.experimental import pallas as pl
from jax.experimental.pallas import tpu as pltpu
from jax.sharding import PartitionSpec as P

APT = 4
RIM = 4
STENCIL_COEFS = (-205.0 / 72.0, 8.0 / 5.0, -1.0 / 5.0, 8.0 / 315.0, -1.0 / 560.0)
SPACING_RATIO = 0.1

F32 = jnp.float32
BF16 = jnp.bfloat16
IN_VMEM = pl.BlockSpec(memory_space=pltpu.VMEM)
IN_SMEM = pl.BlockSpec(memory_space=pltpu.SMEM)
IN_PLACE = pl.BlockSpec(memory_space=pl.ANY)


def kept(shape):
    return pltpu.VMEM(shape, F32)


def given(shape):
    return jax.ShapeDtypeStruct(shape, F32)


def on_chip(value):
    return pltpu.with_memory_space_constraint(value, pltpu.VMEM)


def call(kernel, outs, ins, out_specs=None, scratch=(), name=None):
    return pl.pallas_call(
        kernel,
        out_shape=tuple(outs),
        in_specs=[spec for spec, _ in ins],
        out_specs=tuple(out_specs or [IN_VMEM] * len(outs)),
        scratch_shapes=list(scratch),
        compiler_params=pltpu.CompilerParams(vmem_limit_bytes=40 * 1024 * 1024),
        name=name,
    )(*[array for _, array in ins])


def partners(count):
    reach = APT - 1
    if count <= 2 * reach and count & (count - 1) == 0:
        plans = []
        for bit in range(1, count):
            pairs = [(i, i ^ bit) for i in range(count)]
            plans.append((pairs, pairs, functools.partial(lambda bit, i: i ^ bit, bit)))
        return plans
    if count <= 2 * reach:
        offsets = range(1, count)
    else:
        offsets = [o for o in range(-reach, reach + 1) if o != 0]
    plans = []
    for o in offsets:
        fetch = [((i + o) % count, i) for i in range(count)]
        send = [(i, (i + o) % count) for i in range(count)]
        plans.append((fetch, send, functools.partial(lambda o, i: lax.rem(i + o + count, count), o)))
    return plans


def y_operator(width):
    row = lax.broadcasted_iota(jnp.int32, (width, width), 0)
    column = lax.broadcasted_iota(jnp.int32, (width, width), 1)
    apart = jnp.abs(row - column)
    total = jnp.zeros((width, width), F32)
    for o in range(1, RIM + 1):
        total = jnp.where(apart == o, F32(STENCIL_COEFS[o]), total)
    high = total.astype(BF16)
    return high, (total - high.astype(F32)).astype(BF16)


def y_part(field, high, low):
    rows, depth, width = field.shape
    flat = field.reshape(rows * depth, width)
    top = flat.astype(BF16)
    rest = (flat - top.astype(F32)).astype(BF16)
    total = jnp.dot(top, high, preferred_element_type=F32)
    total = total + jnp.dot(rest, high, preferred_element_type=F32)
    total = total + jnp.dot(top, low, preferred_element_type=F32)
    return total.reshape(rows, depth, width)


def xz_part(padded, rim, x, own, depth):
    total = F32(3.0 * STENCIL_COEFS[0]) * own
    window = jnp.concatenate([own, rim], axis=0)
    rows = depth + 2 * RIM
    for o in range(1, RIM + 1):
        pair = padded[x + RIM + o] + padded[x + RIM - o]
        below = pltpu.roll(window, rows - o, 0)[:depth]
        above = pltpu.roll(window, o, 0)[:depth]
        total = total + F32(STENCIL_COEFS[o]) * (pair + (below + above))
    return total


def fill_padded(padded, field):
    rows = padded.shape[0] - 2 * RIM
    zero = jnp.zeros((RIM,) + padded.shape[1:], F32)
    padded[0:RIM] = zero
    padded[RIM + rows : RIM + rows + RIM] = zero
    padded[RIM : RIM + rows] = field


def first_four(shape):
    return lax.broadcasted_iota(jnp.int32, shape, len(shape) - 2) < RIM


def pack_rims(p, q, depth):
    last = depth - 2 * RIM
    p_first, p_last = p[:, 0 : 2 * RIM], p[:, last:depth]
    q_first, q_last = q[:, 0 : 2 * RIM], q[:, last:depth]
    here = first_four(p_first.shape)
    deeper = jnp.where(here, pltpu.roll(q_last, RIM, 1), p_last)
    shallower = jnp.where(here, p_first, pltpu.roll(q_first, RIM, 1))
    return deeper, shallower


def p_rim(from_above, from_below):
    return jnp.where(first_four(from_above.shape), from_below, from_above)


def q_rim(from_above, from_below):
    both = jnp.where(first_four(from_above.shape), from_above, from_below)
    return pltpu.roll(both, RIM, both.ndim - 2)


def cell_mask(source, depth, width):
    start = lax.axis_index("sub") * depth
    layer = lax.broadcasted_iota(jnp.int32, (depth, width), 0)
    column = lax.broadcasted_iota(jnp.int32, (depth, width), 1)
    return (layer == source[0, 1] - start) & (column == source[0, 2])


def rims_kernel(p_ref, q_ref, deeper, shallower):
    depth = p_ref.shape[1]
    deeper[...], shallower[...] = pack_rims(p_ref[...], q_ref[...], depth)


def first_kernel(
    source, wavelet, receivers, residuals, forward, adjoint, above, below,
    free_p, lap_p, free_q, lap_q, mixed, free_q2, injected, padded, spread,
):
    rows, depth, width = lap_p.shape
    high, low = y_operator(width)
    start = lax.axis_index("sub") * depth

    first, layer, column = receivers[0, 0:1], receivers[0, 1:2] - start, receivers[0, 2:3]
    inside = (layer >= 0) & (layer < depth)
    place = jnp.where(inside, first * depth + layer, -1)
    count = place.shape[1]
    lines = lax.broadcasted_iota(jnp.int32, (rows * depth, count), 0)
    onto = (lines == place).astype(F32).astype(BF16)
    columns = lax.broadcasted_iota(jnp.int32, (width, count), 0)
    for step in range(2):
        value = jnp.where(columns == column, residuals[0, step : step + 1], 0.0)
        total = None
        for _ in range(3):
            part = value.astype(BF16)
            value = value - part.astype(F32)
            term = lax.dot_general(onto, part, (((1,), (1,)), ((), ())), preferred_element_type=F32)
            total = term if total is None else total + term
        spread[step] = total.reshape(rows, depth, width)

    here = cell_mask(source, depth, width)
    for name, pair, rim_of, lap, free in (
        ("p", forward, p_rim, lap_p, free_p), ("q", adjoint, q_rim, lap_q, free_q),
    ):
        fill_padded(padded, pair[0, 1])
        lap[...] = y_part(pair[0, 1], high, low)

        def row(x, _):
            own = pair[0, 1, x]
            rim = rim_of(above[x], below[x])
            value = lap[x] + xz_part(padded, rim, x, own, depth)
            lap[x] = value
            moved = 2.0 * own - pair[0, 0, x]
            if name == "q":
                moved = moved + spread[0, x]
                free_q2[x] = spread[1, x] - own
                mixed[x] = own * lap_p[x]
            free[x] = moved
            return 0

        lax.fori_loop(0, rows, row, 0, unroll=2)
    x0 = source[0, 0]
    amount = jnp.where(here, wavelet[0, 0], 0.0)
    free_p[x0] = free_p[x0] + amount
    injected[...] = adjoint[0, 1, x0] * amount


def step_kernel(plans, anchors, free_p, lap_p, free_q, lap_q, *refs):
    tiles, (courant, p1, q1, deeper, shallower) = refs[: len(plans) + 1], refs[len(plans) + 1 :]
    tile_rows = tiles[0].shape[0]
    depth = p1.shape[1]
    for tile, place in zip(tiles, places(plans, anchors)):

        def put():
            speed = F32(SPACING_RATIO) * tile[...]
            factor = speed * speed
            span = pl.ds(place * tile_rows, tile_rows)
            courant[span] = factor
            p = free_p[span] + factor * lap_p[span]
            q = free_q[span] + factor * lap_q[span]
            p1[span] = p
            q1[span] = q
            deeper[span], shallower[span] = pack_rims(p, q, depth)

        pl.when((place >= 0) & (place < APT))(put)


def places(plans, anchors):
    count = lax.axis_size("shot")
    me = lax.axis_index("shot")
    peers = [me] + [peer(me) for _, _, peer in plans]
    return [lax.rem(peer - anchors[0] + count, count) for peer in peers]


def image_kernel(plans, source, wavelet, anchors, p1, q1, courant, mixed, injected, above, below, *refs):
    outs, (lap_p, padded, image) = refs[: len(plans) + 1], refs[len(plans) + 1 :]
    rows, depth, width = p1.shape
    high, low = y_operator(width)
    fill_padded(padded, p1[...])
    lap_p[...] = y_part(p1[...], high, low)

    def row(x, _):
        own = p1[x]
        value = lap_p[x] + xz_part(padded, p_rim(above[x], below[x]), x, own, depth)
        lap_p[x] = value
        image[x] = courant[x] * (mixed[x] + q1[x] * value)
        return 0

    lax.fori_loop(0, rows, row, 0, unroll=2)
    x0 = source[0, 0]
    amount = jnp.where(cell_mask(source, depth, width), wavelet[0, 1], 0.0)
    image[x0] = image[x0] + injected[...] + q1[x0] * amount
    tile_rows = outs[0].shape[0]
    for out, place in zip(outs, places(plans, anchors)):
        inside = (place >= 0) & (place < APT)

        def put():
            out[...] = image[pl.ds(place * tile_rows, tile_rows)]

        def clear():
            out[...] = jnp.zeros(out.shape, F32)

        pl.when(inside)(put)
        pl.when(jnp.logical_not(inside))(clear)


def last_kernel(source, wavelet, forward, p1, q1, courant, lap_p, free_q2, above, below, forward_out, adjoint_out, padded):
    rows, depth, width = p1.shape
    high, low = y_operator(width)
    fill_padded(padded, q1[...])
    adjoint_out[0, 1] = y_part(q1[...], high, low)

    def row(x, _):
        own_p, own_q, factor = p1[x], q1[x], courant[x]
        forward_out[0, 0, x] = own_p
        adjoint_out[0, 0, x] = own_q
        forward_out[0, 1, x] = 2.0 * own_p - forward[x] + factor * lap_p[x]
        value = adjoint_out[0, 1, x] + xz_part(padded, q_rim(above[x], below[x]), x, own_q, depth)
        adjoint_out[0, 1, x] = 2.0 * own_q + free_q2[x] + factor * value
        return 0

    lax.fori_loop(0, rows, row, 0, unroll=2)
    x0 = source[0, 0]
    amount = jnp.where(cell_mask(source, depth, width), wavelet[0, 1], 0.0)
    forward_out[0, 1, x0] = forward_out[0, 1, x0] + amount


def gradient_kernel(velocity, *refs):
    parts, out = refs[:-1], refs[-1]
    total = parts[0][...]
    for part in parts[1:]:
        total = total + part[...]
    out[...] = -(2.0 / velocity[...]) * total


def swap_rims(deeper, shallower):
    count = lax.axis_size("sub")
    down = [(i, i + 1) for i in range(count - 1)]
    up = [(i + 1, i) for i in range(count - 1)]
    return lax.ppermute(deeper, "sub", down), lax.ppermute(shallower, "sub", up)


def on_device(
    velocity, anchors, source_cells, receiver_cells, wavelet, residuals, forward_pair, adjoint_pair
):
    tile_rows, depth, width = velocity.shape
    rows = APT * tile_rows
    field = (rows, depth, width)
    rim = (rows, 2 * RIM, width)
    padded = pltpu.VMEM((rows + 2 * RIM, depth, width), F32)
    plans = partners(lax.axis_size("shot"))

    tiles = [velocity] + [lax.ppermute(velocity, "shot", fetch) for fetch, _, _ in plans]

    now = pl.BlockSpec((None, None, rows, depth, width), lambda i: (0, 1, 0, 0, 0))
    whole_rim = pl.BlockSpec(rim, lambda i: (0, 0, 0))
    deeper, shallower = pl.pallas_call(
        rims_kernel, out_shape=(given(rim),) * 2, grid=(1,), in_specs=[now, now], out_specs=(whole_rim,) * 2,
        name="rims",
    )(forward_pair, adjoint_pair)
    above, below = swap_rims(deeper, shallower)

    free_p, lap_p, free_q, lap_q, mixed, free_q2, injected = call(
        first_kernel,
        [kept(field)] * 6 + [kept((depth, width))],
        [
            (IN_SMEM, source_cells), (IN_SMEM, wavelet), (IN_VMEM, receiver_cells), (IN_VMEM, residuals),
            (IN_VMEM, forward_pair), (IN_VMEM, adjoint_pair), (IN_VMEM, above), (IN_VMEM, below),
        ],
        scratch=[padded, pltpu.VMEM((2,) + field, F32)],
        name="first",
    )

    courant, p1, q1, deeper, shallower = call(
        functools.partial(step_kernel, plans),
        [kept(field)] * 3 + [given(rim)] * 2,
        [(IN_SMEM, anchors)]
        + [(IN_VMEM, on_chip(a)) for a in (free_p, lap_p, free_q, lap_q)]
        + [(IN_VMEM, tile) for tile in tiles],
        name="step",
    )
    above, below = swap_rims(deeper, shallower)

    *images, lap_p1 = call(
        functools.partial(image_kernel, plans),
        [given(velocity.shape)] * len(tiles) + [kept(field)],
        [(IN_SMEM, source_cells), (IN_SMEM, wavelet), (IN_SMEM, anchors)]
        + [(IN_VMEM, on_chip(a)) for a in (p1, q1, courant, mixed, injected)]
        + [(IN_VMEM, above), (IN_VMEM, below)],
        scratch=[padded, pltpu.VMEM(field, F32)],
        name="image",
    )
    gathered = [images[0]] + [
        lax.ppermute(image, "shot", send) for image, (_, send, _) in zip(images[1:], plans)
    ]

    forward_out, adjoint_out = call(
        last_kernel,
        [given(forward_pair.shape), given(adjoint_pair.shape)],
        [(IN_SMEM, source_cells), (IN_SMEM, wavelet), (IN_VMEM, forward_pair[0, 1])]
        + [(IN_VMEM, on_chip(a)) for a in (p1, q1, courant, lap_p1, free_q2)]
        + [(IN_VMEM, above), (IN_VMEM, below)],
        scratch=[padded],
        name="last",
    )

    (gradient,) = call(
        gradient_kernel,
        [given(velocity.shape)],
        [(IN_VMEM, velocity)] + [(IN_VMEM, part) for part in gathered],
        name="gradient",
    )
    return gradient, forward_out, adjoint_out


def solution(mesh):
    shot = ("grp", "shot")
    fields = P(shot, None, None, "sub", None)
    return jax.shard_map(
        on_device,
        mesh=mesh,
        in_specs=(
            P(shot, "sub", None),
            P(shot),
            P(shot, None),
            P(shot, None, None),
            P(shot, None),
            P(shot, None, None),
            fields,
            fields,
        ),
        out_specs=(P(shot, "sub", None), fields, fields),
        check_vma=False,
    )
```

time: 129 us -> 48.7 us (0.38)
  other arithmetic: 68.8 us -> 0 us
  blocking collectives: 14.5 us -> 0 us
  Pallas kernels: 0 us -> 12.1 us
  between operations: 11.3 us -> 1.45 us
  waiting for transfers between devices: 6.29 us -> 14.6 us
  local copies, waits for them, and re-layouts: 7.15 us -> 0.07 us
    scatter-add x2 -> x0, other arithmetic: 31.4 us -> none  [inject(): field.at[first, local_depth, side].add(jnp.where(inside, amount, 0.0))]
    add x4 -> x0, other arithmetic: 20.5 us -> none  [the longest x2 16.5 us: stencil(): total = total + STENCIL_COEFS[offset] * (along_x + along_z + along_y)]
    all_gather x1 -> x0, blocking collectives: 14.5 us -> none  [on_device(): whole = lax.all_gather(velocity, 'shot', axis=0, tiled=True)]
    pallas_call x0 -> x6, Pallas kernels: none -> 12.1 us  [the longest x5 9.96 us: call(): pl.pallas_call(kernel, out_shape=tuple(outs), in_specs=[spec for spec, _...]
    concatenate x5 -> x0, other arithmetic: 10.5 us -> none  [the longest x4 10.5 us: extended(): block = jnp.concatenate([low, block, high], axis=dim)]
    ppermute x10, waiting for transfers between devices: 6.29 us -> 14.6 us  [the longest x2 6.26 us: swap_rims(): lax.ppermute(shallower, 'sub', up)]
    another operation x3 -> x0, local copies, waits for them, and re-layouts: 2.52 us -> none  [the longest x1 1.33 us: on_device(): both = jnp.stack([now_p, now_q])]
    broadcast_in_dim x2 -> x0, other arithmetic: 2.21 us -> none  [the longest x1 1.11 us: on_device(): adjoint_out = jnp.stack([later_q, now_q])[None]]
  transfers between devices with their start and end apart: 10 -> 10, of which waited for: 3 -> 5; matrix products, arithmetic and copies ran while one was open for 17% -> 0% of each run, Pallas kernels for 0% -> 15%
where the time goes in v1:
time: 48.7 us; the launch traced here: 48.5 us
  starting transfers between devices  20.2 us (41%)
  waiting for transfers between devices  14.6 us (30%)
  Pallas kernels  12.1 us (25%)
  between operations  1.45 us (3%)
    pallas_call x5, Pallas kernels, call(): pl.pallas_call(kernel, out_shape=tuple(outs), in_specs=[spec for spec, _...  9.96 us
    ppermute x2, starting transfers between devices, swap_rims(): lax.ppermute(deeper, 'sub', down)  8.77 us
    ppermute x2, waiting for transfers between devices, swap_rims(): lax.ppermute(shallower, 'sub', up)  6.26 us
    ppermute x3, starting transfers between devices, on_device(): lax.ppermute(image, 'shot', send)  3.92 us
    ppermute x3, waiting for transfers between devices, on_device(): lax.ppermute(image, 'shot', send)  3.86 us
    ppermute x2, starting transfers between devices, swap_rims(): lax.ppermute(shallower, 'sub', up)  3.84 us
    ppermute x3, starting transfers between devices, on_device(): lax.ppermute(velocity, 'shot', fetch)  3.67 us
    ppermute x3, waiting for transfers between devices, on_device(): lax.ppermute(velocity, 'shot', fetch)  3.14 us
  transfers between devices with their start and end apart: 10, of which 5 were waited for; matrix products, arithmetic and copies ran while one was open for 0% of the time, Pallas kernels for 15%

profile of v1, /device:TPU:1, one launch (start us, length us, event | category | flops | bytes accessed | tf_op | source)
XLA Modules:
  0.0 48.5 jit_solution(11909189634807492112)
XLA Ops:
  0.6 0.0 copy-start
  0.6 0.0 copy-start.1
  0.7 2.2 %rims.1 = (f32[32,8,256]{2,1,0:T(8,128)}, f32[32,8,256]{2,1,0:T(8,128)}) custom-call(f32[1,2,32,16,256]{4,3,2,1,0:T(8,128)} %forward.1, f32[1,2,32,16,256]{4,3,2,1,0:T(8,128)} %adjoint.1), custom_call_target="tpu_custom_call" | custom-call | tf_op jit(solution)/shard_map/rims/pallas_call | solution.py:304
  2.8 0.0 copy-start.6
  2.8 4.6 %collective-permute-start = (f32[32,8,256]{2,1,0:T(8,128)}, f32[32,8,256]{2,1,0:T(8,128)S(1)}, u32[]{:S(2)}, u32[]{:S(2)}) collective-permute-start(f32[32,8,256]{2,1,0:T(8,128)} %get-tuple-element.24), channel_id=1, source_target_pairs={{0,1},{1,2},{2,3},{4,5},{5,6},{6,7},{8,9},{9,10},{10,11},{12,13},{... | collective-permute-start | bytes 786440 | tf_op jit(solution)/shard_map/ppermute | solution.py:287
  7.5 1.9 %collective-permute-start.1 = (f32[32,8,256]{2,1,0:T(8,128)}, f32[32,8,256]{2,1,0:T(8,128)S(1)}, u32[]{:S(2)}, u32[]{:S(2)}) collective-permute-start(f32[32,8,256]{2,1,0:T(8,128)} %get-tuple-element.25), channel_id=1, source_target_pairs={{1,0},{2,1},{3,2},{5,4},{6,5},{7,6},{9,8},{10,9},{11,10},{13,12},{... | collective-permute-start | bytes 786440 | tf_op jit(solution)/shard_map/ppermute | solution.py:287
  9.4 1.4 %collective-permute-start.2 = (f32[8,16,256]{2,1,0:T(8,128)}, f32[8,16,256]{2,1,0:T(8,128)S(1)}, u32[]{:S(2)}, u32[]{:S(2)}) collective-permute-start(f32[8,16,256]{2,1,0:T(8,128)} %velocity.1), channel_id=1, source_target_pairs={{0,4},{4,0},{8,12},{12,8},{1,5},{5,1},{9,13},{13,9},{2,6},{6,2},{1... | collective-permute-start | bytes 393224 | tf_op jit(solution)/shard_map/ppermute | solution.py:300
  10.8 2.3 %collective-permute-start.3 = (f32[8,16,256]{2,1,0:T(8,128)}, f32[8,16,256]{2,1,0:T(8,128)S(1)}, u32[]{:S(2)}, u32[]{:S(2)}) collective-permute-start(f32[8,16,256]{2,1,0:T(8,128)} %velocity.1), channel_id=1, source_target_pairs={{0,8},{4,12},{8,0},{12,4},{1,9},{5,13},{9,1},{13,5},{2,10},{6,14},... | collective-permute-start | bytes 393224 | tf_op jit(solution)/shard_map/ppermute | solution.py:300
  13.1 0.0 collective-permute-start.4
  13.7 0.0 copy-done.6
  13.7 0.0 copy-start.3
  13.7 0.0 copy-start.4
  13.7 0.0 copy-start.5
  13.8 0.0 copy-start.2
  13.8 0.0 collective-permute-done.above
  13.8 1.9 %collective-permute-done.1.below = f32[32,8,256]{2,1,0:T(8,128)S(1)} collective-permute-done((f32[32,8,256]{2,1,0:T(8,128)}, f32[32,8,256]{2,1,0:T(8,128)S(1)}, u32[]{:S(2)}, u32[]{:S(2)}) %collective-permute-start.1) | collective-permute-done | bytes 262176 | tf_op jit(solution)/shard_map/ppermute | solution.py:287
  15.7 0.0 copy-done
  15.7 0.0 copy-done.1
  15.7 0.0 copy-done.3
  15.7 0.0 copy-done.4
  15.7 0.0 copy-done.5
  15.7 3.8 %first.1 = (f32[32,16,256]{2,1,0:T(8,128)S(1)}, f32[32,16,256]{2,1,0:T(8,128)S(1)}, f32[32,16,256]{2,1,0:T(8,128)S(1)}, f32[32,16,256]{2,1,0:T(8,128)S(1)}, f32[...) custom-call(s32[1,3]{1,0:T(1,128)S(1)} %copy-done.3, f32[1,2]{1,0:T(1,128)S(1)} %copy-done.4, ...), custom_call_target="tpu_custom_call" | custom-call | tf_op jit(solution)/shard_map/first/pallas_call | solution.py:35
  19.5 0.0 collective-permute-done.2.refs_1_
  19.5 3.1 %collective-permute-done.3.refs_2_ = f32[8,16,256]{2,1,0:T(8,128)S(1)} collective-permute-done((f32[8,16,256]{2,1,0:T(8,128)}, f32[8,16,256]{2,1,0:T(8,128)S(1)}, u32[]{:S(2)}, u32[]{:S(2)}) %collective-permute-start.3) | collective-permute-done | bytes 131104 | tf_op jit(solution)/shard_map/ppermute | solution.py:300
  22.6 0.0 collective-permute-done.4.refs_3_
  22.6 0.0 copy-done.2
  22.6 0.2 step.1
  22.9 4.1 %collective-permute-start.5 = (f32[32,8,256]{2,1,0:T(8,128)S(1)}, f32[32,8,256]{2,1,0:T(8,128)S(1)}, u32[]{:S(2)}, u32[]{:S(2)}) collective-permute-start(f32[32,8,256]{2,1,0:T(8,128)S(1)} %get-tuple-element.35), channel_id=1, source_target_pairs={{0,1},{1,2},{2,3},{4,5},{5,6},{6,7},{8,9},{9,10},{10,11},{12,13},{... | collective-permute-start | bytes 786440 | tf_op jit(solution)/shard_map/ppermute | solution.py:287
  27.0 1.9 %collective-permute-start.6 = (f32[32,8,256]{2,1,0:T(8,128)S(1)}, f32[32,8,256]{2,1,0:T(8,128)S(1)}, u32[]{:S(2)}, u32[]{:S(2)}) collective-permute-start(f32[32,8,256]{2,1,0:T(8,128)S(1)} %get-tuple-element.36), channel_id=1, source_target_pairs={{1,0},{2,1},{3,2},{5,4},{6,5},{7,6},{9,8},{10,9},{11,10},{13,12},{... | collective-permute-start | bytes 786440 | tf_op jit(solution)/shard_map/ppermute | solution.py:287
  28.9 1.4 %collective-permute-done.5.above = f32[32,8,256]{2,1,0:T(8,128)S(1)} collective-permute-done((f32[32,8,256]{2,1,0:T(8,128)S(1)}, f32[32,8,256]{2,1,0:T(8,128)S(1)}, u32[]{:S(2)}, u32[]{:S(2)}) %collective-permute-start.5) | collective-permute-done | bytes 262176 | tf_op jit(solution)/shard_map/ppermute | solution.py:287
  30.3 4.4 %collective-permute-done.6.below = f32[32,8,256]{2,1,0:T(8,128)S(1)} collective-permute-done((f32[32,8,256]{2,1,0:T(8,128)S(1)}, f32[32,8,256]{2,1,0:T(8,128)S(1)}, u32[]{:S(2)}, u32[]{:S(2)}) %collective-permute-start.6) | collective-permute-done | bytes 262176 | tf_op jit(solution)/shard_map/ppermute | solution.py:287
  34.7 1.9 %image.1 = (f32[8,16,256]{2,1,0:T(8,128)S(1)}, f32[8,16,256]{2,1,0:T(8,128)S(1)}, f32[8,16,256]{2,1,0:T(8,128)S(1)}, f32[8,16,256]{2,1,0:T(8,128)S(1)}, f32[32,16,256]{2,1,0:T(8,128)S(1)}) custom-call(s32[1,3]{1,0:T(1,128)S(1)} %copy-done.3, f32[1,2]{1,0:T(1,128)S(1)} %copy-done.4, s32[1]{0:T(128)S(6)} %copy.12.anchors, ...), custom_call_target="tpu_custom_call" | custom-call | tf_op jit(solution)/shard_map/image/pallas_call | solution.py:35
  36.7 1.8 %collective-permute-start.7 = (f32[8,16,256]{2,1,0:T(8,128)S(1)}, f32[8,16,256]{2,1,0:T(8,128)S(1)}, u32[]{:S(2)}, u32[]{:S(2)}) collective-permute-start(f32[8,16,256]{2,1,0:T(8,128)S(1)} %get-tuple-element.38), channel_id=1, source_target_pairs={{0,4},{4,0},{8,12},{12,8},{1,5},{5,1},{9,13},{13,9},{2,6},{6,2},{1... | collective-permute-start | bytes 393224 | tf_op jit(solution)/shard_map/ppermute | solution.py:341
  38.4 1.1 %collective-permute-start.8 = (f32[8,16,256]{2,1,0:T(8,128)S(1)}, f32[8,16,256]{2,1,0:T(8,128)S(1)}, u32[]{:S(2)}, u32[]{:S(2)}) collective-permute-start(f32[8,16,256]{2,1,0:T(8,128)S(1)} %get-tuple-element.39), channel_id=1, source_target_pairs={{0,8},{4,12},{8,0},{12,4},{1,9},{5,13},{9,1},{13,5},{2,10},{6,14},... | collective-permute-start | bytes 393224 | tf_op jit(solution)/shard_map/ppermute | solution.py:341
  39.5 1.1 %collective-permute-start.9 = (f32[8,16,256]{2,1,0:T(8,128)S(1)}, f32[8,16,256]{2,1,0:T(8,128)S(1)}, u32[]{:S(2)}, u32[]{:S(2)}) collective-permute-start(f32[8,16,256]{2,1,0:T(8,128)S(1)} %get-tuple-element.40), channel_id=1, source_target_pairs={{0,12},{4,8},{8,4},{12,0},{1,13},{5,9},{9,5},{13,1},{2,14},{6,10},... | collective-permute-start | bytes 393224 | tf_op jit(solution)/shard_map/ppermute | solution.py:341
  40.6 3.3 %last.1 = (f32[1,2,32,16,256]{4,3,2,1,0:T(8,128)}, f32[1,2,32,16,256]{4,3,2,1,0:T(8,128)}) custom-call(s32[1,3]{1,0:T(1,128)S(1)} %copy-done.3, f32[1,2]{1,0:T(1,128)S(1)} %copy-done.4, f32[32,16,256]{2,1,0:T(8,128)S(1)} %slice_bitcast_fusion.forward, f32[32,16,256]{2,1,0:T(8,128)S(1)} %get-tuple-element.30.p1, f32[32,16,256]{2,1,0:T(8,128)S(1)} %get-tuple-element.31.q1, ...), custom_call_target="tpu_custom_call" | custom-call | tf_op jit(solution)/shard_map/last/pallas_call | solution.py:35
  43.9 0.0 collective-permute-done.7.refs_1_
  43.9 3.9 %collective-permute-done.8.refs_2_ = f32[8,16,256]{2,1,0:T(8,128)S(1)} collective-permute-done((f32[8,16,256]{2,1,0:T(8,128)S(1)}, f32[8,16,256]{2,1,0:T(8,128)S(1)}, u32[]{:S(2)}, u32[]{:S(2)}) %collective-permute-start.8) | collective-permute-done | bytes 131104 | tf_op jit(solution)/shard_map/ppermute | solution.py:341
  47.8 0.0 collective-permute-done.9.refs_3_
  47.8 0.7 %gradient.1 = f32[8,16,256]{2,1,0:T(8,128)} custom-call(f32[8,16,256]{2,1,0:T(8,128)S(1)} %copy-done.2, f32[8,16,256]{2,1,0:T(8,128)S(1)} %get-tuple-element.37.refs_0_, f32[8,16,256]{2,1,0:T(8,128)S(1)} %collective-permute-done.7.refs_1_, f32[8,16,256]{2,1,0:T(8,128)S(1)} %collective-permute-done.8.refs_2_, f32[8,16,256]{2,1,0:T(8,128)S(1)} %collective-permute-done.9.refs_3_), custom_call_target="tpu_custom_call" | custom-call | tf_op jit(solution)/shard_map/gradient/pallas_call | solution.py:35
  (2 shorter events, 0.0 us)
Async XLA Ops:
  0.6 15.0 %copy-start = (f32[1,2,32,16,256]{4,3,2,1,0:T(8,128)S(1)}, f32[1,2,32,16,256]{4,3,2,1,0:T(8,128)}, u32[]{:S(2)}) copy-start(f32[1,2,32,16,256]{4,3,2,1,0:T(8,128)} %forward.1) | copy-start | bytes 3145732
  0.6 15.0 %copy-start.1 = (f32[1,2,32,16,256]{4,3,2,1,0:T(8,128)S(1)}, f32[1,2,32,16,256]{4,3,2,1,0:T(8,128)}, u32[]{:S(2)}) copy-start(f32[1,2,32,16,256]{4,3,2,1,0:T(8,128)} %adjoint.1) | copy-start | bytes 3145732
  2.8 10.9 %copy-start.6 = (s32[1,3,256]{2,0,1:T(1,128)S(1)}, s32[1,3,256]{2,0,1:T(1,128)}, u32[]{:S(2)}) copy-start(s32[1,3,256]{2,0,1:T(1,128)} %param.11) | copy-start | bytes 9220
  2.8 11.0 %collective-permute-start = (f32[32,8,256]{2,1,0:T(8,128)}, f32[32,8,256]{2,1,0:T(8,128)S(1)}, u32[]{:S(2)}, u32[]{:S(2)}) collective-permute-start(f32[32,8,256]{2,1,0:T(8,128)} %get-tuple-element.24), channel_id=1, source_target_pairs={{0,1},{1,2},{2,3},{4,5},{5,6},{6,7},{8,9},{9,10},{10,11},{12,13},{... | collective-permute-start | bytes 786440 | tf_op jit(solution)/shard_map/ppermute | solution.py:287
  7.5 8.2 %collective-permute-start.1 = (f32[32,8,256]{2,1,0:T(8,128)}, f32[32,8,256]{2,1,0:T(8,128)S(1)}, u32[]{:S(2)}, u32[]{:S(2)}) collective-permute-start(f32[32,8,256]{2,1,0:T(8,128)} %get-tuple-element.25), channel_id=1, source_target_pairs={{1,0},{2,1},{3,2},{5,4},{6,5},{7,6},{9,8},{10,9},{11,10},{13,12},{... | collective-permute-start | bytes 786440 | tf_op jit(solution)/shard_map/ppermute | solution.py:287
  9.4 10.1 %collective-permute-start.2 = (f32[8,16,256]{2,1,0:T(8,128)}, f32[8,16,256]{2,1,0:T(8,128)S(1)}, u32[]{:S(2)}, u32[]{:S(2)}) collective-permute-start(f32[8,16,256]{2,1,0:T(8,128)} %velocity.1), channel_id=1, source_target_pairs={{0,4},{4,0},{8,12},{12,8},{1,5},{5,1},{9,13},{13,9},{2,6},{6,2},{1... | collective-permute-start | bytes 393224 | tf_op jit(solution)/shard_map/ppermute | solution.py:300
  10.8 11.9 %collective-permute-start.3 = (f32[8,16,256]{2,1,0:T(8,128)}, f32[8,16,256]{2,1,0:T(8,128)S(1)}, u32[]{:S(2)}, u32[]{:S(2)}) collective-permute-start(f32[8,16,256]{2,1,0:T(8,128)} %velocity.1), channel_id=1, source_target_pairs={{0,8},{4,12},{8,0},{12,4},{1,9},{5,13},{9,1},{13,5},{2,10},{6,14},... | collective-permute-start | bytes 393224 | tf_op jit(solution)/shard_map/ppermute | solution.py:300
  13.1 9.6 %collective-permute-start.4 = (f32[8,16,256]{2,1,0:T(8,128)}, f32[8,16,256]{2,1,0:T(8,128)S(1)}, u32[]{:S(2)}, u32[]{:S(2)}) collective-permute-start(f32[8,16,256]{2,1,0:T(8,128)} %velocity.1), channel_id=1, source_target_pairs={{0,12},{4,8},{8,4},{12,0},{1,13},{5,9},{9,5},{13,1},{2,14},{6,10},... | collective-permute-start | bytes 393224 | tf_op jit(solution)/shard_map/ppermute | solution.py:300
  13.7 1.9 %copy-start.3 = (s32[1,3]{1,0:T(1,128)S(1)}, s32[1,3]{1,0:T(1,128)}, u32[]{:S(2)}) copy-start(s32[1,3]{1,0:T(1,128)} %source.5) | copy-start | bytes 40
  13.7 1.9 %copy-start.4 = (f32[1,2]{1,0:T(1,128)S(1)}, f32[1,2]{1,0:T(1,128)}, u32[]{:S(2)}) copy-start(f32[1,2]{1,0:T(1,128)} %wavelet.5) | copy-start | bytes 28
  13.7 1.9 %copy-start.5 = (f32[1,2,256]{2,1,0:T(2,128)S(1)}, f32[1,2,256]{2,1,0:T(2,128)}, u32[]{:S(2)}) copy-start(f32[1,2,256]{2,1,0:T(2,128)} %residuals.1) | copy-start | bytes 6148
  13.8 8.9 %copy-start.2 = (f32[8,16,256]{2,1,0:T(8,128)S(1)}, f32[8,16,256]{2,1,0:T(8,128)}, u32[]{:S(2)}) copy-start(f32[8,16,256]{2,1,0:T(8,128)} %velocity.1) | copy-start | bytes 393220
  22.9 7.4 %collective-permute-start.5 = (f32[32,8,256]{2,1,0:T(8,128)S(1)}, f32[32,8,256]{2,1,0:T(8,128)S(1)}, u32[]{:S(2)}, u32[]{:S(2)}) collective-permute-start(f32[32,8,256]{2,1,0:T(8,128)S(1)} %get-tuple-element.35), channel_id=1, source_target_pairs={{0,1},{1,2},{2,3},{4,5},{5,6},{6,7},{8,9},{9,10},{10,11},{12,13},{... | collective-permute-start | bytes 786440 | tf_op jit(solution)/shard_map/ppermute | solution.py:287
  27.0 7.7 %collective-permute-start.6 = (f32[32,8,256]{2,1,0:T(8,128)S(1)}, f32[32,8,256]{2,1,0:T(8,128)S(1)}, u32[]{:S(2)}, u32[]{:S(2)}) collective-permute-start(f32[32,8,256]{2,1,0:T(8,128)S(1)} %get-tuple-element.36), channel_id=1, source_target_pairs={{1,0},{2,1},{3,2},{5,4},{6,5},{7,6},{9,8},{10,9},{11,10},{13,12},{... | collective-permute-start | bytes 786440 | tf_op jit(solution)/shard_map/ppermute | solution.py:287
  36.7 7.3 %collective-permute-start.7 = (f32[8,16,256]{2,1,0:T(8,128)S(1)}, f32[8,16,256]{2,1,0:T(8,128)S(1)}, u32[]{:S(2)}, u32[]{:S(2)}) collective-permute-start(f32[8,16,256]{2,1,0:T(8,128)S(1)} %get-tuple-element.38), channel_id=1, source_target_pairs={{0,4},{4,0},{8,12},{12,8},{1,5},{5,1},{9,13},{13,9},{2,6},{6,2},{1... | collective-permute-start | bytes 393224 | tf_op jit(solution)/shard_map/ppermute | solution.py:341
  38.4 9.4 %collective-permute-start.8 = (f32[8,16,256]{2,1,0:T(8,128)S(1)}, f32[8,16,256]{2,1,0:T(8,128)S(1)}, u32[]{:S(2)}, u32[]{:S(2)}) collective-permute-start(f32[8,16,256]{2,1,0:T(8,128)S(1)} %get-tuple-element.39), channel_id=1, source_target_pairs={{0,8},{4,12},{8,0},{12,4},{1,9},{5,13},{9,1},{13,5},{2,10},{6,14},... | collective-permute-start | bytes 393224 | tf_op jit(solution)/shard_map/ppermute | solution.py:341
  39.5 8.3 %collective-permute-start.9 = (f32[8,16,256]{2,1,0:T(8,128)S(1)}, f32[8,16,256]{2,1,0:T(8,128)S(1)}, u32[]{:S(2)}, u32[]{:S(2)}) collective-permute-start(f32[8,16,256]{2,1,0:T(8,128)S(1)} %get-tuple-element.40), channel_id=1, source_target_pairs={{0,12},{4,8},{8,4},{12,0},{1,13},{5,9},{9,5},{13,1},{2,14},{6,10},... | collective-permute-start | bytes 393224 | tf_op jit(solution)/shard_map/ppermute | solution.py:341

commit v2 on v1

v2 whole, which is shorter than its diff:
```python
import functools

import jax
import jax.numpy as jnp
from jax import lax
from jax.experimental import pallas as pl
from jax.experimental.pallas import tpu as pltpu
from jax.sharding import PartitionSpec as P

APT = 4
RIM = 4
STENCIL_COEFS = (-205.0 / 72.0, 8.0 / 5.0, -1.0 / 5.0, 8.0 / 315.0, -1.0 / 560.0)
SPACING_RATIO = 0.1

F32 = jnp.float32
BF16 = jnp.bfloat16
IN_VMEM = pl.BlockSpec(memory_space=pltpu.VMEM)
IN_SMEM = pl.BlockSpec(memory_space=pltpu.SMEM)
LONG = pl.CostEstimate(flops=10**9, bytes_accessed=10**8, transcendentals=0)


def kept(shape):
    return pltpu.VMEM(shape, F32)


def given(shape):
    return jax.ShapeDtypeStruct(shape, F32)


def on_chip(value):
    return pltpu.with_memory_space_constraint(value, pltpu.VMEM)


def call(kernel, outs, ins, out_specs=None, scratch=(), name=None, long=False):
    return pl.pallas_call(
        kernel,
        out_shape=tuple(outs),
        in_specs=[spec for spec, _ in ins],
        out_specs=tuple(out_specs or [IN_VMEM] * len(outs)),
        scratch_shapes=list(scratch),
        compiler_params=pltpu.CompilerParams(vmem_limit_bytes=40 * 1024 * 1024),
        cost_estimate=LONG if long else None,
        name=name,
    )(*[array for _, array in ins])


def partners(count):
    reach = APT - 1
    if count <= 2 * reach and count & (count - 1) == 0:
        plans = []
        for bit in range(1, count):
            pairs = [(i, i ^ bit) for i in range(count)]
            plans.append((pairs, pairs, functools.partial(lambda bit, i: i ^ bit, bit)))
        return plans
    if count <= 2 * reach:
        offsets = range(1, count)
    else:
        offsets = [o for o in range(-reach, reach + 1) if o != 0]
    plans = []
    for o in offsets:
        fetch = [((i + o) % count, i) for i in range(count)]
        send = [(i, (i + o) % count) for i in range(count)]
        plans.append((fetch, send, functools.partial(lambda o, i: lax.rem(i + o + count, count), o)))
    return plans


def y_operator(width):
    row = lax.broadcasted_iota(jnp.int32, (width, width), 0)
    column = lax.broadcasted_iota(jnp.int32, (width, width), 1)
    apart = jnp.abs(row - column)
    total = jnp.zeros((width, width), F32)
    for o in range(1, RIM + 1):
        total = jnp.where(apart == o, F32(STENCIL_COEFS[o]), total)
    high = total.astype(BF16)
    return high, (total - high.astype(F32)).astype(BF16)


def y_part(field, high, low):
    rows, depth, width = field.shape
    flat = field.reshape(rows * depth, width)
    top = flat.astype(BF16)
    rest = (flat - top.astype(F32)).astype(BF16)
    total = jnp.dot(top, high, preferred_element_type=F32)
    total = total + jnp.dot(rest, high, preferred_element_type=F32)
    total = total + jnp.dot(top, low, preferred_element_type=F32)
    return total.reshape(rows, depth, width)


def xz_part(padded, x, own, depth):
    total = F32(3.0 * STENCIL_COEFS[0]) * own
    window = jnp.concatenate([own, jnp.zeros((2 * RIM,) + own.shape[1:], F32)], axis=0)
    rows = depth + 2 * RIM
    for o in range(1, RIM + 1):
        pair = padded[x + RIM + o] + padded[x + RIM - o]
        below = pltpu.roll(window, rows - o, 0)[:depth]
        above = pltpu.roll(window, o, 0)[:depth]
        total = total + F32(STENCIL_COEFS[o]) * (pair + (below + above))
    return total


def rim_part(rim):
    axis, size = rim.ndim - 2, 2 * RIM
    line = lax.broadcasted_iota(jnp.int32, rim.shape, axis)
    first, last = jnp.zeros(rim.shape, F32), jnp.zeros(rim.shape, F32)
    for o in range(1, RIM + 1):
        coef = F32(STENCIL_COEFS[o])
        first = first + jnp.where(line < o, coef, 0.0) * pltpu.roll(rim, o, axis)
        last = last + jnp.where(line >= size - o, coef, 0.0) * pltpu.roll(rim, size - o, axis)
    return first, last


def fill_padded(padded, field):
    rows = padded.shape[0] - 2 * RIM
    zero = jnp.zeros((RIM,) + padded.shape[1:], F32)
    padded[0:RIM] = zero
    padded[RIM + rows : RIM + rows + RIM] = zero
    padded[RIM : RIM + rows] = field


def first_four(shape):
    return lax.broadcasted_iota(jnp.int32, shape, len(shape) - 2) < RIM


def is_even():
    return lax.rem(lax.axis_index("sub"), 2) == 0


def pack_rims(field):
    rows, depth, _ = field.shape
    half = rows // 2
    first, last = field[:, 0 : 2 * RIM], field[:, depth - 2 * RIM : depth]
    here = first_four(first[:half].shape)
    deeper = jnp.where(here, pltpu.roll(last[:half], RIM, 1), last[half:])
    shallower = jnp.where(here, first[:half], pltpu.roll(first[half:], RIM, 1))
    even = is_even()
    return jnp.where(even, deeper, shallower), jnp.where(even, shallower, deeper)


def unpack_rims(pair, other):
    even = is_even()
    above, below = jnp.where(even, other, pair), jnp.where(even, pair, other)
    here = first_four(above.shape)
    low = jnp.where(here, below, pltpu.roll(above, RIM, 1))
    high = jnp.where(here, pltpu.roll(below, RIM, 1), above)
    return low, high


def add_rims(pair, other, add):
    half = pair.shape[0]
    for index, rim in enumerate(unpack_rims(pair[...], other[...])):
        add(slice(index * half, (index + 1) * half), *rim_part(rim))


def cell_mask(source, depth, width):
    start = lax.axis_index("sub") * depth
    layer = lax.broadcasted_iota(jnp.int32, (depth, width), 0)
    column = lax.broadcasted_iota(jnp.int32, (depth, width), 1)
    return (layer == source[0, 1] - start) & (column == source[0, 2])


def rims_kernel(p_ref, q_ref, pair, other):
    half = pair.shape[0] // 2
    for index, ref in enumerate((p_ref, q_ref)):
        span = slice(index * half, (index + 1) * half)
        pair[span], other[span] = pack_rims(ref[...])


def first_kernel(
    source, wavelet, receivers, residuals, forward, adjoint,
    free_p, lap_p, free_q, lap_q, free_q2, injected, padded, spread,
):
    rows, depth, width = lap_p.shape
    high, low = y_operator(width)
    start = lax.axis_index("sub") * depth

    first, layer, column = receivers[0, 0:1], receivers[0, 1:2] - start, receivers[0, 2:3]
    inside = (layer >= 0) & (layer < depth)
    place = jnp.where(inside, first * depth + layer, -1)
    count = place.shape[1]
    lines = lax.broadcasted_iota(jnp.int32, (rows * depth, count), 0)
    onto = (lines == place).astype(F32).astype(BF16)
    columns = lax.broadcasted_iota(jnp.int32, (width, count), 0)
    for step in range(2):
        value = jnp.where(columns == column, residuals[0, step : step + 1], 0.0)
        total = None
        for _ in range(3):
            part = value.astype(BF16)
            value = value - part.astype(F32)
            term = lax.dot_general(onto, part, (((1,), (1,)), ((), ())), preferred_element_type=F32)
            total = term if total is None else total + term
        spread[step] = total.reshape(rows, depth, width)

    here = cell_mask(source, depth, width)
    for name, pair, lap, free in (("p", forward, lap_p, free_p), ("q", adjoint, lap_q, free_q)):
        fill_padded(padded, pair[0, 1])
        lap[...] = y_part(pair[0, 1], high, low)

        def row(x, _):
            own = pair[0, 1, x]
            lap[x] = lap[x] + xz_part(padded, x, own, depth)
            moved = 2.0 * own - pair[0, 0, x]
            if name == "q":
                moved = moved + spread[0, x]
                free_q2[x] = spread[1, x] - own
            free[x] = moved
            return 0

        lax.fori_loop(0, rows, row, 0, unroll=2)
    x0 = source[0, 0]
    amount = jnp.where(here, wavelet[0, 0], 0.0)
    free_p[x0] = free_p[x0] + amount
    injected[...] = adjoint[0, 1, x0] * amount


def add_rims_to(full, pair, other):
    edge = full.shape[1] - 2 * RIM

    def add(span, first, last):
        full[span, 0 : 2 * RIM] = full[span, 0 : 2 * RIM] + first
        full[span, edge:] = full[span, edge:] + last

    add_rims(pair, other, add)


def full_kernel(lap_p, lap_q, pair, other, now_q, full_p, full_q, mixed):
    half = pair.shape[0] // 2
    for index, (lap, full) in enumerate(((lap_p, full_p), (lap_q, full_q))):
        full[...] = lap[...]
        part = slice(index * half, (index + 1) * half)
        add_rims_to(full, pair.at[part], other.at[part])
    mixed[...] = now_q[...] * full_p[...]


def step_kernel(plans, anchors, free_p, free_q, full_p, full_q, *refs):
    tiles, (courant, p1, q1, pair_p, other_p) = refs[: len(plans) + 1], refs[len(plans) + 1 :]
    tile_rows = tiles[0].shape[0]
    for tile, place in zip(tiles, places(plans, anchors)):

        def put():
            speed = F32(SPACING_RATIO) * tile[...]
            factor = speed * speed
            span = pl.ds(place * tile_rows, tile_rows)
            courant[span] = factor
            p1[span] = free_p[span] + factor * full_p[span]
            q1[span] = free_q[span] + factor * full_q[span]

        pl.when((place >= 0) & (place < APT))(put)
    pair_p[...], other_p[...] = pack_rims(p1[...])


def places(plans, anchors):
    count = lax.axis_size("shot")
    me = lax.axis_index("shot")
    peers = [me] + [peer(me) for _, _, peer in plans]
    return [lax.rem(peer - anchors[0] + count, count) for peer in peers]


def inner_kernel(source, wavelet, p1, q1, courant, mixed, injected, lap_p, image, padded):
    rows, depth, width = p1.shape
    high, low = y_operator(width)
    fill_padded(padded, p1[...])
    lap_p[...] = y_part(p1[...], high, low)

    def row(x, _):
        value = lap_p[x] + xz_part(padded, x, p1[x], depth)
        lap_p[x] = value
        image[x] = courant[x] * (mixed[x] + q1[x] * value)
        return 0

    lax.fori_loop(0, rows, row, 0, unroll=2)
    x0 = source[0, 0]
    amount = jnp.where(cell_mask(source, depth, width), wavelet[0, 1], 0.0)
    image[x0] = image[x0] + injected[...] + q1[x0] * amount


def image_kernel(plans, anchors, q1, courant, lap_p, image, pair, other, *refs):
    outs, (full_p, whole) = refs[: len(plans) + 1], refs[len(plans) + 1 :]
    depth = q1.shape[1]
    edge = depth - 2 * RIM
    full_p[...] = lap_p[...]
    whole[...] = image[...]

    def add(span, first, last):
        for lines, more in ((slice(0, 2 * RIM), first), (slice(edge, depth), last)):
            full_p[span, lines] = full_p[span, lines] + more
            whole[span, lines] = whole[span, lines] + courant[span, lines] * (q1[span, lines] * more)

    add_rims(pair, other, add)
    tile_rows = outs[0].shape[0]
    for out, place in zip(outs, places(plans, anchors)):
        inside = (place >= 0) & (place < APT)

        def put():
            out[...] = whole[pl.ds(place * tile_rows, tile_rows)]

        def clear():
            out[...] = jnp.zeros(out.shape, F32)

        pl.when(inside)(put)
        pl.when(jnp.logical_not(inside))(clear)


def rims_q_kernel(q1, _, pair, other):
    pair[...], other[...] = pack_rims(q1[...])


def last_kernel(source, wavelet, forward, p1, q1, courant, lap_p, free_q2, forward_out, part_q, padded):
    rows, depth, width = p1.shape
    high, low = y_operator(width)
    fill_padded(padded, q1[...])
    part_q[...] = y_part(q1[...], high, low)

    def row(x, _):
        own_p, own_q, factor = p1[x], q1[x], courant[x]
        forward_out[0, 0, x] = own_p
        forward_out[0, 1, x] = 2.0 * own_p - forward[x] + factor * lap_p[x]
        value = part_q[x] + xz_part(padded, x, own_q, depth)
        part_q[x] = 2.0 * own_q + free_q2[x] + factor * value
        return 0

    lax.fori_loop(0, rows, row, 0, unroll=2)
    x0 = source[0, 0]
    amount = jnp.where(cell_mask(source, depth, width), wavelet[0, 1], 0.0)
    forward_out[0, 1, x0] = forward_out[0, 1, x0] + amount


def last_q_kernel(q1, courant, part_q, pair, other, adjoint_out):
    edge = q1.shape[1] - 2 * RIM
    adjoint_out[0, 0] = q1[...]
    adjoint_out[0, 1] = part_q[...]

    def add(span, first, last):
        for lines, more in ((slice(0, 2 * RIM), first), (slice(edge, None), last)):
            adjoint_out[0, 1, span, lines] = adjoint_out[0, 1, span, lines] + courant[span, lines] * more

    add_rims(pair, other, add)


def gradient_kernel(velocity, *refs):
    parts, out = refs[:-1], refs[-1]
    total = parts[0][...]
    for part in parts[1:]:
        total = total + part[...]
    out[...] = -(2.0 / velocity[...]) * total


def swap_rims(pair, other):
    count = lax.axis_size("sub")

    def both_ways(start):
        ahead = [(i, i + 1) for i in range(start, count - 1, 2)]
        return ahead + [(i, j) for j, i in ahead]

    return lax.ppermute(pair, "sub", both_ways(0)), lax.ppermute(other, "sub", both_ways(1))


def on_device(
    velocity, anchors, source_cells, receiver_cells, wavelet, residuals, forward_pair, adjoint_pair
):
    tile_rows, depth, width = velocity.shape
    rows = APT * tile_rows
    field = (rows, depth, width)
    rim = (rows // 2, 2 * RIM, width)
    padded = pltpu.VMEM((rows + 2 * RIM, depth, width), F32)
    plans = partners(lax.axis_size("shot"))

    tiles = [velocity] + [lax.ppermute(velocity, "shot", fetch) for fetch, _, _ in plans]

    now = pl.BlockSpec((None, None, rows, depth, width), lambda i: (0, 1, 0, 0, 0))
    two_rims = pl.BlockSpec((rows, 2 * RIM, width), lambda i: (0, 0, 0))
    pair, other = pl.pallas_call(
        rims_kernel, out_shape=(given((rows, 2 * RIM, width)),) * 2, grid=(1,), in_specs=[now, now],
        out_specs=(two_rims,) * 2, name="rims",
    )(forward_pair, adjoint_pair)
    pair, other = swap_rims(pair, other)

    free_p, lap_p, free_q, lap_q, free_q2, injected = call(
        first_kernel,
        [kept(field)] * 5 + [kept((depth, width))],
        [
            (IN_SMEM, source_cells), (IN_SMEM, wavelet), (IN_VMEM, receiver_cells), (IN_VMEM, residuals),
            (IN_VMEM, forward_pair), (IN_VMEM, adjoint_pair),
        ],
        scratch=[padded, pltpu.VMEM((2,) + field, F32)],
        name="first",
        long=True,
    )

    full_p, full_q, mixed = call(
        full_kernel,
        [kept(field)] * 3,
        [(IN_VMEM, on_chip(a)) for a in (lap_p, lap_q)]
        + [(IN_VMEM, pair), (IN_VMEM, other), (IN_VMEM, adjoint_pair[0, 1])],
        name="full",
    )
    courant, p1, q1, pair_p, other_p = call(
        functools.partial(step_kernel, plans),
        [kept(field)] * 3 + [given(rim)] * 2,
        [(IN_SMEM, anchors)]
        + [(IN_VMEM, on_chip(a)) for a in (free_p, free_q, full_p, full_q)]
        + [(IN_VMEM, tile) for tile in tiles],
        name="step",
    )
    pair_p, other_p = swap_rims(pair_p, other_p)

    lap_p1, image = call(
        inner_kernel,
        [kept(field)] * 2,
        [(IN_SMEM, source_cells), (IN_SMEM, wavelet)]
        + [(IN_VMEM, on_chip(a)) for a in (p1, q1, courant, mixed, injected)],
        scratch=[padded],
        name="inner",
    )
    *images, lap_p1 = call(
        functools.partial(image_kernel, plans),
        [given(velocity.shape)] * len(tiles) + [kept(field)],
        [(IN_SMEM, anchors)]
        + [(IN_VMEM, on_chip(a)) for a in (q1, courant, lap_p1, image)]
        + [(IN_VMEM, pair_p), (IN_VMEM, other_p)],
        scratch=[pltpu.VMEM(field, F32)],
        name="image",
    )
    gathered = [images[0]] + [
        lax.ppermute(image, "shot", send) for image, (_, send, _) in zip(images[1:], plans)
    ]

    pair_q, other_q = call(
        rims_q_kernel, [given(rim)] * 2, [(IN_VMEM, on_chip(a)) for a in (q1, lap_p1)], name="rims_q"
    )
    pair_q, other_q = swap_rims(pair_q, other_q)
    forward_out, part_q = call(
        last_kernel,
        [given(forward_pair.shape), kept(field)],
        [(IN_SMEM, source_cells), (IN_SMEM, wavelet), (IN_VMEM, forward_pair[0, 1])]
        + [(IN_VMEM, on_chip(a)) for a in (p1, q1, courant, lap_p1, free_q2)],
        scratch=[padded],
        name="last",
        long=True,
    )
    (adjoint_out,) = call(
        last_q_kernel,
        [given(adjoint_pair.shape)],
        [(IN_VMEM, on_chip(a)) for a in (q1, courant, part_q)] + [(IN_VMEM, pair_q), (IN_VMEM, other_q)],
        name="last_q",
    )

    (gradient,) = call(
        gradient_kernel,
        [given(velocity.shape)],
        [(IN_VMEM, velocity)] + [(IN_VMEM, part) for part in gathered],
        name="gradient",
    )
    return gradient, forward_out, adjoint_out


def solution(mesh):
    shot = ("grp", "shot")
    fields = P(shot, None, None, "sub", None)
    return jax.shard_map(
        on_device,
        mesh=mesh,
        in_specs=(
            P(shot, "sub", None),
            P(shot),
            P(shot, None),
            P(shot, None, None),
            P(shot, None),
            P(shot, None, None),
            fields,
            fields,
        ),
        out_specs=(P(shot, "sub", None), fields, fields),
        check_vma=False,
    )
```

time: 48.7 us -> 37.5 us (0.77)
  waiting for transfers between devices: 14.6 us -> 1.73 us
  Pallas kernels: 12.1 us -> 14 us
  starting transfers between devices: 20.2 us -> 19.2 us
  local copies, waits for them, and re-layouts: 0.07 us -> 0.91 us
    ppermute x4 -> x6, waiting for transfers between devices: 7.63 us -> 1.71 us  [the longest x3 1.7 us: swap_rims(): lax.ppermute(other, 'sub', both_ways(1))]
    ppermute x3, waiting for transfers between devices: 3.86 us -> 0.01 us  [on_device(): lax.ppermute(image, 'shot', send)]
    ppermute x3, waiting for transfers between devices: 3.14 us -> 0.01 us  [on_device(): lax.ppermute(velocity, 'shot', fetch)]
    pallas_call x5 -> x9, Pallas kernels: 9.96 us -> 11.9 us  [call(): pl.pallas_call(kernel, out_shape=tuple(outs), in_specs=[spec for spec, _...]
    ppermute x4 -> x6, starting transfers between devices: 12.6 us -> 11 us  [the longest x3 9.62 us: swap_rims(): lax.ppermute(other, 'sub', both_ways(1))]
    ppermute x3, starting transfers between devices: 3.67 us -> 4.5 us  [on_device(): lax.ppermute(velocity, 'shot', fetch)]
    unnamed x15, local copies, waits for them, and re-layouts: 0.04 us -> 0.84 us
  transfers between devices with their start and end apart: 10 -> 12, of which waited for: 5 -> 1; matrix products, arithmetic and copies ran while one was open for 0% -> 0% of each run, Pallas kernels for 15% -> 34%
where the time goes in v2:
time: 37.5 us; the launch traced here: 37.3 us
  starting transfers between devices  19.2 us (51%)
  Pallas kernels  14 us (37%)
  waiting for transfers between devices  1.73 us (5%)
  between operations  1.51 us (4%)
  local copies, waits for them, and re-layouts  0.91 us (2%)
    pallas_call x9, Pallas kernels, call(): pl.pallas_call(kernel, out_shape=tuple(outs), in_specs=[spec for spec, _...  11.9 us
    ppermute x3, starting transfers between devices, swap_rims(): lax.ppermute(other, 'sub', both_ways(1))  9.62 us
    ppermute x3, starting transfers between devices, on_device(): lax.ppermute(velocity, 'shot', fetch)  4.5 us
    ppermute x3, starting transfers between devices, on_device(): lax.ppermute(image, 'shot', send)  3.68 us
    pallas_call x1, Pallas kernels, on_device(): pl.pallas_call(rims_kernel, out_shape=(given((rows, 2 * RIM, width)),) *...  2.05 us
    ppermute x3, waiting for transfers between devices, swap_rims(): lax.ppermute(other, 'sub', both_ways(1))  1.7 us
    ppermute x3, starting transfers between devices, swap_rims(): lax.ppermute(pair, 'sub', both_ways(0))  1.38 us
    unnamed x15, local copies, waits for them, and re-layouts  0.84 us
  transfers between devices with their start and end apart: 12, of which 1 were waited for; matrix products, arithmetic and copies ran while one was open for 0% of the time, Pallas kernels for 34%

profile of v2, /device:TPU:1, one launch (start us, length us, event | category | flops | bytes accessed | tf_op | source)
XLA Modules:
  0.0 37.3 jit_solution(14860909902037183203)
XLA Ops:
  0.6 0.0 copy-start
  0.6 2.2 %collective-permute-start.2 = (f32[8,16,256]{2,1,0:T(8,128)}, f32[8,16,256]{2,1,0:T(8,128)S(1)}, u32[]{:S(2)}, u32[]{:S(2)}) collective-permute-start(f32[8,16,256]{2,1,0:T(8,128)} %velocity.1), channel_id=1, source_target_pairs={{0,4},{4,0},{8,12},{12,8},{1,5},{5,1},{9,13},{13,9},{2,6},{6,2},{1... | collective-permute-start | bytes 393224 | tf_op jit(solution)/shard_map/ppermute | solution.py:367
  2.8 2.3 %collective-permute-start.3 = (f32[8,16,256]{2,1,0:T(8,128)}, f32[8,16,256]{2,1,0:T(8,128)S(1)}, u32[]{:S(2)}, u32[]{:S(2)}) collective-permute-start(f32[8,16,256]{2,1,0:T(8,128)} %velocity.1), channel_id=1, source_target_pairs={{0,8},{4,12},{8,0},{12,4},{1,9},{5,13},{9,1},{13,5},{2,10},{6,14},... | collective-permute-start | bytes 393224 | tf_op jit(solution)/shard_map/ppermute | solution.py:367
  5.1 0.0 collective-permute-start.4
  5.1 2.0 %rims.1 = (f32[32,8,256]{2,1,0:T(8,128)}, f32[32,8,256]{2,1,0:T(8,128)}) custom-call(f32[1,2,32,16,256]{4,3,2,1,0:T(8,128)} %p_ref.1, f32[1,2,32,16,256]{4,3,2,1,0:T(8,128)} %q_ref.1), custom_call_target="tpu_custom_call" | custom-call | tf_op jit(solution)/shard_map/rims/pallas_call | solution.py:371
  7.2 0.0 copy-start.1
  7.2 1.2 %collective-permute-start = (f32[32,8,256]{2,1,0:T(8,128)}, f32[32,8,256]{2,1,0:T(8,128)S(1)}, u32[]{:S(2)}, u32[]{:S(2)}) collective-permute-start(f32[32,8,256]{2,1,0:T(8,128)} %get-tuple-element.34), channel_id=1, source_target_pairs={{0,1},{2,3},{1,0},{3,2},{4,5},{6,7},{5,4},{7,6},{8,9},{10,11},{9,8... | collective-permute-start | bytes 786440 | tf_op jit(solution)/shard_map/ppermute | solution.py:354
  8.4 3.3 %collective-permute-start.1 = (f32[32,8,256]{2,1,0:T(8,128)}, f32[32,8,256]{2,1,0:T(8,128)S(1)}, u32[]{:S(2)}, u32[]{:S(2)}) collective-permute-start(f32[32,8,256]{2,1,0:T(8,128)} %get-tuple-element.35), channel_id=1, source_target_pairs={{1,2},{2,1},{5,6},{6,5},{9,10},{10,9},{13,14},{14,13},{17,18},{18,... | collective-permute-start | bytes 786440 | tf_op jit(solution)/shard_map/ppermute | solution.py:354
  11.8 0.0 copy-done
  11.8 0.0 copy-start.6
  12.5 0.0 copy-done.6
  12.5 0.0 copy-start.3
  12.5 0.0 copy-start.4
  12.5 0.0 copy-start.5
  12.6 0.0 copy-done.1
  12.6 0.6 %copy-done.3 = s32[1,3]{1,0:T(1,128)S(1)} copy-done((s32[1,3]{1,0:T(1,128)S(1)}, s32[1,3]{1,0:T(1,128)}, u32[]{:S(2)}) %copy-start.3) | copy-done | bytes 36
  13.2 0.0 copy-done.4
  13.2 0.0 copy-done.5
  13.2 3.7 %first.1 = (f32[32,16,256]{2,1,0:T(8,128)S(1)}, f32[32,16,256]{2,1,0:T(8,128)S(1)}, f32[32,16,256]{2,1,0:T(8,128)S(1)}, f32[32,16,256]{2,1,0:T(8,128)S(1)}, f32[...) custom-call(s32[1,3]{1,0:T(1,128)S(1)} %copy-done.3, f32[1,2]{1,0:T(1,128)S(1)} %copy-done.4, ...), custom_call_target="tpu_custom_call" | custom-call | flops 1000000000 | bytes 100000000 | tf_op jit(solution)/shard_map/first/pallas_call | solution.py:35
  16.9 0.0 collective-permute-done.pair
  16.9 0.0 collective-permute-done.1.other
  16.9 0.0 copy-start.2
  16.9 0.7 %full.1 = (f32[32,16,256]{2,1,0:T(8,128)S(1)}, f32[32,16,256]{2,1,0:T(8,128)S(1)}, f32[32,16,256]{2,1,0:T(8,128)S(1)}) custom-call(f32[32,16,256]{2,1,0:T(8,128)S(1)} %get-tuple-element.32.lap_p, f32[32,16,256]{2,1,0:T(8,128)S(1)} %get-tuple-element.33.lap_q, f32[32,8,256]{2,1,0:T(8,128)S(1)} %collective-permute-done.pair, ...), custom_call_target="tpu_custom_call" | custom-call | tf_op jit(solution)/shard_map/full/pallas_call | solution.py:35
  17.7 0.0 collective-permute-done.2.refs_1_
  17.7 0.0 collective-permute-done.3.refs_2_
  17.7 0.0 collective-permute-done.4.refs_3_
  17.7 0.1 copy-done.2
  17.8 0.2 step.1
  18.0 0.1 collective-permute-start.5
  18.1 2.7 %collective-permute-start.6 = (f32[16,8,256]{2,1,0:T(8,128)S(1)}, f32[16,8,256]{2,1,0:T(8,128)S(1)}, u32[]{:S(2)}, u32[]{:S(2)}) collective-permute-start(f32[16,8,256]{2,1,0:T(8,128)S(1)} %get-tuple-element.46), channel_id=1, source_target_pairs={{1,2},{2,1},{5,6},{6,5},{9,10},{10,9},{13,14},{14,13},{17,18},{18,... | collective-permute-start | bytes 393224 | tf_op jit(solution)/shard_map/ppermute | solution.py:354
  20.9 1.8 %inner.1 = (f32[32,16,256]{2,1,0:T(8,128)S(1)}, f32[32,16,256]{2,1,0:T(8,128)S(1)}) custom-call(s32[1,3]{1,0:T(1,128)S(1)} %copy-done.3, f32[1,2]{1,0:T(1,128)S(1)} %copy-done.4, f32[32,16,256]{2,1,0:T(8,128)S(1)} %get-tuple-element.40.p1, f32[32,16,256]{2,1,0:T(8,128)S(1)} %get-tuple-element.38.q1, f32[32,16,256]{2,1,0:T(8,128)S(1)} %get-tuple-element.39.courant, ...), custom_call_target="tpu_custom_call" | custom-call | tf_op jit(solution)/shard_map/inner/pallas_call | solution.py:35
  22.7 0.0 collective-permute-done.5.pair
  22.7 1.7 %collective-permute-done.6.other = f32[16,8,256]{2,1,0:T(8,128)S(1)} collective-permute-done((f32[16,8,256]{2,1,0:T(8,128)S(1)}, f32[16,8,256]{2,1,0:T(8,128)S(1)}, u32[]{:S(2)}, u32[]{:S(2)}) %collective-permute-start.6) | collective-permute-done | bytes 131104 | tf_op jit(solution)/shard_map/ppermute | solution.py:354
  24.4 0.5 %image.1 = (f32[8,16,256]{2,1,0:T(8,128)S(1)}, f32[8,16,256]{2,1,0:T(8,128)S(1)}, f32[8,16,256]{2,1,0:T(8,128)S(1)}, f32[8,16,256]{2,1,0:T(8,128)S(1)}, f32[32,16,256]{2,1,0:T(8,128)S(1)}) custom-call(s32[1]{0:T(128)S(6)} %copy.12.anchors, f32[32,16,256]{2,1,0:T(8,128)S(1)} %get-tuple-element.38.q1, f32[32,16,256]{2,1,0:T(8,128)S(1)} %get-tuple-element.39.courant, ...), custom_call_target="tpu_custom_call" | custom-call | tf_op jit(solution)/shard_map/image/pallas_call | solution.py:35
  24.9 1.1 %collective-permute-start.7 = (f32[8,16,256]{2,1,0:T(8,128)S(1)}, f32[8,16,256]{2,1,0:T(8,128)S(1)}, u32[]{:S(2)}, u32[]{:S(2)}) collective-permute-start(f32[8,16,256]{2,1,0:T(8,128)S(1)} %get-tuple-element.48), channel_id=1, source_target_pairs={{0,4},{4,0},{8,12},{12,8},{1,5},{5,1},{9,13},{13,9},{2,6},{6,2},{1... | collective-permute-start | bytes 393224 | tf_op jit(solution)/shard_map/ppermute | solution.py:424
  26.1 2.5 %collective-permute-start.8 = (f32[8,16,256]{2,1,0:T(8,128)S(1)}, f32[8,16,256]{2,1,0:T(8,128)S(1)}, u32[]{:S(2)}, u32[]{:S(2)}) collective-permute-start(f32[8,16,256]{2,1,0:T(8,128)S(1)} %get-tuple-element.49), channel_id=1, source_target_pairs={{0,8},{4,12},{8,0},{12,4},{1,9},{5,13},{9,1},{13,5},{2,10},{6,14},... | collective-permute-start | bytes 393224 | tf_op jit(solution)/shard_map/ppermute | solution.py:424
  28.6 0.0 collective-permute-start.9
  28.7 0.1 collective-permute-start.10
  28.7 3.5 %collective-permute-start.11 = (f32[16,8,256]{2,1,0:T(8,128)S(1)}, f32[16,8,256]{2,1,0:T(8,128)S(1)}, u32[]{:S(2)}, u32[]{:S(2)}) collective-permute-start(f32[16,8,256]{2,1,0:T(8,128)S(1)} %get-tuple-element.56), channel_id=1, source_target_pairs={{1,2},{2,1},{5,6},{6,5},{9,10},{10,9},{13,14},{14,13},{17,18},{18,... | collective-permute-start | bytes 393224 | tf_op jit(solution)/shard_map/ppermute | solution.py:354
  32.3 2.9 %last.1 = (f32[1,2,32,16,256]{4,3,2,1,0:T(8,128)}, f32[32,16,256]{2,1,0:T(8,128)S(1)}) custom-call(s32[1,3]{1,0:T(1,128)S(1)} %copy-done.3, f32[1,2]{1,0:T(1,128)S(1)} %copy-done.4, f32[32,16,256]{2,1,0:T(8,128)S(1)} %slice_bitcast_fusion.forward, f32[32,16,256]{2,1,0:T(8,128)S(1)} %get-tuple-element.40.p1, f32[32,16,256]{2,1,0:T(8,128)S(1)} %get-tuple-element.38.q1, ...), custom_call_target="tpu_custom_call" | custom-call | flops 1000000000 | bytes 100000000 | tf_op jit(solution)/shard_map/last/pallas_call | solution.py:35
  35.2 0.0 collective-permute-done.10.pair
  35.2 0.0 collective-permute-done.11.other
  35.2 1.4 %last_q.1 = f32[1,2,32,16,256]{4,3,2,1,0:T(8,128)} custom-call(f32[32,16,256]{2,1,0:T(8,128)S(1)} %get-tuple-element.38.q1, f32[32,16,256]{2,1,0:T(8,128)S(1)} %get-tuple-element.39.courant, f32[32,16,256]{2,1,0:T(8,128)S(1)} %get-tuple-element.54.part_q, f32[16,8,256]{2,1,0:T(8,128)S(1)} %collective-permute-done.10.pair, ...), custom_call_target="tpu_custom_call" | custom-call | tf_op jit(solution)/shard_map/last_q/pallas_call | solution.py:35
  36.6 0.0 collective-permute-done.7.refs_1_
  36.6 0.0 collective-permute-done.8.refs_2_
  36.6 0.0 collective-permute-done.9.refs_3_
  36.6 0.7 %gradient.1 = f32[8,16,256]{2,1,0:T(8,128)} custom-call(f32[8,16,256]{2,1,0:T(8,128)S(1)} %copy-done.2, f32[8,16,256]{2,1,0:T(8,128)S(1)} %get-tuple-element.47.refs_0_, f32[8,16,256]{2,1,0:T(8,128)S(1)} %collective-permute-done.7.refs_1_, f32[8,16,256]{2,1,0:T(8,128)S(1)} %collective-permute-done.8.refs_2_, f32[8,16,256]{2,1,0:T(8,128)S(1)} %collective-permute-done.9.refs_3_), custom_call_target="tpu_custom_call" | custom-call | tf_op jit(solution)/shard_map/gradient/pallas_call | solution.py:35
  (4 shorter events, 0.1 us)
Async XLA Ops:
  0.6 11.2 %copy-start = (f32[1,2,32,16,256]{4,3,2,1,0:T(8,128)S(1)}, f32[1,2,32,16,256]{4,3,2,1,0:T(8,128)}, u32[]{:S(2)}) copy-start(f32[1,2,32,16,256]{4,3,2,1,0:T(8,128)} %q_ref.1) | copy-start | bytes 3145732
  0.6 17.0 %collective-permute-start.2 = (f32[8,16,256]{2,1,0:T(8,128)}, f32[8,16,256]{2,1,0:T(8,128)S(1)}, u32[]{:S(2)}, u32[]{:S(2)}) collective-permute-start(f32[8,16,256]{2,1,0:T(8,128)} %velocity.1), channel_id=1, source_target_pairs={{0,4},{4,0},{8,12},{12,8},{1,5},{5,1},{9,13},{13,9},{2,6},{6,2},{1... | collective-permute-start | bytes 393224 | tf_op jit(solution)/shard_map/ppermute | solution.py:367
  2.8 14.8 %collective-permute-start.3 = (f32[8,16,256]{2,1,0:T(8,128)}, f32[8,16,256]{2,1,0:T(8,128)S(1)}, u32[]{:S(2)}, u32[]{:S(2)}) collective-permute-start(f32[8,16,256]{2,1,0:T(8,128)} %velocity.1), channel_id=1, source_target_pairs={{0,8},{4,12},{8,0},{12,4},{1,9},{5,13},{9,1},{13,5},{2,10},{6,14},... | collective-permute-start | bytes 393224 | tf_op jit(solution)/shard_map/ppermute | solution.py:367
  5.1 12.5 %collective-permute-start.4 = (f32[8,16,256]{2,1,0:T(8,128)}, f32[8,16,256]{2,1,0:T(8,128)S(1)}, u32[]{:S(2)}, u32[]{:S(2)}) collective-permute-start(f32[8,16,256]{2,1,0:T(8,128)} %velocity.1), channel_id=1, source_target_pairs={{0,12},{4,8},{8,4},{12,0},{1,13},{5,9},{9,5},{13,1},{2,14},{6,10},... | collective-permute-start | bytes 393224 | tf_op jit(solution)/shard_map/ppermute | solution.py:367
  7.2 5.4 %copy-start.1 = (f32[1,2,32,16,256]{4,3,2,1,0:T(8,128)S(1)}, f32[1,2,32,16,256]{4,3,2,1,0:T(8,128)}, u32[]{:S(2)}) copy-start(f32[1,2,32,16,256]{4,3,2,1,0:T(8,128)} %p_ref.1) | copy-start | bytes 3145732
  7.2 9.7 %collective-permute-start = (f32[32,8,256]{2,1,0:T(8,128)}, f32[32,8,256]{2,1,0:T(8,128)S(1)}, u32[]{:S(2)}, u32[]{:S(2)}) collective-permute-start(f32[32,8,256]{2,1,0:T(8,128)} %get-tuple-element.34), channel_id=1, source_target_pairs={{0,1},{2,3},{1,0},{3,2},{4,5},{6,7},{5,4},{7,6},{8,9},{10,11},{9,8... | collective-permute-start | bytes 786440 | tf_op jit(solution)/shard_map/ppermute | solution.py:354
  8.4 8.5 %collective-permute-start.1 = (f32[32,8,256]{2,1,0:T(8,128)}, f32[32,8,256]{2,1,0:T(8,128)S(1)}, u32[]{:S(2)}, u32[]{:S(2)}) collective-permute-start(f32[32,8,256]{2,1,0:T(8,128)} %get-tuple-element.35), channel_id=1, source_target_pairs={{1,2},{2,1},{5,6},{6,5},{9,10},{10,9},{13,14},{14,13},{17,18},{18,... | collective-permute-start | bytes 786440 | tf_op jit(solution)/shard_map/ppermute | solution.py:354
  11.8 0.7 %copy-start.6 = (s32[1,3,256]{2,0,1:T(1,128)S(1)}, s32[1,3,256]{2,0,1:T(1,128)}, u32[]{:S(2)}) copy-start(s32[1,3,256]{2,0,1:T(1,128)} %param.11) | copy-start | bytes 9220
  12.5 0.7 %copy-start.3 = (s32[1,3]{1,0:T(1,128)S(1)}, s32[1,3]{1,0:T(1,128)}, u32[]{:S(2)}) copy-start(s32[1,3]{1,0:T(1,128)} %source.5) | copy-start | bytes 40
  12.5 0.7 %copy-start.4 = (f32[1,2]{1,0:T(1,128)S(1)}, f32[1,2]{1,0:T(1,128)}, u32[]{:S(2)}) copy-start(f32[1,2]{1,0:T(1,128)} %wavelet.5) | copy-start | bytes 28
  12.5 0.7 %copy-start.5 = (f32[1,2,256]{2,1,0:T(2,128)S(1)}, f32[1,2,256]{2,1,0:T(2,128)}, u32[]{:S(2)}) copy-start(f32[1,2,256]{2,1,0:T(2,128)} %residuals.1) | copy-start | bytes 6148
  16.9 0.9 %copy-start.2 = (f32[8,16,256]{2,1,0:T(8,128)S(1)}, f32[8,16,256]{2,1,0:T(8,128)}, u32[]{:S(2)}) copy-start(f32[8,16,256]{2,1,0:T(8,128)} %velocity.1) | copy-start | bytes 393220
  18.0 4.7 %collective-permute-start.5 = (f32[16,8,256]{2,1,0:T(8,128)S(1)}, f32[16,8,256]{2,1,0:T(8,128)S(1)}, u32[]{:S(2)}, u32[]{:S(2)}) collective-permute-start(f32[16,8,256]{2,1,0:T(8,128)S(1)} %get-tuple-element.45), channel_id=1, source_target_pairs={{0,1},{2,3},{1,0},{3,2},{4,5},{6,7},{5,4},{7,6},{8,9},{10,11},{9,8... | collective-permute-start | bytes 393224 | tf_op jit(solution)/shard_map/ppermute | solution.py:354
  18.1 6.3 %collective-permute-start.6 = (f32[16,8,256]{2,1,0:T(8,128)S(1)}, f32[16,8,256]{2,1,0:T(8,128)S(1)}, u32[]{:S(2)}, u32[]{:S(2)}) collective-permute-start(f32[16,8,256]{2,1,0:T(8,128)S(1)} %get-tuple-element.46), channel_id=1, source_target_pairs={{1,2},{2,1},{5,6},{6,5},{9,10},{10,9},{13,14},{14,13},{17,18},{18,... | collective-permute-start | bytes 393224 | tf_op jit(solution)/shard_map/ppermute | solution.py:354
  24.9 11.6 %collective-permute-start.7 = (f32[8,16,256]{2,1,0:T(8,128)S(1)}, f32[8,16,256]{2,1,0:T(8,128)S(1)}, u32[]{:S(2)}, u32[]{:S(2)}) collective-permute-start(f32[8,16,256]{2,1,0:T(8,128)S(1)} %get-tuple-element.48), channel_id=1, source_target_pairs={{0,4},{4,0},{8,12},{12,8},{1,5},{5,1},{9,13},{13,9},{2,6},{6,2},{1... | collective-permute-start | bytes 393224 | tf_op jit(solution)/shard_map/ppermute | solution.py:424
  26.1 10.5 %collective-permute-start.8 = (f32[8,16,256]{2,1,0:T(8,128)S(1)}, f32[8,16,256]{2,1,0:T(8,128)S(1)}, u32[]{:S(2)}, u32[]{:S(2)}) collective-permute-start(f32[8,16,256]{2,1,0:T(8,128)S(1)} %get-tuple-element.49), channel_id=1, source_target_pairs={{0,8},{4,12},{8,0},{12,4},{1,9},{5,13},{9,1},{13,5},{2,10},{6,14},... | collective-permute-start | bytes 393224 | tf_op jit(solution)/shard_map/ppermute | solution.py:424
  28.6 8.0 %collective-permute-start.9 = (f32[8,16,256]{2,1,0:T(8,128)S(1)}, f32[8,16,256]{2,1,0:T(8,128)S(1)}, u32[]{:S(2)}, u32[]{:S(2)}) collective-permute-start(f32[8,16,256]{2,1,0:T(8,128)S(1)} %get-tuple-element.50), channel_id=1, source_target_pairs={{0,12},{4,8},{8,4},{12,0},{1,13},{5,9},{9,5},{13,1},{2,14},{6,10},... | collective-permute-start | bytes 393224 | tf_op jit(solution)/shard_map/ppermute | solution.py:424
  28.7 6.5 %collective-permute-start.10 = (f32[16,8,256]{2,1,0:T(8,128)S(1)}, f32[16,8,256]{2,1,0:T(8,128)S(1)}, u32[]{:S(2)}, u32[]{:S(2)}) collective-permute-start(f32[16,8,256]{2,1,0:T(8,128)S(1)} %get-tuple-element.55), channel_id=1, source_target_pairs={{0,1},{2,3},{1,0},{3,2},{4,5},{6,7},{5,4},{7,6},{8,9},{10,11},{9,8... | collective-permute-start | bytes 393224 | tf_op jit(solution)/shard_map/ppermute | solution.py:354
  28.7 6.5 %collective-permute-start.11 = (f32[16,8,256]{2,1,0:T(8,128)S(1)}, f32[16,8,256]{2,1,0:T(8,128)S(1)}, u32[]{:S(2)}, u32[]{:S(2)}) collective-permute-start(f32[16,8,256]{2,1,0:T(8,128)S(1)} %get-tuple-element.56), channel_id=1, source_target_pairs={{1,2},{2,1},{5,6},{6,5},{9,10},{10,9},{13,14},{14,13},{17,18},{18,... | collective-permute-start | bytes 393224 | tf_op jit(solution)/shard_map/ppermute | solution.py:354

commit v3 on v1

v3 whole, which is shorter than its diff:
```python
import functools

import jax
import jax.numpy as jnp
from jax import lax
from jax.experimental import pallas as pl
from jax.experimental.pallas import tpu as pltpu
from jax.sharding import PartitionSpec as P

APT = 4
RIM = 4
SPACING_RATIO = 0.1
SCALE = 5040
CENTRE = (-43008.0, -42.0)
COEFS = (0.0, 8064.0, -1008.0, 128.0, -9.0)

F32 = jnp.float32
BF16 = jnp.bfloat16
IN_VMEM = pl.BlockSpec(memory_space=pltpu.VMEM)
IN_SMEM = pl.BlockSpec(memory_space=pltpu.SMEM)
IN_PLACE = pl.BlockSpec(memory_space=pltpu.HBM)
LONG = pl.CostEstimate(flops=10**10, bytes_accessed=10**8, transcendentals=0)
LAST = LONG


def kept(shape):
    return pltpu.VMEM(shape, F32)


def given(shape):
    return jax.ShapeDtypeStruct(shape, F32)


def on_chip(value):
    return pltpu.with_memory_space_constraint(value, pltpu.VMEM)


def on_smem(value):
    return pltpu.with_memory_space_constraint(value, pltpu.SMEM)


def in_hbm(value):
    return pltpu.with_memory_space_constraint(value, pltpu.HBM)


def call(kernel, outs, ins, out_specs=None, scratch=(), name=None, cost=None, aliases=None):
    return pl.pallas_call(
        kernel,
        out_shape=tuple(outs),
        in_specs=[spec for spec, _ in ins],
        out_specs=tuple(out_specs or [IN_VMEM] * len(outs)),
        scratch_shapes=list(scratch),
        compiler_params=pltpu.CompilerParams(vmem_limit_bytes=40 * 1024 * 1024),
        cost_estimate=cost,
        input_output_aliases=aliases or {},
        name=name,
    )(*[array for _, array in ins])


def partners(count):
    reach = APT - 1
    if count <= 2 * reach and count & (count - 1) == 0:
        plans = []
        middle = count // 2
        for bit in [*range(middle, count), *range(1, middle)]:
            pairs = [(i, i ^ bit) for i in range(count)]
            plans.append((pairs, pairs, functools.partial(lambda bit, i: i ^ bit, bit)))
        return plans
    if count <= 2 * reach:
        offsets = range(1, count)
    else:
        offsets = [o for o in range(-reach, reach + 1) if o != 0]
    plans = []
    for o in offsets:
        fetch = [((i + o) % count, i) for i in range(count)]
        send = [(i, (i + o) % count) for i in range(count)]
        plans.append((fetch, send, functools.partial(lambda o, i: lax.rem(i + o + count, count), o)))
    return plans


def coefs_at(apart):
    total = jnp.zeros(apart.shape, F32)
    for o in range(1, RIM + 1):
        total = jnp.where(apart == o, F32(COEFS[o]), total)
    return total


def put_operators(along_y, along_xz, across, depth):
    width, size = along_y.shape[1], along_xz.shape[0]

    def grid(columns):
        row = lax.broadcasted_iota(jnp.int32, (size, columns), 0)
        column = lax.broadcasted_iota(jnp.int32, (size, columns), 1)
        return lax.div(row, depth), lax.rem(row, depth), lax.div(column, depth), lax.rem(column, depth)

    row = lax.broadcasted_iota(jnp.int32, (width, width), 0)
    column = lax.broadcasted_iota(jnp.int32, (width, width), 1)
    value = jnp.where(row == column, F32(CENTRE[1]), coefs_at(jnp.abs(row - column))).astype(BF16)
    along_y[0:width] = value
    along_y[width:] = value

    x, z, other_x, other_z = grid(size)
    same_x, same_z = x == other_x, z == other_z
    value = jnp.where(same_z, coefs_at(jnp.abs(x - other_x)), 0.0)
    value = value + jnp.where(same_x, coefs_at(jnp.abs(z - other_z)), 0.0)
    value = jnp.where(same_x & same_z, F32(CENTRE[0]), value).astype(BF16)
    along_xz[:, 0:size] = value
    along_xz[:, size:] = value

    rim = RIM * depth
    x, z, other_x, other_z = grid(rim)
    for index, first in enumerate((size // depth, -RIM)):
        value = jnp.where(z == other_z, coefs_at(jnp.abs(other_x + first - x)), 0.0).astype(BF16)
        across[index, :, 0:rim] = value
        across[index, :, rim:] = value


def put_laplacian(out, field, along_y, along_xz, across):
    rows, depth, width = field.shape
    flat = field.reshape(rows * depth, width)
    top = flat.astype(BF16)
    rest = (flat - top.astype(F32)).astype(BF16)
    size, rim = along_xz.shape[0], RIM * depth
    for start in range(0, rows * depth, size):
        here = slice(start, start + size)
        left = [top[here], rest[here], along_xz[...]]
        right = [along_y[...], top[here], rest[here]]
        sides = ((0, start + size), (1, start - rim))
        for index, low in sides:
            if 0 <= low < rows * depth:
                left.append(across[index])
                right += [top[low : low + rim], rest[low : low + rim]]
        total = jnp.dot(
            jnp.concatenate(left, axis=1), jnp.concatenate(right, axis=0), preferred_element_type=F32
        )
        out[start // depth : (start + size) // depth] = total.reshape(size // depth, depth, width)


def first_four(shape):
    return lax.broadcasted_iota(jnp.int32, shape, len(shape) - 2) < RIM


def is_even():
    return lax.rem(lax.axis_index("sub"), 2) == 0


def pack_rims(field):
    rows, depth, _ = field.shape
    half = rows // 2
    first, last = field[:, 0 : 2 * RIM], field[:, depth - 2 * RIM : depth]
    here = first_four(first[:half].shape)
    deeper = jnp.where(here, pltpu.roll(last[:half], RIM, 1), last[half:])
    shallower = jnp.where(here, first[:half], pltpu.roll(first[half:], RIM, 1))
    even = is_even()
    return jnp.where(even, deeper, shallower), jnp.where(even, shallower, deeper)


def side_part(message, below, index):
    axis, size = message.ndim - 2, 2 * RIM
    line = lax.broadcasted_iota(jnp.int32, message.shape, axis)
    turn = RIM * (index if below else 1 - index)
    total = None
    for o in range(1, RIM + 1):
        reached = line >= size - o if below else line < o
        shift = (turn + (size - o if below else o)) % size
        moved = pltpu.roll(message, shift, axis) if shift else message
        term = jnp.where(reached, F32(COEFS[o]), 0.0) * moved
        total = term if total is None else total + term
    return total


def add_side(message, pair, depth, add):
    half = message.shape[0]
    for even in (True, False):
        below = pair == even

        def put(below=below):
            layers = slice(depth - 2 * RIM, depth) if below else slice(0, 2 * RIM)
            for index in range(2):
                add(slice(index * half, (index + 1) * half), layers, side_part(message[...], below, index))

        pl.when(is_even() == even)(put)


def cell_mask(cells, depth, width):
    start = lax.axis_index("sub") * depth
    layer = lax.broadcasted_iota(jnp.int32, (depth, width), 0)
    column = lax.broadcasted_iota(jnp.int32, (depth, width), 1)
    return (layer == cells[1] - start) & (column == cells[2])


def load(sources, fields, sems):
    pieces = sems.shape[1]
    copies = []
    for index, (source, field) in enumerate(zip(sources, fields)):
        step = field.shape[0] // pieces
        for piece in range(pieces):
            span = pl.ds(piece * step, step)
            copies.append(pltpu.make_async_copy(source.at[span], field.at[span], sems.at[index, piece]))
    for copy in copies:
        copy.start()
    return copies


def rims_kernel(
    forward, adjoint, velocity, pair, other, p, q, *refs
):
    onto, (sems, small_sems) = refs[:-2], refs[-2:]
    half = pair.shape[0] // 2
    copies = load((forward.at[0, 1], adjoint.at[0, 1]), (p, q), sems)
    small = [
        pltpu.make_async_copy(source, target, small_sems.at[index])
        for index, (source, target) in enumerate(zip((velocity,), onto))
    ]
    for copy in small:
        copy.start()
    for index, field in enumerate((p, q)):
        for copy in copies[index * len(copies) // 2 : (index + 1) * len(copies) // 2]:
            copy.wait()
        span = slice(index * half, (index + 1) * half)
        pair[span], other[span] = pack_rims(field[...])
    for copy in small:
        copy.wait()


def first_kernel(
    source, wavelet, anchors, receivers_in, residuals_in, forward, adjoint, p, q,
    cells, amounts, free_p, lap_p, free_q, lap_q, free_q2, mixed, along_y, along_xz, across,
    spread, later, receivers, residuals, sems, small_sems,
):
    rows, depth, width = lap_p.shape
    for index in range(3):
        cells[index] = source[0, index]
    cells[3] = jnp.max(anchors[...])
    for step in range(2):
        amounts[step] = wavelet[0, step]
    copies = load((forward.at[0, 0], adjoint.at[0, 0]), (later.at[0], later.at[1]), sems)
    small = [
        pltpu.make_async_copy(given_ref, target, small_sems.at[index])
        for index, (given_ref, target) in enumerate(
            ((receivers_in, receivers), (residuals_in, residuals))
        )
    ]
    for copy in small:
        copy.start()
    put_operators(along_y, along_xz, across, depth)
    put_laplacian(lap_p, p[...], along_y, along_xz, across)
    put_laplacian(lap_q, q[...], along_y, along_xz, across)
    for copy in small:
        copy.wait()
    start = lax.axis_index("sub") * depth

    first, layer, column = receivers[0], receivers[1] - start, receivers[2]
    inside = (layer >= 0) & (layer < depth)
    place = jnp.where(inside, first * depth + layer, -1)
    count = place.shape[1]
    lines = lax.broadcasted_iota(jnp.int32, (rows * depth, count), 0)
    onto = (lines == place).astype(F32).astype(BF16)
    columns = lax.broadcasted_iota(jnp.int32, (width, count), 0)
    for step in range(2):
        value = jnp.where(columns == column, residuals[0, step : step + 1], 0.0)
        total = None
        for _ in range(3):
            part = value.astype(BF16)
            value = value - part.astype(F32)
            term = lax.dot_general(onto, part, (((1,), (1,)), ((), ())), preferred_element_type=F32)
            total = term if total is None else total + term
        spread[step] = total.reshape(rows, depth, width)

    for copy in copies:
        copy.wait()

    def row(x, _):
        own = q[x]
        free_p[x] = 2.0 * p[x] - later[0, x]
        free_q[x] = 2.0 * own - later[1, x] + spread[0, x]
        free_q2[x] = spread[1, x] - own
        mixed[x] = own * lap_p[x]
        return 0

    lax.fori_loop(0, rows, row, 0, unroll=4)


def full_kernel(lap_p, lap_q, mixed, now_q, pair, other, full_p, full_q, full_mixed):
    depth = lap_p.shape[1]
    half = pair.shape[0] // 2
    full_p[...] = lap_p[...]
    full_q[...] = lap_q[...]
    full_mixed[...] = mixed[...]

    def add_p(span, layers, part):
        full_p[span, layers] = full_p[span, layers] + part
        full_mixed[span, layers] = full_mixed[span, layers] + now_q[span, layers] * part

    def add_q(span, layers, part):
        full_q[span, layers] = full_q[span, layers] + part

    for message, is_pair in ((pair, True), (other, False)):
        add_side(message.at[0:half], is_pair, depth, add_p)
        add_side(message.at[half:], is_pair, depth, add_q)


def step_kernel(plans, cells, amounts, free_p, free_q, full_p, full_q, *refs):
    tiles, (courant, p1, q1, pair, other_p, other_q) = refs[: len(plans) + 1], refs[len(plans) + 1 :]
    tile_rows = tiles[0].shape[0]
    for tile, place in zip(tiles, places(plans, cells)):

        def put():
            speed = F32(SPACING_RATIO) * tile[...]
            factor = speed * speed * F32(1.0 / SCALE)
            span = pl.ds(place * tile_rows, tile_rows)
            courant[span] = factor
            p1[span] = free_p[span] + factor * full_p[span]
            q1[span] = free_q[span] + factor * full_q[span]

        pl.when((place >= 0) & (place < APT))(put)
    rows, depth, width = p1.shape
    half = rows // 2
    x0 = cells[0]
    p1[x0] = p1[x0] + jnp.where(cell_mask(cells, depth, width), amounts[0], 0.0)
    pair[0:half], other_p[...] = pack_rims(p1[...])
    pair[half:], other_q[...] = pack_rims(q1[...])


def places(plans, cells):
    count = lax.axis_size("shot")
    me = lax.axis_index("shot")
    peers = [me] + [peer(me) for _, _, peer in plans]
    return [lax.rem(peer - cells[3] + count, count) for peer in peers]


def put_tile(out, image, place):
    tile_rows = out.shape[0]
    inside = (place >= 0) & (place < APT)

    def put():
        out[...] = image[pl.ds(place * tile_rows, tile_rows)]

    def clear():
        out[...] = jnp.zeros(out.shape, F32)

    pl.when(inside)(put)
    pl.when(jnp.logical_not(inside))(clear)


def inner_kernel(p1, along_y, along_xz, across, lap_p):
    put_laplacian(lap_p, p1[...], along_y, along_xz, across)


def image_kernel(
    plans, cells, amounts, q0, q1, courant, mixed, lap_p, pair, other, full_p, *refs
):
    outs, image = refs[:-1], refs[-1]
    rows, depth, width = q1.shape
    full_p[...] = lap_p[...]

    def add(span, layers, part):
        full_p[span, layers] = full_p[span, layers] + part

    add_side(pair.at[0 : rows // 2], True, depth, add)
    add_side(other, False, depth, add)

    def row(x, _):
        image[x] = courant[x] * (mixed[x] + q1[x] * full_p[x])
        return 0

    lax.fori_loop(0, rows, row, 0, unroll=4)
    x0 = cells[0]
    here = cell_mask(cells, depth, width)
    added = q0[x0] * jnp.where(here, amounts[0], 0.0) + q1[x0] * jnp.where(here, amounts[1], 0.0)
    image[x0] = image[x0] + added
    for out, place in zip(outs, places(plans, cells)):
        put_tile(out, image, place)


def last_kernel(
    cells, amounts, p0, p1, q1, courant, lap_p, free_q2, along_y, along_xz, across, pair, other,
    forward_out, adjoint_out, p2, q2, lap_q, sems,
):
    rows, depth, width = p1.shape
    copies = []

    def save(field, out):
        copies.append(pltpu.make_async_copy(field, out, sems.at[len(copies)]))
        copies[-1].start()

    save(p1, forward_out.at[0, 0])
    save(q1, adjoint_out.at[0, 0])

    def row_p(x, _):
        p2[x] = 2.0 * p1[x] - p0[x] + courant[x] * lap_p[x]
        return 0

    lax.fori_loop(0, rows, row_p, 0, unroll=4)
    x0 = cells[0]
    amount = jnp.where(cell_mask(cells, depth, width), amounts[1], 0.0)
    p2[x0] = p2[x0] + amount
    save(p2, forward_out.at[0, 1])
    put_laplacian(lap_q, q1[...], along_y, along_xz, across)

    def add(span, layers, part):
        lap_q[span, layers] = lap_q[span, layers] + part

    add_side(pair.at[rows // 2 :], True, depth, add)
    add_side(other, False, depth, add)

    def row_q(x, _):
        q2[x] = 2.0 * q1[x] + free_q2[x] + courant[x] * lap_q[x]
        return 0

    lax.fori_loop(0, rows, row_q, 0, unroll=4)
    save(q2, adjoint_out.at[0, 1])
    for copy in copies:
        copy.wait()


def gradient_kernel(velocity, *refs):
    parts, out = refs[:-1], refs[-1]
    total = parts[0][...]
    for part in parts[1:]:
        total = total + part[...]
    out[...] = -(2.0 / velocity[...]) * total


def swap(message, start):
    ahead = [(i, i + 1) for i in range(start, lax.axis_size("sub") - 1, 2)]
    return lax.ppermute(message, "sub", ahead + [(i, j) for j, i in ahead])


def on_device(
    velocity, anchors, source_cells, receiver_cells, wavelet, residuals, forward_pair, adjoint_pair
):
    tile_rows, depth, width = velocity.shape
    rows = APT * tile_rows
    receiver_cells = jnp.transpose(receiver_cells, (1, 0, 2))
    field = (rows, depth, width)
    rims = (rows, 2 * RIM, width)
    plans = partners(lax.axis_size("shot"))
    plans_in = [plans[0], *plans[:0:-1]]

    arriving = [lax.ppermute(velocity, "shot", fetch) for fetch, _, _ in plans_in]

    pair, other, p0, q0, tile = call(
        rims_kernel,
        [given(rims)] * 2 + [kept(field)] * 2 + [kept(velocity.shape)],
        [(IN_PLACE, in_hbm(a)) for a in (forward_pair, adjoint_pair, velocity)],
        out_specs=[IN_VMEM] * 5,
        scratch=[pltpu.SemaphoreType.DMA((2, 4)), pltpu.SemaphoreType.DMA((1,))],
        name="rims",
    )
    pair, other = swap(pair, 0), swap(other, 1)

    size = min(rows, 256 // depth) * depth
    operators = [
        pltpu.VMEM((2 * width, width), BF16),
        pltpu.VMEM((size, 2 * size), BF16),
        pltpu.VMEM((2, size, 2 * RIM * depth), BF16),
    ]
    cells, amounts, free_p, lap_p, free_q, lap_q, free_q2, mixed, *operators = call(
        first_kernel,
        [pltpu.SMEM((4,), jnp.int32), pltpu.SMEM((2,), F32)] + [kept(field)] * 6 + operators,
        [
            (IN_SMEM, source_cells), (IN_SMEM, wavelet), (IN_VMEM, anchors),
            (IN_PLACE, in_hbm(receiver_cells)), (IN_PLACE, in_hbm(residuals)),
            (IN_PLACE, in_hbm(forward_pair)), (IN_PLACE, in_hbm(adjoint_pair)),
            (IN_VMEM, on_chip(p0)), (IN_VMEM, on_chip(q0)),
        ],
        out_specs=[IN_SMEM] * 2 + [IN_VMEM] * 9,
        scratch=[
            pltpu.VMEM((2,) + field, F32),
            pltpu.VMEM((2,) + field, F32),
            pltpu.VMEM(receiver_cells.shape, jnp.int32),
            pltpu.VMEM(residuals.shape, F32),
            pltpu.SemaphoreType.DMA((2, 2)),
            pltpu.SemaphoreType.DMA((2,)),
        ],
        name="first",
        cost=LONG,
    )
    scalars = [(IN_SMEM, on_smem(cells)), (IN_SMEM, on_smem(amounts))]

    full_p, full_q, mixed = call(
        full_kernel,
        [kept(field)] * 3,
        [(IN_VMEM, on_chip(a)) for a in (lap_p, lap_q, mixed, q0)] + [(IN_VMEM, pair), (IN_VMEM, other)],
        name="full",
    )
    courant, p1, q1, pair, other_p, other_q = call(
        functools.partial(step_kernel, plans_in),
        [kept(field)] * 3 + [given(rims)] + [given((rows // 2, 2 * RIM, width))] * 2,
        scalars
        + [(IN_VMEM, on_chip(a)) for a in (free_p, free_q, full_p, full_q)]
        + [(IN_VMEM, on_chip(tile))]
        + [(IN_VMEM, other_tile) for other_tile in arriving],
        name="step",
    )
    pair, other_p, other_q = swap(pair, 0), swap(other_p, 1), swap(other_q, 1)

    (lap_p1,) = call(
        inner_kernel,
        [kept(field)],
        [(IN_VMEM, on_chip(a)) for a in (p1, *operators)],
        name="inner",
    )
    lap_p1, *images = call(
        functools.partial(image_kernel, plans),
        [kept(field)] + [given(velocity.shape)] * (len(plans) + 1),
        scalars
        + [(IN_VMEM, on_chip(a)) for a in (q0, q1, courant, mixed, lap_p1)]
        + [(IN_VMEM, pair), (IN_VMEM, other_p)],
        scratch=[pltpu.VMEM(field, F32)],
        name="image",
    )
    gathered = [images[0]] + [
        lax.ppermute(image, "shot", send) for image, (_, send, _) in zip(images[1:], plans)
    ]

    forward_out, adjoint_out = call(
        last_kernel,
        [given(forward_pair.shape), given(adjoint_pair.shape)],
        scalars
        + [(IN_VMEM, on_chip(a)) for a in (p0, p1, q1, courant, lap_p1, free_q2, *operators)]
        + [(IN_VMEM, pair), (IN_VMEM, other_q)],
        out_specs=[IN_PLACE, IN_PLACE],
        scratch=[pltpu.VMEM(field, F32)] * 3 + [pltpu.SemaphoreType.DMA((4,))],
        name="last",
        cost=LAST,
    )

    (gradient,) = call(
        gradient_kernel,
        [given(velocity.shape)],
        [(IN_VMEM, a) for a in (on_chip(tile), *gathered)],
        name="gradient",
    )
    return gradient, forward_out, adjoint_out


def solution(mesh):
    shot = ("grp", "shot")
    fields = P(shot, None, None, "sub", None)
    return jax.shard_map(
        on_device,
        mesh=mesh,
        in_specs=(
            P(shot, "sub", None),
            P(shot),
            P(shot, None),
            P(shot, None, None),
            P(shot, None),
            P(shot, None, None),
            fields,
            fields,
        ),
        out_specs=(P(shot, "sub", None), fields, fields),
        check_vma=False,
    )
```

time: 48.7 us -> 34.5 us (0.71)
  waiting for transfers between devices: 14.6 us -> 5.38 us
  Pallas kernels: 12.1 us -> 8.76 us
  starting transfers between devices: 20.2 us -> 18.1 us
  local copies, waits for them, and re-layouts: 0.07 us -> 0.66 us
    ppermute x4 -> x5, waiting for transfers between devices: 7.63 us -> 0.52 us  [swap(): return lax.ppermute(message, 'sub', ahead + [(i, j) for j, i in ahead])]
    ppermute x3, waiting for transfers between devices: 3.14 us -> 0.01 us  [on_device(): lax.ppermute(velocity, 'shot', fetch)]
    ppermute x4 -> x5, starting transfers between devices: 12.6 us -> 9.95 us  [swap(): return lax.ppermute(message, 'sub', ahead + [(i, j) for j, i in ahead])]
    pallas_call x1 -> x0, Pallas kernels: 2.17 us -> none  [on_device(): pl.pallas_call(rims_kernel, out_shape=(given(rim),) * 2, grid=(1,), in_sp...]
    pallas_call x5 -> x8, Pallas kernels: 9.96 us -> 8.76 us  [call(): pl.pallas_call(kernel, out_shape=tuple(outs), in_specs=[spec for spec, _...]
    ppermute x3, waiting for transfers between devices: 3.86 us -> 4.85 us  [on_device(): lax.ppermute(image, 'shot', send)]
    ppermute x3, starting transfers between devices: 3.67 us -> 4.5 us  [on_device(): lax.ppermute(velocity, 'shot', fetch)]
    unnamed x15 -> x4, local copies, waits for them, and re-layouts: 0.04 us -> 0.66 us
  transfers between devices with their start and end apart: 10 -> 11, of which waited for: 5 -> 4; matrix products, arithmetic and copies ran while one was open for 0% -> 0% of each run, Pallas kernels for 15% -> 23%
where the time goes in v3:
time: 34.5 us; the launch traced here: 34.3 us
  starting transfers between devices  18.1 us (52%)
  Pallas kernels  8.76 us (25%)
  waiting for transfers between devices  5.38 us (16%)
  between operations  1.41 us (4%)
  local copies, waits for them, and re-layouts  0.66 us (2%)
    ppermute x5, starting transfers between devices, swap(): return lax.ppermute(message, 'sub', ahead + [(i, j) for j, i in ahead])  9.95 us
    pallas_call x8, Pallas kernels, call(): pl.pallas_call(kernel, out_shape=tuple(outs), in_specs=[spec for spec, _...  8.76 us
    ppermute x3, waiting for transfers between devices, on_device(): lax.ppermute(image, 'shot', send)  4.85 us
    ppermute x3, starting transfers between devices, on_device(): lax.ppermute(velocity, 'shot', fetch)  4.5 us
    ppermute x3, starting transfers between devices, on_device(): lax.ppermute(image, 'shot', send)  3.66 us
  transfers between devices with their start and end apart: 11, of which 4 were waited for; matrix products, arithmetic and copies ran while one was open for 0% of the time, Pallas kernels for 23%

profile of v3, /device:TPU:1, one launch (start us, length us, event | category | flops | bytes accessed | tf_op | source)
XLA Modules:
  0.0 34.3 jit_solution(14486086019834578165)
XLA Ops:
  0.6 3.2 %collective-permute-start.2 = (f32[8,16,256]{2,1,0:T(8,128)}, f32[8,16,256]{2,1,0:T(8,128)S(1)}, u32[]{:S(2)}, u32[]{:S(2)}) collective-permute-start(f32[8,16,256]{2,1,0:T(8,128)} %velocity.1), channel_id=1, source_target_pairs={{0,8},{4,12},{8,0},{12,4},{1,9},{5,13},{9,1},{13,5},{2,10},{6,14},... | collective-permute-start | bytes 393224 | tf_op jit(solution)/shard_map/ppermute | solution.py:441
  3.8 1.1 %collective-permute-start.4 = (f32[8,16,256]{2,1,0:T(8,128)}, f32[8,16,256]{2,1,0:T(8,128)S(1)}, u32[]{:S(2)}, u32[]{:S(2)}) collective-permute-start(f32[8,16,256]{2,1,0:T(8,128)} %velocity.1), channel_id=1, source_target_pairs={{0,12},{4,8},{8,4},{12,0},{1,13},{5,9},{9,5},{13,1},{2,14},{6,10},... | collective-permute-start | bytes 393224 | tf_op jit(solution)/shard_map/ppermute | solution.py:441
  4.9 0.2 collective-permute-start.3
  5.1 1.4 %rims.1 = (f32[32,8,256]{2,1,0:T(8,128)S(1)}, f32[32,8,256]{2,1,0:T(8,128)S(1)}, f32[32,16,256]{2,1,0:T(8,128)S(1)}, f32[32,16,256]{2,1,0:T(8,128)S(1)}, f32[8,16,256]{2,1,0:T(8,128)S(1)}) custom-call(f32[1,2,32,16,256]{4,3,2,1,0:T(8,128)} %forward.3, f32[1,2,32,16,256]{4,3,2,1,0:T(8,128)} %adjoint.3, f32[8,16,256]{2,1,0:T(8,128)} %velocity.1), custom_call_target="tpu_custom_call" | custom-call | tf_op jit(solution)/shard_map/rims/pallas_call | solution.py:47
  6.5 1.3 %collective-permute-start = (f32[32,8,256]{2,1,0:T(8,128)S(1)}, f32[32,8,256]{2,1,0:T(8,128)S(1)}, u32[]{:S(2)}, u32[]{:S(2)}) collective-permute-start(f32[32,8,256]{2,1,0:T(8,128)S(1)} %get-tuple-element.45), channel_id=1, source_target_pairs={{0,1},{2,3},{1,0},{3,2},{4,5},{6,7},{5,4},{7,6},{8,9},{10,11},{9,8... | collective-permute-start | bytes 786440 | tf_op jit(solution)/shard_map/ppermute | solution.py:427
  7.8 3.0 %collective-permute-start.1 = (f32[32,8,256]{2,1,0:T(8,128)S(1)}, f32[32,8,256]{2,1,0:T(8,128)S(1)}, u32[]{:S(2)}, u32[]{:S(2)}) collective-permute-start(f32[32,8,256]{2,1,0:T(8,128)S(1)} %get-tuple-element.46), channel_id=1, source_target_pairs={{1,2},{2,1},{5,6},{6,5},{9,10},{10,9},{13,14},{14,13},{17,18},{18,... | collective-permute-start | bytes 786440 | tf_op jit(solution)/shard_map/ppermute | solution.py:427
  11.5 0.0 copy-start
  11.5 0.0 copy-start.1
  11.5 0.6 %copy-done = s32[1,3]{1,0:T(1,128)S(1)} copy-done((s32[1,3]{1,0:T(1,128)S(1)}, s32[1,3]{1,0:T(1,128)}, u32[]{:S(2)}) %copy-start) | copy-done | bytes 36
  12.2 0.0 copy-done.1
  12.2 3.0 %first.1 = (s32[4]{0:T(128)S(4)}, f32[2]{0:T(128)S(4)}, f32[32,16,256]{2,1,0:T(8,128)S(1)}, f32[32,16,256]{2,1,0:T(8,128)S(1)}, f32[32,16,256]{2,1,0:T(8,128)S(1...) custom-call(s32[1,3]{1,0:T(1,128)S(1)} %copy-done, ...), custom_call_target="tpu_custom_call" | custom-call | flops 10000000000 | bytes 100000000 | tf_op jit(solution)/shard_map/first/pallas_call | solution.py:47
  15.2 0.0 collective-permute-done.pair
  15.2 0.3 collective-permute-done.1.other
  15.5 0.6 %full.1 = (f32[32,16,256]{2,1,0:T(8,128)S(1)}, f32[32,16,256]{2,1,0:T(8,128)S(1)}, f32[32,16,256]{2,1,0:T(8,128)S(1)}) custom-call(f32[32,16,256]{2,1,0:T(8,128)S(1)} %get-tuple-element.42.lap_p, f32[32,16,256]{2,1,0:T(8,128)S(1)} %get-tuple-element.43.lap_q, f32[32,16,256]{2,1,0:T(8,128)S(1)} %get-tuple-element.44.mixed, ...), custom_call_target="tpu_custom_call" | custom-call | tf_op jit(solution)/shard_map/full/pallas_call | solution.py:47
  16.1 0.0 collective-permute-done.2.refs_1_
  16.1 0.0 collective-permute-done.4.refs_3_
  16.1 0.0 collective-permute-done.3.refs_2_
  16.1 0.3 step.1
  16.4 0.1 collective-permute-start.5
  16.5 3.0 %collective-permute-start.6 = (f32[16,8,256]{2,1,0:T(8,128)S(1)}, f32[16,8,256]{2,1,0:T(8,128)S(1)}, u32[]{:S(2)}, u32[]{:S(2)}) collective-permute-start(f32[16,8,256]{2,1,0:T(8,128)S(1)} %get-tuple-element.57), channel_id=1, source_target_pairs={{1,2},{2,1},{5,6},{6,5},{9,10},{10,9},{13,14},{14,13},{17,18},{18,... | collective-permute-start | bytes 393224 | tf_op jit(solution)/shard_map/ppermute | solution.py:427
  19.6 2.5 %collective-permute-start.10 = (f32[16,8,256]{2,1,0:T(8,128)S(1)}, f32[16,8,256]{2,1,0:T(8,128)S(1)}, u32[]{:S(2)}, u32[]{:S(2)}) collective-permute-start(f32[16,8,256]{2,1,0:T(8,128)S(1)} %get-tuple-element.64), channel_id=1, source_target_pairs={{1,2},{2,1},{5,6},{6,5},{9,10},{10,9},{13,14},{14,13},{17,18},{18,... | collective-permute-start | bytes 393224 | tf_op jit(solution)/shard_map/ppermute | solution.py:427
  22.1 0.5 %inner.1.lap_p = f32[32,16,256]{2,1,0:T(8,128)S(1)} custom-call(f32[32,16,256]{2,1,0:T(8,128)S(1)} %get-tuple-element.52.p1, bf16[512,256]{1,0:T(8,128)(2,1)S(1)} %get-tuple-element.53.along_y, bf16[256,512]{1,0:T(8,128)(2,1)S(1)} %get-tuple-element.54.along_xz, bf16[2,256,128]{2,1,0:T(8,128)(2,1)S(1)} %get-tuple-element.55.across), custom_call_target="tpu_custom_call" | custom-call | tf_op jit(solution)/shard_map/inner/pallas_call | solution.py:47
  22.6 0.2 collective-permute-done.6.other
  22.8 0.0 collective-permute-done.5.pair
  22.8 0.5 %image.1 = (f32[32,16,256]{2,1,0:T(8,128)S(1)}, f32[8,16,256]{2,1,0:T(8,128)S(1)}, f32[8,16,256]{2,1,0:T(8,128)S(1)}, f32[8,16,256]{2,1,0:T(8,128)S(1)}, f32[8,16,256]{2,1,0:T(8,128)S(1)}) custom-call(s32[4]{0:T(128)S(4)} %get-tuple-element.38.cells, f32[2]{0:T(128)S(4)} %get-tuple-element.39.amounts, f32[32,16,256]{2,1,0:T(8,128)S(1)} %get-tuple-element.37.q.now_q.q0, ...), custom_call_target="tpu_custom_call" | custom-call | tf_op jit(solution)/shard_map/image/pallas_call | solution.py:47
  23.3 3.2 %collective-permute-start.7 = (f32[8,16,256]{2,1,0:T(8,128)S(1)}, f32[8,16,256]{2,1,0:T(8,128)S(1)}, u32[]{:S(2)}, u32[]{:S(2)}) collective-permute-start(f32[8,16,256]{2,1,0:T(8,128)S(1)} %get-tuple-element.59), channel_id=1, source_target_pairs={{0,8},{4,12},{8,0},{12,4},{1,9},{5,13},{9,1},{13,5},{2,10},{6,14},... | collective-permute-start | bytes 393224 | tf_op jit(solution)/shard_map/ppermute | solution.py:515
  26.5 0.4 %collective-permute-start.8 = (f32[8,16,256]{2,1,0:T(8,128)S(1)}, f32[8,16,256]{2,1,0:T(8,128)S(1)}, u32[]{:S(2)}, u32[]{:S(2)}) collective-permute-start(f32[8,16,256]{2,1,0:T(8,128)S(1)} %get-tuple-element.60), channel_id=1, source_target_pairs={{0,12},{4,8},{8,4},{12,0},{1,13},{5,9},{9,5},{13,1},{2,14},{6,10},... | collective-permute-start | bytes 393224 | tf_op jit(solution)/shard_map/ppermute | solution.py:515
  26.9 0.0 collective-permute-start.9
  26.9 0.0 collective-permute-done.10.other
  26.9 1.8 %last.1 = (f32[1,2,32,16,256]{4,3,2,1,0:T(8,128)}, f32[1,2,32,16,256]{4,3,2,1,0:T(8,128)}) custom-call(s32[4]{0:T(128)S(4)} %get-tuple-element.38.cells, f32[2]{0:T(128)S(4)} %get-tuple-element.39.amounts, f32[32,16,256]{2,1,0:T(8,128)S(1)} %get-tuple-element.36.p.p0, f32[32,16,256]{2,1,0:T(8,128)S(1)} %get-tuple-element.52.p1, ...), custom_call_target="tpu_custom_call" | custom-call | flops 10000000000 | bytes 100000000 | tf_op jit(solution)/shard_map/last/pallas_call | solution.py:47
  28.8 4.5 %collective-permute-done.7.refs_1_ = f32[8,16,256]{2,1,0:T(8,128)S(1)} collective-permute-done((f32[8,16,256]{2,1,0:T(8,128)S(1)}, f32[8,16,256]{2,1,0:T(8,128)S(1)}, u32[]{:S(2)}, u32[]{:S(2)}) %collective-permute-start.7) | collective-permute-done | bytes 131104 | tf_op jit(solution)/shard_map/ppermute | solution.py:515
  33.3 0.0 collective-permute-done.8.refs_2_
  33.3 0.4 %collective-permute-done.9.refs_3_ = f32[8,16,256]{2,1,0:T(8,128)S(1)} collective-permute-done((f32[8,16,256]{2,1,0:T(8,128)S(1)}, f32[8,16,256]{2,1,0:T(8,128)S(1)}, u32[]{:S(2)}, u32[]{:S(2)}) %collective-permute-start.9) | collective-permute-done | bytes 131104 | tf_op jit(solution)/shard_map/ppermute | solution.py:515
  33.6 0.7 %gradient.1 = f32[8,16,256]{2,1,0:T(8,128)} custom-call(f32[8,16,256]{2,1,0:T(8,128)S(1)} %get-tuple-element.35.refs_0_.velocity, f32[8,16,256]{2,1,0:T(8,128)S(1)} %get-tuple-element.58.refs_0_, f32[8,16,256]{2,1,0:T(8,128)S(1)} %collective-permute-done.7.refs_1_, f32[8,16,256]{2,1,0:T(8,128)S(1)} %collective-permute-done.8.refs_2_, ...), custom_call_target="tpu_custom_call" | custom-call | tf_op jit(solution)/shard_map/gradient/pallas_call | solution.py:47
Async XLA Ops:
  0.6 15.5 %collective-permute-start.2 = (f32[8,16,256]{2,1,0:T(8,128)}, f32[8,16,256]{2,1,0:T(8,128)S(1)}, u32[]{:S(2)}, u32[]{:S(2)}) collective-permute-start(f32[8,16,256]{2,1,0:T(8,128)} %velocity.1), channel_id=1, source_target_pairs={{0,8},{4,12},{8,0},{12,4},{1,9},{5,13},{9,1},{13,5},{2,10},{6,14},... | collective-permute-start | bytes 393224 | tf_op jit(solution)/shard_map/ppermute | solution.py:441
  3.8 12.3 %collective-permute-start.4 = (f32[8,16,256]{2,1,0:T(8,128)}, f32[8,16,256]{2,1,0:T(8,128)S(1)}, u32[]{:S(2)}, u32[]{:S(2)}) collective-permute-start(f32[8,16,256]{2,1,0:T(8,128)} %velocity.1), channel_id=1, source_target_pairs={{0,12},{4,8},{8,4},{12,0},{1,13},{5,9},{9,5},{13,1},{2,14},{6,10},... | collective-permute-start | bytes 393224 | tf_op jit(solution)/shard_map/ppermute | solution.py:441
  4.9 11.2 %collective-permute-start.3 = (f32[8,16,256]{2,1,0:T(8,128)}, f32[8,16,256]{2,1,0:T(8,128)S(1)}, u32[]{:S(2)}, u32[]{:S(2)}) collective-permute-start(f32[8,16,256]{2,1,0:T(8,128)} %velocity.1), channel_id=1, source_target_pairs={{0,4},{4,0},{8,12},{12,8},{1,5},{5,1},{9,13},{13,9},{2,6},{6,2},{1... | collective-permute-start | bytes 393224 | tf_op jit(solution)/shard_map/ppermute | solution.py:441
  6.5 8.7 %collective-permute-start = (f32[32,8,256]{2,1,0:T(8,128)S(1)}, f32[32,8,256]{2,1,0:T(8,128)S(1)}, u32[]{:S(2)}, u32[]{:S(2)}) collective-permute-start(f32[32,8,256]{2,1,0:T(8,128)S(1)} %get-tuple-element.45), channel_id=1, source_target_pairs={{0,1},{2,3},{1,0},{3,2},{4,5},{6,7},{5,4},{7,6},{8,9},{10,11},{9,8... | collective-permute-start | bytes 786440 | tf_op jit(solution)/shard_map/ppermute | solution.py:427
  7.8 7.7 %collective-permute-start.1 = (f32[32,8,256]{2,1,0:T(8,128)S(1)}, f32[32,8,256]{2,1,0:T(8,128)S(1)}, u32[]{:S(2)}, u32[]{:S(2)}) collective-permute-start(f32[32,8,256]{2,1,0:T(8,128)S(1)} %get-tuple-element.46), channel_id=1, source_target_pairs={{1,2},{2,1},{5,6},{6,5},{9,10},{10,9},{13,14},{14,13},{17,18},{18,... | collective-permute-start | bytes 786440 | tf_op jit(solution)/shard_map/ppermute | solution.py:427
  11.5 0.7 %copy-start = (s32[1,3]{1,0:T(1,128)S(1)}, s32[1,3]{1,0:T(1,128)}, u32[]{:S(2)}) copy-start(s32[1,3]{1,0:T(1,128)} %source.1) | copy-start | bytes 40
  11.5 0.7 %copy-start.1 = (f32[1,2]{1,0:T(1,128)S(1)}, f32[1,2]{1,0:T(1,128)}, u32[]{:S(2)}) copy-start(f32[1,2]{1,0:T(1,128)} %wavelet.1) | copy-start | bytes 28
  16.4 6.4 %collective-permute-start.5 = (f32[32,8,256]{2,1,0:T(8,128)S(1)}, f32[32,8,256]{2,1,0:T(8,128)S(1)}, u32[]{:S(2)}, u32[]{:S(2)}) collective-permute-start(f32[32,8,256]{2,1,0:T(8,128)S(1)} %get-tuple-element.56), channel_id=1, source_target_pairs={{0,1},{2,3},{1,0},{3,2},{4,5},{6,7},{5,4},{7,6},{8,9},{10,11},{9,8... | collective-permute-start | bytes 786440 | tf_op jit(solution)/shard_map/ppermute | solution.py:427
  16.5 6.3 %collective-permute-start.6 = (f32[16,8,256]{2,1,0:T(8,128)S(1)}, f32[16,8,256]{2,1,0:T(8,128)S(1)}, u32[]{:S(2)}, u32[]{:S(2)}) collective-permute-start(f32[16,8,256]{2,1,0:T(8,128)S(1)} %get-tuple-element.57), channel_id=1, source_target_pairs={{1,2},{2,1},{5,6},{6,5},{9,10},{10,9},{13,14},{14,13},{17,18},{18,... | collective-permute-start | bytes 393224 | tf_op jit(solution)/shard_map/ppermute | solution.py:427
  19.6 7.4 %collective-permute-start.10 = (f32[16,8,256]{2,1,0:T(8,128)S(1)}, f32[16,8,256]{2,1,0:T(8,128)S(1)}, u32[]{:S(2)}, u32[]{:S(2)}) collective-permute-start(f32[16,8,256]{2,1,0:T(8,128)S(1)} %get-tuple-element.64), channel_id=1, source_target_pairs={{1,2},{2,1},{5,6},{6,5},{9,10},{10,9},{13,14},{14,13},{17,18},{18,... | collective-permute-start | bytes 393224 | tf_op jit(solution)/shard_map/ppermute | solution.py:427
  23.3 10.0 %collective-permute-start.7 = (f32[8,16,256]{2,1,0:T(8,128)S(1)}, f32[8,16,256]{2,1,0:T(8,128)S(1)}, u32[]{:S(2)}, u32[]{:S(2)}) collective-permute-start(f32[8,16,256]{2,1,0:T(8,128)S(1)} %get-tuple-element.59), channel_id=1, source_target_pairs={{0,8},{4,12},{8,0},{12,4},{1,9},{5,13},{9,1},{13,5},{2,10},{6,14},... | collective-permute-start | bytes 393224 | tf_op jit(solution)/shard_map/ppermute | solution.py:515
  26.5 6.8 %collective-permute-start.8 = (f32[8,16,256]{2,1,0:T(8,128)S(1)}, f32[8,16,256]{2,1,0:T(8,128)S(1)}, u32[]{:S(2)}, u32[]{:S(2)}) collective-permute-start(f32[8,16,256]{2,1,0:T(8,128)S(1)} %get-tuple-element.60), channel_id=1, source_target_pairs={{0,12},{4,8},{8,4},{12,0},{1,13},{5,9},{9,5},{13,1},{2,14},{6,10},... | collective-permute-start | bytes 393224 | tf_op jit(solution)/shard_map/ppermute | solution.py:515
  26.9 6.7 %collective-permute-start.9 = (f32[8,16,256]{2,1,0:T(8,128)S(1)}, f32[8,16,256]{2,1,0:T(8,128)S(1)}, u32[]{:S(2)}, u32[]{:S(2)}) collective-permute-start(f32[8,16,256]{2,1,0:T(8,128)S(1)} %get-tuple-element.61), channel_id=1, source_target_pairs={{0,4},{4,0},{8,12},{12,8},{1,5},{5,1},{9,13},{13,9},{2,6},{6,2},{1... | collective-permute-start | bytes 393224 | tf_op jit(solution)/shard_map/ppermute | solution.py:515

commit v4 on v3

--- a/solution.py
+++ b/solution.py
@@ -20,7 +20,6 @@
 IN_SMEM = pl.BlockSpec(memory_space=pltpu.SMEM)
 IN_PLACE = pl.BlockSpec(memory_space=pltpu.HBM)
 LONG = pl.CostEstimate(flops=10**10, bytes_accessed=10**8, transcendentals=0)
-LAST = LONG
 
 
 def kept(shape):
@@ -186,7 +185,7 @@
     start = lax.axis_index("sub") * depth
     layer = lax.broadcasted_iota(jnp.int32, (depth, width), 0)
     column = lax.broadcasted_iota(jnp.int32, (depth, width), 1)
-    return (layer == cells[1] - start) & (column == cells[2])
+    return (layer == cells[0, 1] - start) & (column == cells[0, 2])
 
 
 def load(sources, fields, sems):
@@ -203,14 +202,14 @@
 
 
 def rims_kernel(
-    forward, adjoint, velocity, pair, other, p, q, *refs
+    forward, adjoint, velocity, source, wavelet, pair, other, p, q, *refs
 ):
     onto, (sems, small_sems) = refs[:-2], refs[-2:]
     half = pair.shape[0] // 2
     copies = load((forward.at[0, 1], adjoint.at[0, 1]), (p, q), sems)
     small = [
         pltpu.make_async_copy(source, target, small_sems.at[index])
-        for index, (source, target) in enumerate(zip((velocity,), onto))
+        for index, (source, target) in enumerate(zip((velocity, source, wavelet), onto))
     ]
     for copy in small:
         copy.start()
@@ -224,16 +223,11 @@
 
 
 def first_kernel(
-    source, wavelet, anchors, receivers_in, residuals_in, forward, adjoint, p, q,
-    cells, amounts, free_p, lap_p, free_q, lap_q, free_q2, mixed, along_y, along_xz, across,
+    receivers_in, residuals_in, forward, adjoint, p, q,
+    free_p, lap_p, free_q, lap_q, free_q2, mixed, along_y, along_xz, across,
     spread, later, receivers, residuals, sems, small_sems,
 ):
     rows, depth, width = lap_p.shape
-    for index in range(3):
-        cells[index] = source[0, index]
-    cells[3] = jnp.max(anchors[...])
-    for step in range(2):
-        amounts[step] = wavelet[0, step]
     copies = load((forward.at[0, 0], adjoint.at[0, 0]), (later.at[0], later.at[1]), sems)
     small = [
         pltpu.make_async_copy(given_ref, target, small_sems.at[index])
@@ -281,7 +275,7 @@
     lax.fori_loop(0, rows, row, 0, unroll=4)
 
 
-def full_kernel(lap_p, lap_q, mixed, now_q, pair, other, full_p, full_q, full_mixed):
+def full_kernel(lap_p, lap_q, mixed, now_q, other, pair, full_p, full_q, full_mixed):
     depth = lap_p.shape[1]
     half = pair.shape[0] // 2
     full_p[...] = lap_p[...]
@@ -300,10 +294,10 @@
         add_side(message.at[half:], is_pair, depth, add_q)
 
 
-def step_kernel(plans, cells, amounts, free_p, free_q, full_p, full_q, *refs):
+def step_kernel(plans, anchors, cells, amounts, free_p, free_q, full_p, full_q, *refs):
     tiles, (courant, p1, q1, pair, other_p, other_q) = refs[: len(plans) + 1], refs[len(plans) + 1 :]
     tile_rows = tiles[0].shape[0]
-    for tile, place in zip(tiles, places(plans, cells)):
+    for tile, place in zip(tiles, places(plans, anchors)):
 
         def put():
             speed = F32(SPACING_RATIO) * tile[...]
@@ -316,17 +310,17 @@
         pl.when((place >= 0) & (place < APT))(put)
     rows, depth, width = p1.shape
     half = rows // 2
-    x0 = cells[0]
-    p1[x0] = p1[x0] + jnp.where(cell_mask(cells, depth, width), amounts[0], 0.0)
+    x0 = cells[0, 0]
+    p1[x0] = p1[x0] + jnp.where(cell_mask(cells, depth, width), amounts[0, 0], 0.0)
     pair[0:half], other_p[...] = pack_rims(p1[...])
     pair[half:], other_q[...] = pack_rims(q1[...])
 
 
-def places(plans, cells):
+def places(plans, anchors):
     count = lax.axis_size("shot")
     me = lax.axis_index("shot")
     peers = [me] + [peer(me) for _, _, peer in plans]
-    return [lax.rem(peer - cells[3] + count, count) for peer in peers]
+    return [lax.rem(peer - anchors[0] + count, count) for peer in peers]
 
 
 def put_tile(out, image, place):
@@ -348,7 +342,7 @@
 
 
 def image_kernel(
-    plans, cells, amounts, q0, q1, courant, mixed, lap_p, pair, other, full_p, *refs
+    plans, anchors, cells, amounts, q0, q1, courant, mixed, lap_p, pair, other, full_p, *refs
 ):
     outs, image = refs[:-1], refs[-1]
     rows, depth, width = q1.shape
@@ -365,11 +359,11 @@
         return 0
 
     lax.fori_loop(0, rows, row, 0, unroll=4)
-    x0 = cells[0]
+    x0 = cells[0, 0]
     here = cell_mask(cells, depth, width)
-    added = q0[x0] * jnp.where(here, amounts[0], 0.0) + q1[x0] * jnp.where(here, amounts[1], 0.0)
+    added = q0[x0] * jnp.where(here, amounts[0, 0], 0.0) + q1[x0] * jnp.where(here, amounts[0, 1], 0.0)
     image[x0] = image[x0] + added
-    for out, place in zip(outs, places(plans, cells)):
+    for out, place in zip(outs, places(plans, anchors)):
         put_tile(out, image, place)
 
 
@@ -392,8 +386,8 @@
         return 0
 
     lax.fori_loop(0, rows, row_p, 0, unroll=4)
-    x0 = cells[0]
-    amount = jnp.where(cell_mask(cells, depth, width), amounts[1], 0.0)
+    x0 = cells[0, 0]
+    amount = jnp.where(cell_mask(cells, depth, width), amounts[0, 1], 0.0)
     p2[x0] = p2[x0] + amount
     save(p2, forward_out.at[0, 1])
     put_laplacian(lap_q, q1[...], along_y, along_xz, across)
@@ -440,15 +434,16 @@
 
     arriving = [lax.ppermute(velocity, "shot", fetch) for fetch, _, _ in plans_in]
 
-    pair, other, p0, q0, tile = call(
+    pair, other, p0, q0, tile, cells, amounts = call(
         rims_kernel,
-        [given(rims)] * 2 + [kept(field)] * 2 + [kept(velocity.shape)],
-        [(IN_PLACE, in_hbm(a)) for a in (forward_pair, adjoint_pair, velocity)],
-        out_specs=[IN_VMEM] * 5,
-        scratch=[pltpu.SemaphoreType.DMA((2, 4)), pltpu.SemaphoreType.DMA((1,))],
+        [given(rims)] * 2 + [kept(field)] * 2 + [kept(velocity.shape)]
+        + [pltpu.SMEM(a.shape, a.dtype) for a in (source_cells, wavelet)],
+        [(IN_PLACE, in_hbm(a)) for a in (forward_pair, adjoint_pair, velocity, source_cells, wavelet)],
+        out_specs=[IN_VMEM] * 5 + [IN_SMEM] * 2,
+        scratch=[pltpu.SemaphoreType.DMA((2, 2)), pltpu.SemaphoreType.DMA((3,))],
         name="rims",
     )
-    pair, other = swap(pair, 0), swap(other, 1)
+    other, pair = swap(other, 1), swap(pair, 0)
 
     size = min(rows, 256 // depth) * depth
     operators = [
@@ -456,16 +451,14 @@
         pltpu.VMEM((size, 2 * size), BF16),
         pltpu.VMEM((2, size, 2 * RIM * depth), BF16),
     ]
-    cells, amounts, free_p, lap_p, free_q, lap_q, free_q2, mixed, *operators = call(
+    free_p, lap_p, free_q, lap_q, free_q2, mixed, *operators = call(
         first_kernel,
-        [pltpu.SMEM((4,), jnp.int32), pltpu.SMEM((2,), F32)] + [kept(field)] * 6 + operators,
+        [kept(field)] * 6 + operators,
         [
-            (IN_SMEM, source_cells), (IN_SMEM, wavelet), (IN_VMEM, anchors),
             (IN_PLACE, in_hbm(receiver_cells)), (IN_PLACE, in_hbm(residuals)),
             (IN_PLACE, in_hbm(forward_pair)), (IN_PLACE, in_hbm(adjoint_pair)),
             (IN_VMEM, on_chip(p0)), (IN_VMEM, on_chip(q0)),
         ],
-        out_specs=[IN_SMEM] * 2 + [IN_VMEM] * 9,
         scratch=[
             pltpu.VMEM((2,) + field, F32),
             pltpu.VMEM((2,) + field, F32),
@@ -482,13 +475,13 @@
     full_p, full_q, mixed = call(
         full_kernel,
         [kept(field)] * 3,
-        [(IN_VMEM, on_chip(a)) for a in (lap_p, lap_q, mixed, q0)] + [(IN_VMEM, pair), (IN_VMEM, other)],
+        [(IN_VMEM, on_chip(a)) for a in (lap_p, lap_q, mixed, q0)] + [(IN_VMEM, other), (IN_VMEM, pair)],
         name="full",
     )
     courant, p1, q1, pair, other_p, other_q = call(
         functools.partial(step_kernel, plans_in),
         [kept(field)] * 3 + [given(rims)] + [given((rows // 2, 2 * RIM, width))] * 2,
-        scalars
+        [(IN_SMEM, anchors)] + scalars
         + [(IN_VMEM, on_chip(a)) for a in (free_p, free_q, full_p, full_q)]
         + [(IN_VMEM, on_chip(tile))]
         + [(IN_VMEM, other_tile) for other_tile in arriving],
@@ -505,7 +498,7 @@
     lap_p1, *images = call(
         functools.partial(image_kernel, plans),
         [kept(field)] + [given(velocity.shape)] * (len(plans) + 1),
-        scalars
+        [(IN_SMEM, anchors)] + scalars
         + [(IN_VMEM, on_chip(a)) for a in (q0, q1, courant, mixed, lap_p1)]
         + [(IN_VMEM, pair), (IN_VMEM, other_p)],
         scratch=[pltpu.VMEM(field, F32)],
@@ -524,7 +517,7 @@
         out_specs=[IN_PLACE, IN_PLACE],
         scratch=[pltpu.VMEM(field, F32)] * 3 + [pltpu.SemaphoreType.DMA((4,))],
         name="last",
-        cost=LAST,
+        cost=LONG,
     )
 
     (gradient,) = call(

time: 34.5 us -> 34.4 us (level)
  starting transfers between devices: 18.1 us -> 18.8 us
  local copies, waits for them, and re-layouts: 0.66 us -> 0 us
  Pallas kernels: 8.76 us -> 8.15 us
  waiting for transfers between devices: 5.38 us -> 5.88 us
    ppermute x5, waiting for transfers between devices: 0.52 us -> 1.32 us  [swap(): return lax.ppermute(message, 'sub', ahead + [(i, j) for j, i in ahead])]
    ppermute x3, starting transfers between devices: 3.66 us -> 4.33 us  [on_device(): lax.ppermute(image, 'shot', send)]
    unnamed x4 -> x0, local copies, waits for them, and re-layouts: 0.66 us -> none
    pallas_call x8, Pallas kernels: 8.76 us -> 8.15 us  [call(): pl.pallas_call(kernel, out_shape=tuple(outs), in_specs=[spec for spec, _...]
  transfers between devices with their start and end apart: 11 -> 11, of which waited for: 4 -> 4; matrix products, arithmetic and copies ran while one was open for 0% -> 0% of each run, Pallas kernels for 23% -> 21%
where the time goes in v4:
time: 34.4 us; the launch traced here: 34.2 us
  starting transfers between devices  18.8 us (55%)
  Pallas kernels  8.15 us (24%)
  waiting for transfers between devices  5.88 us (17%)
  between operations  1.4 us (4%)
    ppermute x5, starting transfers between devices, swap(): return lax.ppermute(message, 'sub', ahead + [(i, j) for j, i in ahead])  9.94 us
    pallas_call x8, Pallas kernels, call(): pl.pallas_call(kernel, out_shape=tuple(outs), in_specs=[spec for spec, _...  8.15 us
    ppermute x3, waiting for transfers between devices, on_device(): lax.ppermute(image, 'shot', send)  4.55 us
    ppermute x3, starting transfers between devices, on_device(): lax.ppermute(velocity, 'shot', fetch)  4.5 us
    ppermute x3, starting transfers between devices, on_device(): lax.ppermute(image, 'shot', send)  4.33 us
    ppermute x5, waiting for transfers between devices, swap(): return lax.ppermute(message, 'sub', ahead + [(i, j) for j, i in ahead])  1.32 us
  transfers between devices with their start and end apart: 11, of which 4 were waited for; matrix products, arithmetic and copies ran while one was open for 0% of the time, Pallas kernels for 21%

profile of v4, /device:TPU:1, one launch (start us, length us, event | category | flops | bytes accessed | tf_op | source)
XLA Modules:
  0.0 34.2 jit_solution(17577367730218867807)
XLA Ops:
  0.6 3.2 %collective-permute-start.2 = (f32[8,16,256]{2,1,0:T(8,128)}, f32[8,16,256]{2,1,0:T(8,128)S(1)}, u32[]{:S(2)}, u32[]{:S(2)}) collective-permute-start(f32[8,16,256]{2,1,0:T(8,128)} %velocity.1), channel_id=1, source_target_pairs={{0,8},{4,12},{8,0},{12,4},{1,9},{5,13},{9,1},{13,5},{2,10},{6,14},... | collective-permute-start | bytes 393224 | tf_op jit(solution)/shard_map/ppermute | solution.py:435
  3.8 1.1 %collective-permute-start.4 = (f32[8,16,256]{2,1,0:T(8,128)}, f32[8,16,256]{2,1,0:T(8,128)S(1)}, u32[]{:S(2)}, u32[]{:S(2)}) collective-permute-start(f32[8,16,256]{2,1,0:T(8,128)} %velocity.1), channel_id=1, source_target_pairs={{0,12},{4,8},{8,4},{12,0},{1,13},{5,9},{9,5},{13,1},{2,14},{6,10},... | collective-permute-start | bytes 393224 | tf_op jit(solution)/shard_map/ppermute | solution.py:435
  4.9 0.2 collective-permute-start.3
  5.1 1.3 %rims.1 = (f32[32,8,256]{2,1,0:T(8,128)S(1)}, f32[32,8,256]{2,1,0:T(8,128)S(1)}, f32[32,16,256]{2,1,0:T(8,128)S(1)}, f32[32,16,256]{2,1,0:T(8,128)S(1)}, f32[8,1...) custom-call(f32[1,2,32,16,256]{4,3,2,1,0:T(8,128)} %forward.3, f32[1,2,32,16,256]{4,3,2,1,0:T(8,128)} %adjoint.3, ...), custom_call_target="tpu_custom_call" | custom-call | tf_op jit(solution)/shard_map/rims/pallas_call | solution.py:46
  6.5 4.2 %collective-permute-start = (f32[32,8,256]{2,1,0:T(8,128)S(1)}, f32[32,8,256]{2,1,0:T(8,128)S(1)}, u32[]{:S(2)}, u32[]{:S(2)}) collective-permute-start(f32[32,8,256]{2,1,0:T(8,128)S(1)} %get-tuple-element.45), channel_id=1, source_target_pairs={{1,2},{2,1},{5,6},{6,5},{9,10},{10,9},{13,14},{14,13},{17,18},{18,... | collective-permute-start | bytes 786440 | tf_op jit(solution)/shard_map/ppermute | solution.py:421
  10.7 0.1 collective-permute-start.1
  10.8 2.5 %first.1 = (f32[32,16,256]{2,1,0:T(8,128)S(1)}, f32[32,16,256]{2,1,0:T(8,128)S(1)}, f32[32,16,256]{2,1,0:T(8,128)S(1)}, f32[32,16,256]{2,1,0:T(8,128)S(1)}, f32[...) custom-call(s32[3,1,256]{2,1,0:T(1,128)} %bitcast.1, ...), custom_call_target="tpu_custom_call" | custom-call | flops 10000000000 | bytes 100000000 | tf_op jit(solution)/shard_map/first/pallas_call | solution.py:46
  13.9 1.1 %collective-permute-done.other = f32[32,8,256]{2,1,0:T(8,128)S(1)} collective-permute-done((f32[32,8,256]{2,1,0:T(8,128)S(1)}, f32[32,8,256]{2,1,0:T(8,128)S(1)}, u32[]{:S(2)}, u32[]{:S(2)}) %collective-permute-start) | collective-permute-done | bytes 262176 | tf_op jit(solution)/shard_map/ppermute | solution.py:421
  15.1 0.0 collective-permute-done.1.pair
  15.1 0.6 %full.1 = (f32[32,16,256]{2,1,0:T(8,128)S(1)}, f32[32,16,256]{2,1,0:T(8,128)S(1)}, f32[32,16,256]{2,1,0:T(8,128)S(1)}) custom-call(f32[32,16,256]{2,1,0:T(8,128)S(1)} %get-tuple-element.42.lap_p, f32[32,16,256]{2,1,0:T(8,128)S(1)} %get-tuple-element.43.lap_q, f32[32,16,256]{2,1,0:T(8,128)S(1)} %get-tuple-element.44.mixed, ...), custom_call_target="tpu_custom_call" | custom-call | tf_op jit(solution)/shard_map/full/pallas_call | solution.py:46
  15.6 0.0 collective-permute-done.2.refs_1_
  15.6 0.0 collective-permute-done.4.refs_3_
  15.7 0.0 collective-permute-done.3.refs_2_
  15.7 0.3 step.1
  16.0 0.1 collective-permute-start.5
  16.1 3.3 %collective-permute-start.6 = (f32[16,8,256]{2,1,0:T(8,128)S(1)}, f32[16,8,256]{2,1,0:T(8,128)S(1)}, u32[]{:S(2)}, u32[]{:S(2)}) collective-permute-start(f32[16,8,256]{2,1,0:T(8,128)S(1)} %get-tuple-element.57), channel_id=1, source_target_pairs={{1,2},{2,1},{5,6},{6,5},{9,10},{10,9},{13,14},{14,13},{17,18},{18,... | collective-permute-start | bytes 393224 | tf_op jit(solution)/shard_map/ppermute | solution.py:421
  19.4 2.2 %collective-permute-start.10 = (f32[16,8,256]{2,1,0:T(8,128)S(1)}, f32[16,8,256]{2,1,0:T(8,128)S(1)}, u32[]{:S(2)}, u32[]{:S(2)}) collective-permute-start(f32[16,8,256]{2,1,0:T(8,128)S(1)} %get-tuple-element.64), channel_id=1, source_target_pairs={{1,2},{2,1},{5,6},{6,5},{9,10},{10,9},{13,14},{14,13},{17,18},{18,... | collective-permute-start | bytes 393224 | tf_op jit(solution)/shard_map/ppermute | solution.py:421
  21.6 0.5 %inner.1.lap_p = f32[32,16,256]{2,1,0:T(8,128)S(1)} custom-call(f32[32,16,256]{2,1,0:T(8,128)S(1)} %get-tuple-element.52.p1, bf16[512,256]{1,0:T(8,128)(2,1)S(1)} %get-tuple-element.53.along_y, bf16[256,512]{1,0:T(8,128)(2,1)S(1)} %get-tuple-element.54.along_xz, bf16[2,256,128]{2,1,0:T(8,128)(2,1)S(1)} %get-tuple-element.55.across), custom_call_target="tpu_custom_call" | custom-call | tf_op jit(solution)/shard_map/inner/pallas_call | solution.py:46
  22.2 0.2 collective-permute-done.6.other
  22.4 0.0 collective-permute-done.5.pair
  22.4 0.5 %image.1 = (f32[32,16,256]{2,1,0:T(8,128)S(1)}, f32[8,16,256]{2,1,0:T(8,128)S(1)}, f32[8,16,256]{2,1,0:T(8,128)S(1)}, f32[8,16,256]{2,1,0:T(8,128)S(1)}, f32[8,16,256]{2,1,0:T(8,128)S(1)}) custom-call(s32[1]{0:T(128)S(6)} %copy.11.anchors, s32[1,3]{1,0:T(1,128)S(4)} %get-tuple-element.36.cells, f32[1,2]{1,0:T(1,128)S(4)} %get-tuple-element.37.amounts, ...), custom_call_target="tpu_custom_call" | custom-call | tf_op jit(solution)/shard_map/image/pallas_call | solution.py:46
  22.8 4.0 %collective-permute-start.7 = (f32[8,16,256]{2,1,0:T(8,128)S(1)}, f32[8,16,256]{2,1,0:T(8,128)S(1)}, u32[]{:S(2)}, u32[]{:S(2)}) collective-permute-start(f32[8,16,256]{2,1,0:T(8,128)S(1)} %get-tuple-element.59), channel_id=1, source_target_pairs={{0,8},{4,12},{8,0},{12,4},{1,9},{5,13},{9,1},{13,5},{2,10},{6,14},... | collective-permute-start | bytes 393224 | tf_op jit(solution)/shard_map/ppermute | solution.py:508
  26.8 0.0 collective-permute-start.8
  26.8 0.4 %collective-permute-start.9 = (f32[8,16,256]{2,1,0:T(8,128)S(1)}, f32[8,16,256]{2,1,0:T(8,128)S(1)}, u32[]{:S(2)}, u32[]{:S(2)}) collective-permute-start(f32[8,16,256]{2,1,0:T(8,128)S(1)} %get-tuple-element.61), channel_id=1, source_target_pairs={{0,4},{4,0},{8,12},{12,8},{1,5},{5,1},{9,13},{13,9},{2,6},{6,2},{1... | collective-permute-start | bytes 393224 | tf_op jit(solution)/shard_map/ppermute | solution.py:508
  27.2 0.0 collective-permute-done.10.other
  27.2 1.8 %last.1 = (f32[1,2,32,16,256]{4,3,2,1,0:T(8,128)}, f32[1,2,32,16,256]{4,3,2,1,0:T(8,128)}) custom-call(s32[1,3]{1,0:T(1,128)S(4)} %get-tuple-element.36.cells, f32[1,2]{1,0:T(1,128)S(4)} %get-tuple-element.37.amounts, f32[32,16,256]{2,1,0:T(8,128)S(1)} %get-tuple-element.39.p.p0, f32[32,16,256]{2,1,0:T(8,128)S(1)} %get-tuple-element.52.p1, ...), custom_call_target="tpu_custom_call" | custom-call | flops 10000000000 | bytes 100000000 | tf_op jit(solution)/shard_map/last/pallas_call | solution.py:46
  29.0 4.2 %collective-permute-done.7.refs_1_ = f32[8,16,256]{2,1,0:T(8,128)S(1)} collective-permute-done((f32[8,16,256]{2,1,0:T(8,128)S(1)}, f32[8,16,256]{2,1,0:T(8,128)S(1)}, u32[]{:S(2)}, u32[]{:S(2)}) %collective-permute-start.7) | collective-permute-done | bytes 131104 | tf_op jit(solution)/shard_map/ppermute | solution.py:508
  33.1 0.0 collective-permute-done.8.refs_2_
  33.1 0.4 %collective-permute-done.9.refs_3_ = f32[8,16,256]{2,1,0:T(8,128)S(1)} collective-permute-done((f32[8,16,256]{2,1,0:T(8,128)S(1)}, f32[8,16,256]{2,1,0:T(8,128)S(1)}, u32[]{:S(2)}, u32[]{:S(2)}) %collective-permute-start.9) | collective-permute-done | bytes 131104 | tf_op jit(solution)/shard_map/ppermute | solution.py:508
  33.5 0.7 %gradient.1 = f32[8,16,256]{2,1,0:T(8,128)} custom-call(f32[8,16,256]{2,1,0:T(8,128)S(1)} %get-tuple-element.35.refs_0_.velocity, f32[8,16,256]{2,1,0:T(8,128)S(1)} %get-tuple-element.58.refs_0_, f32[8,16,256]{2,1,0:T(8,128)S(1)} %collective-permute-done.7.refs_1_, f32[8,16,256]{2,1,0:T(8,128)S(1)} %collective-permute-done.8.refs_2_, ...), custom_call_target="tpu_custom_call" | custom-call | tf_op jit(solution)/shard_map/gradient/pallas_call | solution.py:46
Async XLA Ops:
  0.6 15.0 %collective-permute-start.2 = (f32[8,16,256]{2,1,0:T(8,128)}, f32[8,16,256]{2,1,0:T(8,128)S(1)}, u32[]{:S(2)}, u32[]{:S(2)}) collective-permute-start(f32[8,16,256]{2,1,0:T(8,128)} %velocity.1), channel_id=1, source_target_pairs={{0,8},{4,12},{8,0},{12,4},{1,9},{5,13},{9,1},{13,5},{2,10},{6,14},... | collective-permute-start | bytes 393224 | tf_op jit(solution)/shard_map/ppermute | solution.py:435
  3.8 11.8 %collective-permute-start.4 = (f32[8,16,256]{2,1,0:T(8,128)}, f32[8,16,256]{2,1,0:T(8,128)S(1)}, u32[]{:S(2)}, u32[]{:S(2)}) collective-permute-start(f32[8,16,256]{2,1,0:T(8,128)} %velocity.1), channel_id=1, source_target_pairs={{0,12},{4,8},{8,4},{12,0},{1,13},{5,9},{9,5},{13,1},{2,14},{6,10},... | collective-permute-start | bytes 393224 | tf_op jit(solution)/shard_map/ppermute | solution.py:435
  4.9 10.7 %collective-permute-start.3 = (f32[8,16,256]{2,1,0:T(8,128)}, f32[8,16,256]{2,1,0:T(8,128)S(1)}, u32[]{:S(2)}, u32[]{:S(2)}) collective-permute-start(f32[8,16,256]{2,1,0:T(8,128)} %velocity.1), channel_id=1, source_target_pairs={{0,4},{4,0},{8,12},{12,8},{1,5},{5,1},{9,13},{13,9},{2,6},{6,2},{1... | collective-permute-start | bytes 393224 | tf_op jit(solution)/shard_map/ppermute | solution.py:435
  6.5 8.6 %collective-permute-start = (f32[32,8,256]{2,1,0:T(8,128)S(1)}, f32[32,8,256]{2,1,0:T(8,128)S(1)}, u32[]{:S(2)}, u32[]{:S(2)}) collective-permute-start(f32[32,8,256]{2,1,0:T(8,128)S(1)} %get-tuple-element.45), channel_id=1, source_target_pairs={{1,2},{2,1},{5,6},{6,5},{9,10},{10,9},{13,14},{14,13},{17,18},{18,... | collective-permute-start | bytes 786440 | tf_op jit(solution)/shard_map/ppermute | solution.py:421
  10.7 4.3 %collective-permute-start.1 = (f32[32,8,256]{2,1,0:T(8,128)S(1)}, f32[32,8,256]{2,1,0:T(8,128)S(1)}, u32[]{:S(2)}, u32[]{:S(2)}) collective-permute-start(f32[32,8,256]{2,1,0:T(8,128)S(1)} %get-tuple-element.46), channel_id=1, source_target_pairs={{0,1},{2,3},{1,0},{3,2},{4,5},{6,7},{5,4},{7,6},{8,9},{10,11},{9,8... | collective-permute-start | bytes 786440 | tf_op jit(solution)/shard_map/ppermute | solution.py:421
  16.0 6.4 %collective-permute-start.5 = (f32[32,8,256]{2,1,0:T(8,128)S(1)}, f32[32,8,256]{2,1,0:T(8,128)S(1)}, u32[]{:S(2)}, u32[]{:S(2)}) collective-permute-start(f32[32,8,256]{2,1,0:T(8,128)S(1)} %get-tuple-element.56), channel_id=1, source_target_pairs={{0,1},{2,3},{1,0},{3,2},{4,5},{6,7},{5,4},{7,6},{8,9},{10,11},{9,8... | collective-permute-start | bytes 786440 | tf_op jit(solution)/shard_map/ppermute | solution.py:421
  16.1 6.3 %collective-permute-start.6 = (f32[16,8,256]{2,1,0:T(8,128)S(1)}, f32[16,8,256]{2,1,0:T(8,128)S(1)}, u32[]{:S(2)}, u32[]{:S(2)}) collective-permute-start(f32[16,8,256]{2,1,0:T(8,128)S(1)} %get-tuple-element.57), channel_id=1, source_target_pairs={{1,2},{2,1},{5,6},{6,5},{9,10},{10,9},{13,14},{14,13},{17,18},{18,... | collective-permute-start | bytes 393224 | tf_op jit(solution)/shard_map/ppermute | solution.py:421
  19.4 7.7 %collective-permute-start.10 = (f32[16,8,256]{2,1,0:T(8,128)S(1)}, f32[16,8,256]{2,1,0:T(8,128)S(1)}, u32[]{:S(2)}, u32[]{:S(2)}) collective-permute-start(f32[16,8,256]{2,1,0:T(8,128)S(1)} %get-tuple-element.64), channel_id=1, source_target_pairs={{1,2},{2,1},{5,6},{6,5},{9,10},{10,9},{13,14},{14,13},{17,18},{18,... | collective-permute-start | bytes 393224 | tf_op jit(solution)/shard_map/ppermute | solution.py:421
  22.8 10.3 %collective-permute-start.7 = (f32[8,16,256]{2,1,0:T(8,128)S(1)}, f32[8,16,256]{2,1,0:T(8,128)S(1)}, u32[]{:S(2)}, u32[]{:S(2)}) collective-permute-start(f32[8,16,256]{2,1,0:T(8,128)S(1)} %get-tuple-element.59), channel_id=1, source_target_pairs={{0,8},{4,12},{8,0},{12,4},{1,9},{5,13},{9,1},{13,5},{2,10},{6,14},... | collective-permute-start | bytes 393224 | tf_op jit(solution)/shard_map/ppermute | solution.py:508
  26.8 6.4 %collective-permute-start.8 = (f32[8,16,256]{2,1,0:T(8,128)S(1)}, f32[8,16,256]{2,1,0:T(8,128)S(1)}, u32[]{:S(2)}, u32[]{:S(2)}) collective-permute-start(f32[8,16,256]{2,1,0:T(8,128)S(1)} %get-tuple-element.60), channel_id=1, source_target_pairs={{0,12},{4,8},{8,4},{12,0},{1,13},{5,9},{9,5},{13,1},{2,14},{6,10},... | collective-permute-start | bytes 393224 | tf_op jit(solution)/shard_map/ppermute | solution.py:508
  26.8 6.7 %collective-permute-start.9 = (f32[8,16,256]{2,1,0:T(8,128)S(1)}, f32[8,16,256]{2,1,0:T(8,128)S(1)}, u32[]{:S(2)}, u32[]{:S(2)}) collective-permute-start(f32[8,16,256]{2,1,0:T(8,128)S(1)} %get-tuple-element.61), channel_id=1, source_target_pairs={{0,4},{4,0},{8,12},{12,8},{1,5},{5,1},{9,13},{13,9},{2,6},{6,2},{1... | collective-permute-start | bytes 393224 | tf_op jit(solution)/shard_map/ppermute | solution.py:508

commit v5 on v4

--- a/solution.py
+++ b/solution.py
@@ -275,12 +275,9 @@
     lax.fori_loop(0, rows, row, 0, unroll=4)
 
 
-def full_kernel(lap_p, lap_q, mixed, now_q, other, pair, full_p, full_q, full_mixed):
+def full_kernel(lap_p, lap_q, mixed, now_q, pair, other, full_p, full_q, full_mixed):
     depth = lap_p.shape[1]
     half = pair.shape[0] // 2
-    full_p[...] = lap_p[...]
-    full_q[...] = lap_q[...]
-    full_mixed[...] = mixed[...]
 
     def add_p(span, layers, part):
         full_p[span, layers] = full_p[span, layers] + part
@@ -342,11 +339,10 @@
 
 
 def image_kernel(
-    plans, anchors, cells, amounts, q0, q1, courant, mixed, lap_p, pair, other, full_p, *refs
+    plans, anchors, cells, amounts, q0, q1, courant, mixed, _, pair, other, full_p, *refs
 ):
     outs, image = refs[:-1], refs[-1]
     rows, depth, width = q1.shape
-    full_p[...] = lap_p[...]
 
     def add(span, layers, part):
         full_p[span, layers] = full_p[span, layers] + part
@@ -430,7 +426,7 @@
     field = (rows, depth, width)
     rims = (rows, 2 * RIM, width)
     plans = partners(lax.axis_size("shot"))
-    plans_in = [plans[0], *plans[:0:-1]]
+    plans_in = [plans[1], plans[2], *plans[3:], plans[0]] if len(plans) == 3 else plans
 
     arriving = [lax.ppermute(velocity, "shot", fetch) for fetch, _, _ in plans_in]
 
@@ -443,7 +439,7 @@
         scratch=[pltpu.SemaphoreType.DMA((2, 2)), pltpu.SemaphoreType.DMA((3,))],
         name="rims",
     )
-    other, pair = swap(other, 1), swap(pair, 0)
+    pair, other = swap(pair, 0), swap(other, 1)
 
     size = min(rows, 256 // depth) * depth
     operators = [
@@ -475,8 +471,9 @@
     full_p, full_q, mixed = call(
         full_kernel,
         [kept(field)] * 3,
-        [(IN_VMEM, on_chip(a)) for a in (lap_p, lap_q, mixed, q0)] + [(IN_VMEM, other), (IN_VMEM, pair)],
+        [(IN_VMEM, on_chip(a)) for a in (lap_p, lap_q, mixed, q0)] + [(IN_VMEM, pair), (IN_VMEM, other)],
         name="full",
+        aliases={0: 0, 1: 1, 2: 2},
     )
     courant, p1, q1, pair, other_p, other_q = call(
         functools.partial(step_kernel, plans_in),
@@ -503,6 +500,7 @@
         + [(IN_VMEM, pair), (IN_VMEM, other_p)],
         scratch=[pltpu.VMEM(field, F32)],
         name="image",
+        aliases={7: 0},
     )
     gathered = [images[0]] + [
         lax.ppermute(image, "shot", send) for image, (_, send, _) in zip(images[1:], plans)

time: 34.4 us -> 34.4 us (level)
  waiting for transfers between devices: 5.88 us -> 6.69 us
  starting transfers between devices: 18.8 us -> 18.1 us
    ppermute x3, starting transfers between devices: 4.33 us -> 2.71 us  [on_device(): lax.ppermute(image, 'shot', send)]
    ppermute x5, starting transfers between devices: 9.94 us -> 10.8 us  [swap(): return lax.ppermute(message, 'sub', ahead + [(i, j) for j, i in ahead])]
    ppermute x5, waiting for transfers between devices: 1.32 us -> 2.16 us  [swap(): return lax.ppermute(message, 'sub', ahead + [(i, j) for j, i in ahead])]
  transfers between devices with their start and end apart: 11 -> 11, of which waited for: 4 -> 3; matrix products, arithmetic and copies ran while one was open for 0% -> 0% of each run, Pallas kernels for 21% -> 20%
where the time goes in v5:
time: 34.4 us; the launch traced here: 34.2 us
  starting transfers between devices  18.1 us (53%)
  Pallas kernels  8 us (23%)
  waiting for transfers between devices  6.69 us (19%)
  between operations  1.4 us (4%)
    ppermute x5, starting transfers between devices, swap(): return lax.ppermute(message, 'sub', ahead + [(i, j) for j, i in ahead])  10.8 us
    pallas_call x8, Pallas kernels, call(): pl.pallas_call(kernel, out_shape=tuple(outs), in_specs=[spec for spec, _...  8 us
    ppermute x3, starting transfers between devices, on_device(): lax.ppermute(velocity, 'shot', fetch)  4.58 us
    ppermute x3, waiting for transfers between devices, on_device(): lax.ppermute(image, 'shot', send)  4.51 us
    ppermute x3, starting transfers between devices, on_device(): lax.ppermute(image, 'shot', send)  2.71 us
    ppermute x5, waiting for transfers between devices, swap(): return lax.ppermute(message, 'sub', ahead + [(i, j) for j, i in ahead])  2.16 us
  transfers between devices with their start and end apart: 11, of which 3 were waited for; matrix products, arithmetic and copies ran while one was open for 0% of the time, Pallas kernels for 20%

profile of v5, /device:TPU:1, one launch (start us, length us, event | category | flops | bytes accessed | tf_op | source)
XLA Modules:
  0.0 34.2 jit_solution(13622733983683259941)
XLA Ops:
  0.6 4.2 %collective-permute-start.2 = (f32[8,16,256]{2,1,0:T(8,128)}, f32[8,16,256]{2,1,0:T(8,128)S(1)}, u32[]{:S(2)}, u32[]{:S(2)}) collective-permute-start(f32[8,16,256]{2,1,0:T(8,128)} %velocity.1), channel_id=1, source_target_pairs={{0,12},{4,8},{8,4},{12,0},{1,13},{5,9},{9,5},{13,1},{2,14},{6,10},... | collective-permute-start | bytes 393224 | tf_op jit(solution)/shard_map/ppermute | solution.py:431
  4.8 0.0 collective-permute-start.4
  4.8 0.4 %collective-permute-start.3 = (f32[8,16,256]{2,1,0:T(8,128)}, f32[8,16,256]{2,1,0:T(8,128)S(1)}, u32[]{:S(2)}, u32[]{:S(2)}) collective-permute-start(f32[8,16,256]{2,1,0:T(8,128)} %velocity.1), channel_id=1, source_target_pairs={{0,4},{4,0},{8,12},{12,8},{1,5},{5,1},{9,13},{13,9},{2,6},{6,2},{1... | collective-permute-start | bytes 393224 | tf_op jit(solution)/shard_map/ppermute | solution.py:431
  5.2 1.3 %rims.1 = (f32[32,8,256]{2,1,0:T(8,128)S(1)}, f32[32,8,256]{2,1,0:T(8,128)S(1)}, f32[32,16,256]{2,1,0:T(8,128)S(1)}, f32[32,16,256]{2,1,0:T(8,128)S(1)}, f32[8,1...) custom-call(f32[1,2,32,16,256]{4,3,2,1,0:T(8,128)} %forward.3, f32[1,2,32,16,256]{4,3,2,1,0:T(8,128)} %adjoint.3, ...), custom_call_target="tpu_custom_call" | custom-call | tf_op jit(solution)/shard_map/rims/pallas_call | solution.py:46
  6.6 1.3 %collective-permute-start = (f32[32,8,256]{2,1,0:T(8,128)S(1)}, f32[32,8,256]{2,1,0:T(8,128)S(1)}, u32[]{:S(2)}, u32[]{:S(2)}) collective-permute-start(f32[32,8,256]{2,1,0:T(8,128)S(1)} %get-tuple-element.45), channel_id=1, source_target_pairs={{0,1},{2,3},{1,0},{3,2},{4,5},{6,7},{5,4},{7,6},{8,9},{10,11},{9,8... | collective-permute-start | bytes 786440 | tf_op jit(solution)/shard_map/ppermute | solution.py:417
  7.9 3.2 %collective-permute-start.1 = (f32[32,8,256]{2,1,0:T(8,128)S(1)}, f32[32,8,256]{2,1,0:T(8,128)S(1)}, u32[]{:S(2)}, u32[]{:S(2)}) collective-permute-start(f32[32,8,256]{2,1,0:T(8,128)S(1)} %get-tuple-element.46), channel_id=1, source_target_pairs={{1,2},{2,1},{5,6},{6,5},{9,10},{10,9},{13,14},{14,13},{17,18},{18,... | collective-permute-start | bytes 786440 | tf_op jit(solution)/shard_map/ppermute | solution.py:417
  11.0 2.5 %first.1 = (f32[32,16,256]{2,1,0:T(8,128)S(1)}, f32[32,16,256]{2,1,0:T(8,128)S(1)}, f32[32,16,256]{2,1,0:T(8,128)S(1)}, f32[32,16,256]{2,1,0:T(8,128)S(1)}, f32[...) custom-call(s32[3,1,256]{2,1,0:T(1,128)} %bitcast.1, ...), custom_call_target="tpu_custom_call" | custom-call | flops 10000000000 | bytes 100000000 | tf_op jit(solution)/shard_map/first/pallas_call | solution.py:46
  14.2 0.0 collective-permute-done.pair
  14.2 1.7 %collective-permute-done.1.other = f32[32,8,256]{2,1,0:T(8,128)S(1)} collective-permute-done((f32[32,8,256]{2,1,0:T(8,128)S(1)}, f32[32,8,256]{2,1,0:T(8,128)S(1)}, u32[]{:S(2)}, u32[]{:S(2)}) %collective-permute-start.1) | collective-permute-done | bytes 262176 | tf_op jit(solution)/shard_map/ppermute | solution.py:417
  15.8 0.5 %full.1 = (f32[32,16,256]{2,1,0:T(8,128)S(1)}, f32[32,16,256]{2,1,0:T(8,128)S(1)}, f32[32,16,256]{2,1,0:T(8,128)S(1)}) custom-call(f32[32,16,256]{2,1,0:T(8,128)S(1)} %get-tuple-element.42.lap_p, f32[32,16,256]{2,1,0:T(8,128)S(1)} %get-tuple-element.43.lap_q, ...), custom_call_target="tpu_custom_call", output_to_operand_aliasing={{0}: (0, {}), {1}: (1, {}), {2}: (2, {})} | custom-call | tf_op jit(solution)/shard_map/full/pallas_call | solution.py:46
  16.3 0.0 collective-permute-done.2.refs_1_
  16.3 0.0 collective-permute-done.4.refs_3_
  16.3 0.0 collective-permute-done.3.refs_2_
  16.3 0.3 step.1
  16.7 0.8 %collective-permute-start.5 = (f32[32,8,256]{2,1,0:T(8,128)S(1)}, f32[32,8,256]{2,1,0:T(8,128)S(1)}, u32[]{:S(2)}, u32[]{:S(2)}) collective-permute-start(f32[32,8,256]{2,1,0:T(8,128)S(1)} %get-tuple-element.56), channel_id=1, source_target_pairs={{0,1},{2,3},{1,0},{3,2},{4,5},{6,7},{5,4},{7,6},{8,9},{10,11},{9,8... | collective-permute-start | bytes 786440 | tf_op jit(solution)/shard_map/ppermute | solution.py:417
  17.5 3.0 %collective-permute-start.6 = (f32[16,8,256]{2,1,0:T(8,128)S(1)}, f32[16,8,256]{2,1,0:T(8,128)S(1)}, u32[]{:S(2)}, u32[]{:S(2)}) collective-permute-start(f32[16,8,256]{2,1,0:T(8,128)S(1)} %get-tuple-element.57), channel_id=1, source_target_pairs={{1,2},{2,1},{5,6},{6,5},{9,10},{10,9},{13,14},{14,13},{17,18},{18,... | collective-permute-start | bytes 393224 | tf_op jit(solution)/shard_map/ppermute | solution.py:417
  20.5 2.5 %collective-permute-start.10 = (f32[16,8,256]{2,1,0:T(8,128)S(1)}, f32[16,8,256]{2,1,0:T(8,128)S(1)}, u32[]{:S(2)}, u32[]{:S(2)}) collective-permute-start(f32[16,8,256]{2,1,0:T(8,128)S(1)} %get-tuple-element.64), channel_id=1, source_target_pairs={{1,2},{2,1},{5,6},{6,5},{9,10},{10,9},{13,14},{14,13},{17,18},{18,... | collective-permute-start | bytes 393224 | tf_op jit(solution)/shard_map/ppermute | solution.py:417
  23.0 0.5 %inner.1._ = f32[32,16,256]{2,1,0:T(8,128)S(1)} custom-call(f32[32,16,256]{2,1,0:T(8,128)S(1)} %get-tuple-element.52.p1, bf16[512,256]{1,0:T(8,128)(2,1)S(1)} %get-tuple-element.53.along_y, bf16[256,512]{1,0:T(8,128)(2,1)S(1)} %get-tuple-element.54.along_xz, bf16[2,256,128]{2,1,0:T(8,128)(2,1)S(1)} %get-tuple-element.55.across), custom_call_target="tpu_custom_call" | custom-call | tf_op jit(solution)/shard_map/inner/pallas_call | solution.py:46
  23.5 0.5 %collective-permute-done.6.other = f32[16,8,256]{2,1,0:T(8,128)S(1)} collective-permute-done((f32[16,8,256]{2,1,0:T(8,128)S(1)}, f32[16,8,256]{2,1,0:T(8,128)S(1)}, u32[]{:S(2)}, u32[]{:S(2)}) %collective-permute-start.6) | collective-permute-done | bytes 131104 | tf_op jit(solution)/shard_map/ppermute | solution.py:417
  24.0 0.0 collective-permute-done.5.pair
  24.0 0.4 %image.1 = (f32[32,16,256]{2,1,0:T(8,128)S(1)}, f32[8,16,256]{2,1,0:T(8,128)S(1)}, f32[8,16,256]{2,1,0:T(8,128)S(1)}, f32[8,16,256]{2,1,0:T(8,128)S(1)}, f32[8,16,256]{2,1,0:T(8,128)S(1)}) custom-call(s32[1]{0:T(128)S(6)} %copy.19.anchors, s32[1,3]{1,0:T(1,128)S(4)} %get-tuple-element.36.cells, ...), custom_call_target="tpu_custom_call", output_to_operand_aliasing={{0}: (7, {})} | custom-call | tf_op jit(solution)/shard_map/image/pallas_call | solution.py:46
  24.4 0.8 %collective-permute-start.7 = (f32[8,16,256]{2,1,0:T(8,128)S(1)}, f32[8,16,256]{2,1,0:T(8,128)S(1)}, u32[]{:S(2)}, u32[]{:S(2)}) collective-permute-start(f32[8,16,256]{2,1,0:T(8,128)S(1)} %get-tuple-element.59), channel_id=1, source_target_pairs={{0,8},{4,12},{8,0},{12,4},{1,9},{5,13},{9,1},{13,5},{2,10},{6,14},... | collective-permute-start | bytes 393224 | tf_op jit(solution)/shard_map/ppermute | solution.py:506
  25.2 1.5 %collective-permute-start.8 = (f32[8,16,256]{2,1,0:T(8,128)S(1)}, f32[8,16,256]{2,1,0:T(8,128)S(1)}, u32[]{:S(2)}, u32[]{:S(2)}) collective-permute-start(f32[8,16,256]{2,1,0:T(8,128)S(1)} %get-tuple-element.60), channel_id=1, source_target_pairs={{0,12},{4,8},{8,4},{12,0},{1,13},{5,9},{9,5},{13,1},{2,14},{6,10},... | collective-permute-start | bytes 393224 | tf_op jit(solution)/shard_map/ppermute | solution.py:506
  26.8 0.4 %collective-permute-start.9 = (f32[8,16,256]{2,1,0:T(8,128)S(1)}, f32[8,16,256]{2,1,0:T(8,128)S(1)}, u32[]{:S(2)}, u32[]{:S(2)}) collective-permute-start(f32[8,16,256]{2,1,0:T(8,128)S(1)} %get-tuple-element.61), channel_id=1, source_target_pairs={{0,4},{4,0},{8,12},{12,8},{1,5},{5,1},{9,13},{13,9},{2,6},{6,2},{1... | collective-permute-start | bytes 393224 | tf_op jit(solution)/shard_map/ppermute | solution.py:506
  27.2 0.0 collective-permute-done.10.other
  27.2 1.8 %last.1 = (f32[1,2,32,16,256]{4,3,2,1,0:T(8,128)}, f32[1,2,32,16,256]{4,3,2,1,0:T(8,128)}) custom-call(s32[1,3]{1,0:T(1,128)S(4)} %get-tuple-element.36.cells, f32[1,2]{1,0:T(1,128)S(4)} %get-tuple-element.37.amounts, f32[32,16,256]{2,1,0:T(8,128)S(1)} %get-tuple-element.39.p.p0, f32[32,16,256]{2,1,0:T(8,128)S(1)} %get-tuple-element.52.p1, ...), custom_call_target="tpu_custom_call" | custom-call | flops 10000000000 | bytes 100000000 | tf_op jit(solution)/shard_map/last/pallas_call | solution.py:46
  29.0 4.5 %collective-permute-done.7.refs_1_ = f32[8,16,256]{2,1,0:T(8,128)S(1)} collective-permute-done((f32[8,16,256]{2,1,0:T(8,128)S(1)}, f32[8,16,256]{2,1,0:T(8,128)S(1)}, u32[]{:S(2)}, u32[]{:S(2)}) %collective-permute-start.7) | collective-permute-done | bytes 131104 | tf_op jit(solution)/shard_map/ppermute | solution.py:506
  33.5 0.0 collective-permute-done.8.refs_2_
  33.5 0.0 collective-permute-done.9.refs_3_
  33.5 0.7 %gradient.1 = f32[8,16,256]{2,1,0:T(8,128)} custom-call(f32[8,16,256]{2,1,0:T(8,128)S(1)} %get-tuple-element.35.refs_0_.velocity, f32[8,16,256]{2,1,0:T(8,128)S(1)} %get-tuple-element.58.refs_0_, f32[8,16,256]{2,1,0:T(8,128)S(1)} %collective-permute-done.7.refs_1_, f32[8,16,256]{2,1,0:T(8,128)S(1)} %collective-permute-done.8.refs_2_, ...), custom_call_target="tpu_custom_call" | custom-call | tf_op jit(solution)/shard_map/gradient/pallas_call | solution.py:46
Async XLA Ops:
  0.6 15.7 %collective-permute-start.2 = (f32[8,16,256]{2,1,0:T(8,128)}, f32[8,16,256]{2,1,0:T(8,128)S(1)}, u32[]{:S(2)}, u32[]{:S(2)}) collective-permute-start(f32[8,16,256]{2,1,0:T(8,128)} %velocity.1), channel_id=1, source_target_pairs={{0,12},{4,8},{8,4},{12,0},{1,13},{5,9},{9,5},{13,1},{2,14},{6,10},... | collective-permute-start | bytes 393224 | tf_op jit(solution)/shard_map/ppermute | solution.py:431
  4.8 11.5 %collective-permute-start.4 = (f32[8,16,256]{2,1,0:T(8,128)}, f32[8,16,256]{2,1,0:T(8,128)S(1)}, u32[]{:S(2)}, u32[]{:S(2)}) collective-permute-start(f32[8,16,256]{2,1,0:T(8,128)} %velocity.1), channel_id=1, source_target_pairs={{0,8},{4,12},{8,0},{12,4},{1,9},{5,13},{9,1},{13,5},{2,10},{6,14},... | collective-permute-start | bytes 393224 | tf_op jit(solution)/shard_map/ppermute | solution.py:431
  4.8 11.5 %collective-permute-start.3 = (f32[8,16,256]{2,1,0:T(8,128)}, f32[8,16,256]{2,1,0:T(8,128)S(1)}, u32[]{:S(2)}, u32[]{:S(2)}) collective-permute-start(f32[8,16,256]{2,1,0:T(8,128)} %velocity.1), channel_id=1, source_target_pairs={{0,4},{4,0},{8,12},{12,8},{1,5},{5,1},{9,13},{13,9},{2,6},{6,2},{1... | collective-permute-start | bytes 393224 | tf_op jit(solution)/shard_map/ppermute | solution.py:431
  6.6 7.6 %collective-permute-start = (f32[32,8,256]{2,1,0:T(8,128)S(1)}, f32[32,8,256]{2,1,0:T(8,128)S(1)}, u32[]{:S(2)}, u32[]{:S(2)}) collective-permute-start(f32[32,8,256]{2,1,0:T(8,128)S(1)} %get-tuple-element.45), channel_id=1, source_target_pairs={{0,1},{2,3},{1,0},{3,2},{4,5},{6,7},{5,4},{7,6},{8,9},{10,11},{9,8... | collective-permute-start | bytes 786440 | tf_op jit(solution)/shard_map/ppermute | solution.py:417
  7.9 8.0 %collective-permute-start.1 = (f32[32,8,256]{2,1,0:T(8,128)S(1)}, f32[32,8,256]{2,1,0:T(8,128)S(1)}, u32[]{:S(2)}, u32[]{:S(2)}) collective-permute-start(f32[32,8,256]{2,1,0:T(8,128)S(1)} %get-tuple-element.46), channel_id=1, source_target_pairs={{1,2},{2,1},{5,6},{6,5},{9,10},{10,9},{13,14},{14,13},{17,18},{18,... | collective-permute-start | bytes 786440 | tf_op jit(solution)/shard_map/ppermute | solution.py:417
  16.7 7.4 %collective-permute-start.5 = (f32[32,8,256]{2,1,0:T(8,128)S(1)}, f32[32,8,256]{2,1,0:T(8,128)S(1)}, u32[]{:S(2)}, u32[]{:S(2)}) collective-permute-start(f32[32,8,256]{2,1,0:T(8,128)S(1)} %get-tuple-element.56), channel_id=1, source_target_pairs={{0,1},{2,3},{1,0},{3,2},{4,5},{6,7},{5,4},{7,6},{8,9},{10,11},{9,8... | collective-permute-start | bytes 786440 | tf_op jit(solution)/shard_map/ppermute | solution.py:417
  17.5 6.6 %collective-permute-start.6 = (f32[16,8,256]{2,1,0:T(8,128)S(1)}, f32[16,8,256]{2,1,0:T(8,128)S(1)}, u32[]{:S(2)}, u32[]{:S(2)}) collective-permute-start(f32[16,8,256]{2,1,0:T(8,128)S(1)} %get-tuple-element.57), channel_id=1, source_target_pairs={{1,2},{2,1},{5,6},{6,5},{9,10},{10,9},{13,14},{14,13},{17,18},{18,... | collective-permute-start | bytes 393224 | tf_op jit(solution)/shard_map/ppermute | solution.py:417
  20.5 6.7 %collective-permute-start.10 = (f32[16,8,256]{2,1,0:T(8,128)S(1)}, f32[16,8,256]{2,1,0:T(8,128)S(1)}, u32[]{:S(2)}, u32[]{:S(2)}) collective-permute-start(f32[16,8,256]{2,1,0:T(8,128)S(1)} %get-tuple-element.64), channel_id=1, source_target_pairs={{1,2},{2,1},{5,6},{6,5},{9,10},{10,9},{13,14},{14,13},{17,18},{18,... | collective-permute-start | bytes 393224 | tf_op jit(solution)/shard_map/ppermute | solution.py:417
  24.4 9.0 %collective-permute-start.7 = (f32[8,16,256]{2,1,0:T(8,128)S(1)}, f32[8,16,256]{2,1,0:T(8,128)S(1)}, u32[]{:S(2)}, u32[]{:S(2)}) collective-permute-start(f32[8,16,256]{2,1,0:T(8,128)S(1)} %get-tuple-element.59), channel_id=1, source_target_pairs={{0,8},{4,12},{8,0},{12,4},{1,9},{5,13},{9,1},{13,5},{2,10},{6,14},... | collective-permute-start | bytes 393224 | tf_op jit(solution)/shard_map/ppermute | solution.py:506
  25.2 8.3 %collective-permute-start.8 = (f32[8,16,256]{2,1,0:T(8,128)S(1)}, f32[8,16,256]{2,1,0:T(8,128)S(1)}, u32[]{:S(2)}, u32[]{:S(2)}) collective-permute-start(f32[8,16,256]{2,1,0:T(8,128)S(1)} %get-tuple-element.60), channel_id=1, source_target_pairs={{0,12},{4,8},{8,4},{12,0},{1,13},{5,9},{9,5},{13,1},{2,14},{6,10},... | collective-permute-start | bytes 393224 | tf_op jit(solution)/shard_map/ppermute | solution.py:506
  26.8 6.7 %collective-permute-start.9 = (f32[8,16,256]{2,1,0:T(8,128)S(1)}, f32[8,16,256]{2,1,0:T(8,128)S(1)}, u32[]{:S(2)}, u32[]{:S(2)}) collective-permute-start(f32[8,16,256]{2,1,0:T(8,128)S(1)} %get-tuple-element.61), channel_id=1, source_target_pairs={{0,4},{4,0},{8,12},{12,8},{1,5},{5,1},{9,13},{13,9},{2,6},{6,2},{1... | collective-permute-start | bytes 393224 | tf_op jit(solution)/shard_map/ppermute | solution.py:506

commit v6 on v5

--- a/solution.py
+++ b/solution.py
@@ -320,20 +320,6 @@
     return [lax.rem(peer - anchors[0] + count, count) for peer in peers]
 
 
-def put_tile(out, image, place):
-    tile_rows = out.shape[0]
-    inside = (place >= 0) & (place < APT)
-
-    def put():
-        out[...] = image[pl.ds(place * tile_rows, tile_rows)]
-
-    def clear():
-        out[...] = jnp.zeros(out.shape, F32)
-
-    pl.when(inside)(put)
-    pl.when(jnp.logical_not(inside))(clear)
-
-
 def inner_kernel(p1, along_y, along_xz, across, lap_p):
     put_laplacian(lap_p, p1[...], along_y, along_xz, across)
 
@@ -341,7 +327,7 @@
 def image_kernel(
     plans, anchors, cells, amounts, q0, q1, courant, mixed, _, pair, other, full_p, *refs
 ):
-    outs, image = refs[:-1], refs[-1]
+    outs = refs
     rows, depth, width = q1.shape
 
     def add(span, layers, part):
@@ -350,17 +336,24 @@
     add_side(pair.at[0 : rows // 2], True, depth, add)
     add_side(other, False, depth, add)
 
-    def row(x, _):
-        image[x] = courant[x] * (mixed[x] + q1[x] * full_p[x])
-        return 0
-
-    lax.fori_loop(0, rows, row, 0, unroll=4)
     x0 = cells[0, 0]
     here = cell_mask(cells, depth, width)
     added = q0[x0] * jnp.where(here, amounts[0, 0], 0.0) + q1[x0] * jnp.where(here, amounts[0, 1], 0.0)
-    image[x0] = image[x0] + added
+    tile_rows = outs[0].shape[0]
     for out, place in zip(outs, places(plans, anchors)):
-        put_tile(out, image, place)
+        inside = (place >= 0) & (place < APT)
+        start = place * tile_rows
+
+        def put():
+            for row in range(tile_rows):
+                x = start + row
+                out[row] = courant[x] * (mixed[x] + q1[x] * full_p[x]) + jnp.where(x == x0, added, 0.0)
+
+        def clear():
+            out[...] = jnp.zeros(out.shape, F32)
+
+        pl.when(inside)(put)
+        pl.when(jnp.logical_not(inside))(clear)
 
 
 def last_kernel(
@@ -498,7 +491,6 @@
         [(IN_SMEM, anchors)] + scalars
         + [(IN_VMEM, on_chip(a)) for a in (q0, q1, courant, mixed, lap_p1)]
         + [(IN_VMEM, pair), (IN_VMEM, other_p)],
-        scratch=[pltpu.VMEM(field, F32)],
         name="image",
         aliases={7: 0},
     )

time: 34.4 us -> 34.3 us (level)
  no operation moved by 1% of the time
where the time goes in v6:
time: 34.3 us; the launch traced here: 34.1 us
  starting transfers between devices  18.1 us (53%)
  Pallas kernels  7.95 us (23%)
  waiting for transfers between devices  6.69 us (20%)
  between operations  1.39 us (4%)
    ppermute x5, starting transfers between devices, swap(): return lax.ppermute(message, 'sub', ahead + [(i, j) for j, i in ahead])  10.8 us
    pallas_call x8, Pallas kernels, call(): pl.pallas_call(kernel, out_shape=tuple(outs), in_specs=[spec for spec, _...  7.95 us
    ppermute x3, starting transfers between devices, on_device(): lax.ppermute(velocity, 'shot', fetch)  4.58 us
    ppermute x3, waiting for transfers between devices, on_device(): lax.ppermute(image, 'shot', send)  4.51 us
    ppermute x3, starting transfers between devices, on_device(): lax.ppermute(image, 'shot', send)  2.71 us
    ppermute x5, waiting for transfers between devices, swap(): return lax.ppermute(message, 'sub', ahead + [(i, j) for j, i in ahead])  2.16 us
  transfers between devices with their start and end apart: 11, of which 3 were waited for; matrix products, arithmetic and copies ran while one was open for 0% of the time, Pallas kernels for 20%

profile of v6, /device:TPU:1, one launch (start us, length us, event | category | flops | bytes accessed | tf_op | source)
XLA Modules:
  0.0 34.1 jit_solution(13209409403975930879)
XLA Ops:
  0.6 4.2 %collective-permute-start.2 = (f32[8,16,256]{2,1,0:T(8,128)}, f32[8,16,256]{2,1,0:T(8,128)S(1)}, u32[]{:S(2)}, u32[]{:S(2)}) collective-permute-start(f32[8,16,256]{2,1,0:T(8,128)} %velocity.1), channel_id=1, source_target_pairs={{0,12},{4,8},{8,4},{12,0},{1,13},{5,9},{9,5},{13,1},{2,14},{6,10},... | collective-permute-start | bytes 393224 | tf_op jit(solution)/shard_map/ppermute | solution.py:424
  4.8 0.0 collective-permute-start.4
  4.8 0.4 %collective-permute-start.3 = (f32[8,16,256]{2,1,0:T(8,128)}, f32[8,16,256]{2,1,0:T(8,128)S(1)}, u32[]{:S(2)}, u32[]{:S(2)}) collective-permute-start(f32[8,16,256]{2,1,0:T(8,128)} %velocity.1), channel_id=1, source_target_pairs={{0,4},{4,0},{8,12},{12,8},{1,5},{5,1},{9,13},{13,9},{2,6},{6,2},{1... | collective-permute-start | bytes 393224 | tf_op jit(solution)/shard_map/ppermute | solution.py:424
  5.2 1.3 %rims.1 = (f32[32,8,256]{2,1,0:T(8,128)S(1)}, f32[32,8,256]{2,1,0:T(8,128)S(1)}, f32[32,16,256]{2,1,0:T(8,128)S(1)}, f32[32,16,256]{2,1,0:T(8,128)S(1)}, f32[8,1...) custom-call(f32[1,2,32,16,256]{4,3,2,1,0:T(8,128)} %forward.3, f32[1,2,32,16,256]{4,3,2,1,0:T(8,128)} %adjoint.3, ...), custom_call_target="tpu_custom_call" | custom-call | tf_op jit(solution)/shard_map/rims/pallas_call | solution.py:46
  6.6 1.3 %collective-permute-start = (f32[32,8,256]{2,1,0:T(8,128)S(1)}, f32[32,8,256]{2,1,0:T(8,128)S(1)}, u32[]{:S(2)}, u32[]{:S(2)}) collective-permute-start(f32[32,8,256]{2,1,0:T(8,128)S(1)} %get-tuple-element.45), channel_id=1, source_target_pairs={{0,1},{2,3},{1,0},{3,2},{4,5},{6,7},{5,4},{7,6},{8,9},{10,11},{9,8... | collective-permute-start | bytes 786440 | tf_op jit(solution)/shard_map/ppermute | solution.py:410
  7.9 3.2 %collective-permute-start.1 = (f32[32,8,256]{2,1,0:T(8,128)S(1)}, f32[32,8,256]{2,1,0:T(8,128)S(1)}, u32[]{:S(2)}, u32[]{:S(2)}) collective-permute-start(f32[32,8,256]{2,1,0:T(8,128)S(1)} %get-tuple-element.46), channel_id=1, source_target_pairs={{1,2},{2,1},{5,6},{6,5},{9,10},{10,9},{13,14},{14,13},{17,18},{18,... | collective-permute-start | bytes 786440 | tf_op jit(solution)/shard_map/ppermute | solution.py:410
  11.0 2.5 %first.1 = (f32[32,16,256]{2,1,0:T(8,128)S(1)}, f32[32,16,256]{2,1,0:T(8,128)S(1)}, f32[32,16,256]{2,1,0:T(8,128)S(1)}, f32[32,16,256]{2,1,0:T(8,128)S(1)}, f32[...) custom-call(s32[3,1,256]{2,1,0:T(1,128)} %bitcast.1, ...), custom_call_target="tpu_custom_call" | custom-call | flops 10000000000 | bytes 100000000 | tf_op jit(solution)/shard_map/first/pallas_call | solution.py:46
  14.2 0.0 collective-permute-done.pair
  14.2 1.7 %collective-permute-done.1.other = f32[32,8,256]{2,1,0:T(8,128)S(1)} collective-permute-done((f32[32,8,256]{2,1,0:T(8,128)S(1)}, f32[32,8,256]{2,1,0:T(8,128)S(1)}, u32[]{:S(2)}, u32[]{:S(2)}) %collective-permute-start.1) | collective-permute-done | bytes 262176 | tf_op jit(solution)/shard_map/ppermute | solution.py:410
  15.8 0.5 %full.1 = (f32[32,16,256]{2,1,0:T(8,128)S(1)}, f32[32,16,256]{2,1,0:T(8,128)S(1)}, f32[32,16,256]{2,1,0:T(8,128)S(1)}) custom-call(f32[32,16,256]{2,1,0:T(8,128)S(1)} %get-tuple-element.42.lap_p, f32[32,16,256]{2,1,0:T(8,128)S(1)} %get-tuple-element.43.lap_q, ...), custom_call_target="tpu_custom_call", output_to_operand_aliasing={{0}: (0, {}), {1}: (1, {}), {2}: (2, {})} | custom-call | tf_op jit(solution)/shard_map/full/pallas_call | solution.py:46
  16.3 0.0 collective-permute-done.2.refs_1_
  16.3 0.0 collective-permute-done.4.refs_3_
  16.3 0.0 collective-permute-done.3.refs_2_
  16.3 0.3 step.1
  16.7 0.8 %collective-permute-start.5 = (f32[32,8,256]{2,1,0:T(8,128)S(1)}, f32[32,8,256]{2,1,0:T(8,128)S(1)}, u32[]{:S(2)}, u32[]{:S(2)}) collective-permute-start(f32[32,8,256]{2,1,0:T(8,128)S(1)} %get-tuple-element.56), channel_id=1, source_target_pairs={{0,1},{2,3},{1,0},{3,2},{4,5},{6,7},{5,4},{7,6},{8,9},{10,11},{9,8... | collective-permute-start | bytes 786440 | tf_op jit(solution)/shard_map/ppermute | solution.py:410
  17.5 3.0 %collective-permute-start.6 = (f32[16,8,256]{2,1,0:T(8,128)S(1)}, f32[16,8,256]{2,1,0:T(8,128)S(1)}, u32[]{:S(2)}, u32[]{:S(2)}) collective-permute-start(f32[16,8,256]{2,1,0:T(8,128)S(1)} %get-tuple-element.57), channel_id=1, source_target_pairs={{1,2},{2,1},{5,6},{6,5},{9,10},{10,9},{13,14},{14,13},{17,18},{18,... | collective-permute-start | bytes 393224 | tf_op jit(solution)/shard_map/ppermute | solution.py:410
  20.5 2.5 %collective-permute-start.10 = (f32[16,8,256]{2,1,0:T(8,128)S(1)}, f32[16,8,256]{2,1,0:T(8,128)S(1)}, u32[]{:S(2)}, u32[]{:S(2)}) collective-permute-start(f32[16,8,256]{2,1,0:T(8,128)S(1)} %get-tuple-element.64), channel_id=1, source_target_pairs={{1,2},{2,1},{5,6},{6,5},{9,10},{10,9},{13,14},{14,13},{17,18},{18,... | collective-permute-start | bytes 393224 | tf_op jit(solution)/shard_map/ppermute | solution.py:410
  23.0 0.5 %inner.1._ = f32[32,16,256]{2,1,0:T(8,128)S(1)} custom-call(f32[32,16,256]{2,1,0:T(8,128)S(1)} %get-tuple-element.52.p1, bf16[512,256]{1,0:T(8,128)(2,1)S(1)} %get-tuple-element.53.along_y, bf16[256,512]{1,0:T(8,128)(2,1)S(1)} %get-tuple-element.54.along_xz, bf16[2,256,128]{2,1,0:T(8,128)(2,1)S(1)} %get-tuple-element.55.across), custom_call_target="tpu_custom_call" | custom-call | tf_op jit(solution)/shard_map/inner/pallas_call | solution.py:46
  23.5 0.5 %collective-permute-done.6.other = f32[16,8,256]{2,1,0:T(8,128)S(1)} collective-permute-done((f32[16,8,256]{2,1,0:T(8,128)S(1)}, f32[16,8,256]{2,1,0:T(8,128)S(1)}, u32[]{:S(2)}, u32[]{:S(2)}) %collective-permute-start.6) | collective-permute-done | bytes 131104 | tf_op jit(solution)/shard_map/ppermute | solution.py:410
  24.0 0.0 collective-permute-done.5.pair
  24.0 0.4 %image.1 = (f32[32,16,256]{2,1,0:T(8,128)S(1)}, f32[8,16,256]{2,1,0:T(8,128)S(1)}, f32[8,16,256]{2,1,0:T(8,128)S(1)}, f32[8,16,256]{2,1,0:T(8,128)S(1)}, f32[8,16,256]{2,1,0:T(8,128)S(1)}) custom-call(s32[1]{0:T(128)S(6)} %copy.19.anchors, s32[1,3]{1,0:T(1,128)S(4)} %get-tuple-element.36.cells, ...), custom_call_target="tpu_custom_call", output_to_operand_aliasing={{0}: (7, {})} | custom-call | tf_op jit(solution)/shard_map/image/pallas_call | solution.py:46
  24.4 0.8 %collective-permute-start.7 = (f32[8,16,256]{2,1,0:T(8,128)S(1)}, f32[8,16,256]{2,1,0:T(8,128)S(1)}, u32[]{:S(2)}, u32[]{:S(2)}) collective-permute-start(f32[8,16,256]{2,1,0:T(8,128)S(1)} %get-tuple-element.59), channel_id=1, source_target_pairs={{0,8},{4,12},{8,0},{12,4},{1,9},{5,13},{9,1},{13,5},{2,10},{6,14},... | collective-permute-start | bytes 393224 | tf_op jit(solution)/shard_map/ppermute | solution.py:498
  25.2 1.5 %collective-permute-start.8 = (f32[8,16,256]{2,1,0:T(8,128)S(1)}, f32[8,16,256]{2,1,0:T(8,128)S(1)}, u32[]{:S(2)}, u32[]{:S(2)}) collective-permute-start(f32[8,16,256]{2,1,0:T(8,128)S(1)} %get-tuple-element.60), channel_id=1, source_target_pairs={{0,12},{4,8},{8,4},{12,0},{1,13},{5,9},{9,5},{13,1},{2,14},{6,10},... | collective-permute-start | bytes 393224 | tf_op jit(solution)/shard_map/ppermute | solution.py:498
  26.7 0.4 %collective-permute-start.9 = (f32[8,16,256]{2,1,0:T(8,128)S(1)}, f32[8,16,256]{2,1,0:T(8,128)S(1)}, u32[]{:S(2)}, u32[]{:S(2)}) collective-permute-start(f32[8,16,256]{2,1,0:T(8,128)S(1)} %get-tuple-element.61), channel_id=1, source_target_pairs={{0,4},{4,0},{8,12},{12,8},{1,5},{5,1},{9,13},{13,9},{2,6},{6,2},{1... | collective-permute-start | bytes 393224 | tf_op jit(solution)/shard_map/ppermute | solution.py:498
  27.1 0.0 collective-permute-done.10.other
  27.1 1.8 %last.1 = (f32[1,2,32,16,256]{4,3,2,1,0:T(8,128)}, f32[1,2,32,16,256]{4,3,2,1,0:T(8,128)}) custom-call(s32[1,3]{1,0:T(1,128)S(4)} %get-tuple-element.36.cells, f32[1,2]{1,0:T(1,128)S(4)} %get-tuple-element.37.amounts, f32[32,16,256]{2,1,0:T(8,128)S(1)} %get-tuple-element.39.p.p0, f32[32,16,256]{2,1,0:T(8,128)S(1)} %get-tuple-element.52.p1, ...), custom_call_target="tpu_custom_call" | custom-call | flops 10000000000 | bytes 100000000 | tf_op jit(solution)/shard_map/last/pallas_call | solution.py:46
  28.9 4.5 %collective-permute-done.7.refs_1_ = f32[8,16,256]{2,1,0:T(8,128)S(1)} collective-permute-done((f32[8,16,256]{2,1,0:T(8,128)S(1)}, f32[8,16,256]{2,1,0:T(8,128)S(1)}, u32[]{:S(2)}, u32[]{:S(2)}) %collective-permute-start.7) | collective-permute-done | bytes 131104 | tf_op jit(solution)/shard_map/ppermute | solution.py:498
  33.4 0.0 collective-permute-done.8.refs_2_
  33.4 0.0 collective-permute-done.9.refs_3_
  33.4 0.7 %gradient.1 = f32[8,16,256]{2,1,0:T(8,128)} custom-call(f32[8,16,256]{2,1,0:T(8,128)S(1)} %get-tuple-element.35.refs_0_.velocity, f32[8,16,256]{2,1,0:T(8,128)S(1)} %get-tuple-element.58.refs_0_, f32[8,16,256]{2,1,0:T(8,128)S(1)} %collective-permute-done.7.refs_1_, f32[8,16,256]{2,1,0:T(8,128)S(1)} %collective-permute-done.8.refs_2_, ...), custom_call_target="tpu_custom_call" | custom-call | tf_op jit(solution)/shard_map/gradient/pallas_call | solution.py:46
Async XLA Ops:
  0.6 15.7 %collective-permute-start.2 = (f32[8,16,256]{2,1,0:T(8,128)}, f32[8,16,256]{2,1,0:T(8,128)S(1)}, u32[]{:S(2)}, u32[]{:S(2)}) collective-permute-start(f32[8,16,256]{2,1,0:T(8,128)} %velocity.1), channel_id=1, source_target_pairs={{0,12},{4,8},{8,4},{12,0},{1,13},{5,9},{9,5},{13,1},{2,14},{6,10},... | collective-permute-start | bytes 393224 | tf_op jit(solution)/shard_map/ppermute | solution.py:424
  4.8 11.5 %collective-permute-start.4 = (f32[8,16,256]{2,1,0:T(8,128)}, f32[8,16,256]{2,1,0:T(8,128)S(1)}, u32[]{:S(2)}, u32[]{:S(2)}) collective-permute-start(f32[8,16,256]{2,1,0:T(8,128)} %velocity.1), channel_id=1, source_target_pairs={{0,8},{4,12},{8,0},{12,4},{1,9},{5,13},{9,1},{13,5},{2,10},{6,14},... | collective-permute-start | bytes 393224 | tf_op jit(solution)/shard_map/ppermute | solution.py:424
  4.8 11.5 %collective-permute-start.3 = (f32[8,16,256]{2,1,0:T(8,128)}, f32[8,16,256]{2,1,0:T(8,128)S(1)}, u32[]{:S(2)}, u32[]{:S(2)}) collective-permute-start(f32[8,16,256]{2,1,0:T(8,128)} %velocity.1), channel_id=1, source_target_pairs={{0,4},{4,0},{8,12},{12,8},{1,5},{5,1},{9,13},{13,9},{2,6},{6,2},{1... | collective-permute-start | bytes 393224 | tf_op jit(solution)/shard_map/ppermute | solution.py:424
  6.6 7.6 %collective-permute-start = (f32[32,8,256]{2,1,0:T(8,128)S(1)}, f32[32,8,256]{2,1,0:T(8,128)S(1)}, u32[]{:S(2)}, u32[]{:S(2)}) collective-permute-start(f32[32,8,256]{2,1,0:T(8,128)S(1)} %get-tuple-element.45), channel_id=1, source_target_pairs={{0,1},{2,3},{1,0},{3,2},{4,5},{6,7},{5,4},{7,6},{8,9},{10,11},{9,8... | collective-permute-start | bytes 786440 | tf_op jit(solution)/shard_map/ppermute | solution.py:410
  7.9 8.0 %collective-permute-start.1 = (f32[32,8,256]{2,1,0:T(8,128)S(1)}, f32[32,8,256]{2,1,0:T(8,128)S(1)}, u32[]{:S(2)}, u32[]{:S(2)}) collective-permute-start(f32[32,8,256]{2,1,0:T(8,128)S(1)} %get-tuple-element.46), channel_id=1, source_target_pairs={{1,2},{2,1},{5,6},{6,5},{9,10},{10,9},{13,14},{14,13},{17,18},{18,... | collective-permute-start | bytes 786440 | tf_op jit(solution)/shard_map/ppermute | solution.py:410
  16.7 7.4 %collective-permute-start.5 = (f32[32,8,256]{2,1,0:T(8,128)S(1)}, f32[32,8,256]{2,1,0:T(8,128)S(1)}, u32[]{:S(2)}, u32[]{:S(2)}) collective-permute-start(f32[32,8,256]{2,1,0:T(8,128)S(1)} %get-tuple-element.56), channel_id=1, source_target_pairs={{0,1},{2,3},{1,0},{3,2},{4,5},{6,7},{5,4},{7,6},{8,9},{10,11},{9,8... | collective-permute-start | bytes 786440 | tf_op jit(solution)/shard_map/ppermute | solution.py:410
  17.5 6.6 %collective-permute-start.6 = (f32[16,8,256]{2,1,0:T(8,128)S(1)}, f32[16,8,256]{2,1,0:T(8,128)S(1)}, u32[]{:S(2)}, u32[]{:S(2)}) collective-permute-start(f32[16,8,256]{2,1,0:T(8,128)S(1)} %get-tuple-element.57), channel_id=1, source_target_pairs={{1,2},{2,1},{5,6},{6,5},{9,10},{10,9},{13,14},{14,13},{17,18},{18,... | collective-permute-start | bytes 393224 | tf_op jit(solution)/shard_map/ppermute | solution.py:410
  20.5 6.6 %collective-permute-start.10 = (f32[16,8,256]{2,1,0:T(8,128)S(1)}, f32[16,8,256]{2,1,0:T(8,128)S(1)}, u32[]{:S(2)}, u32[]{:S(2)}) collective-permute-start(f32[16,8,256]{2,1,0:T(8,128)S(1)} %get-tuple-element.64), channel_id=1, source_target_pairs={{1,2},{2,1},{5,6},{6,5},{9,10},{10,9},{13,14},{14,13},{17,18},{18,... | collective-permute-start | bytes 393224 | tf_op jit(solution)/shard_map/ppermute | solution.py:410
  24.4 9.0 %collective-permute-start.7 = (f32[8,16,256]{2,1,0:T(8,128)S(1)}, f32[8,16,256]{2,1,0:T(8,128)S(1)}, u32[]{:S(2)}, u32[]{:S(2)}) collective-permute-start(f32[8,16,256]{2,1,0:T(8,128)S(1)} %get-tuple-element.59), channel_id=1, source_target_pairs={{0,8},{4,12},{8,0},{12,4},{1,9},{5,13},{9,1},{13,5},{2,10},{6,14},... | collective-permute-start | bytes 393224 | tf_op jit(solution)/shard_map/ppermute | solution.py:498
  25.2 8.3 %collective-permute-start.8 = (f32[8,16,256]{2,1,0:T(8,128)S(1)}, f32[8,16,256]{2,1,0:T(8,128)S(1)}, u32[]{:S(2)}, u32[]{:S(2)}) collective-permute-start(f32[8,16,256]{2,1,0:T(8,128)S(1)} %get-tuple-element.60), channel_id=1, source_target_pairs={{0,12},{4,8},{8,4},{12,0},{1,13},{5,9},{9,5},{13,1},{2,14},{6,10},... | collective-permute-start | bytes 393224 | tf_op jit(solution)/shard_map/ppermute | solution.py:498
  26.7 6.7 %collective-permute-start.9 = (f32[8,16,256]{2,1,0:T(8,128)S(1)}, f32[8,16,256]{2,1,0:T(8,128)S(1)}, u32[]{:S(2)}, u32[]{:S(2)}) collective-permute-start(f32[8,16,256]{2,1,0:T(8,128)S(1)} %get-tuple-element.61), channel_id=1, source_target_pairs={{0,4},{4,0},{8,12},{12,8},{1,5},{5,1},{9,13},{13,9},{2,6},{6,2},{1... | collective-permute-start | bytes 393224 | tf_op jit(solution)/shard_map/ppermute | solution.py:498

commit v7 on v6

--- a/solution.py
+++ b/solution.py
@@ -272,7 +272,7 @@
         mixed[x] = own * lap_p[x]
         return 0
 
-    lax.fori_loop(0, rows, row, 0, unroll=4)
+    lax.fori_loop(0, rows, row, 0, unroll=8)
 
 
 def full_kernel(lap_p, lap_q, mixed, now_q, pair, other, full_p, full_q, full_mixed):
@@ -374,7 +374,7 @@
         p2[x] = 2.0 * p1[x] - p0[x] + courant[x] * lap_p[x]
         return 0
 
-    lax.fori_loop(0, rows, row_p, 0, unroll=4)
+    lax.fori_loop(0, rows, row_p, 0, unroll=8)
     x0 = cells[0, 0]
     amount = jnp.where(cell_mask(cells, depth, width), amounts[0, 1], 0.0)
     p2[x0] = p2[x0] + amount
@@ -391,7 +391,7 @@
         q2[x] = 2.0 * q1[x] + free_q2[x] + courant[x] * lap_q[x]
         return 0
 
-    lax.fori_loop(0, rows, row_q, 0, unroll=4)
+    lax.fori_loop(0, rows, row_q, 0, unroll=8)
     save(q2, adjoint_out.at[0, 1])
     for copy in copies:
         copy.wait()

time: 34.3 us -> 34.3 us (level)
  no operation moved by 1% of the time
where the time goes in v7:
time: 34.3 us; the launch traced here: 34.1 us
  starting transfers between devices  18.1 us (53%)
  Pallas kernels  7.89 us (23%)
  waiting for transfers between devices  6.74 us (20%)
  between operations  1.4 us (4%)
    ppermute x5, starting transfers between devices, swap(): return lax.ppermute(message, 'sub', ahead + [(i, j) for j, i in ahead])  10.8 us
    pallas_call x8, Pallas kernels, call(): pl.pallas_call(kernel, out_shape=tuple(outs), in_specs=[spec for spec, _...  7.89 us
    ppermute x3, starting transfers between devices, on_device(): lax.ppermute(velocity, 'shot', fetch)  4.58 us
    ppermute x3, waiting for transfers between devices, on_device(): lax.ppermute(image, 'shot', send)  4.56 us
    ppermute x3, starting transfers between devices, on_device(): lax.ppermute(image, 'shot', send)  2.71 us
    ppermute x5, waiting for transfers between devices, swap(): return lax.ppermute(message, 'sub', ahead + [(i, j) for j, i in ahead])  2.18 us
  transfers between devices with their start and end apart: 11, of which 3 were waited for; matrix products, arithmetic and copies ran while one was open for 0% of the time, Pallas kernels for 20%

profile of v7, /device:TPU:1, one launch (start us, length us, event | category | flops | bytes accessed | tf_op | source)
XLA Modules:
  0.0 34.1 jit_solution(3143701070168294762)
XLA Ops:
  0.6 4.2 %collective-permute-start.2 = (f32[8,16,256]{2,1,0:T(8,128)}, f32[8,16,256]{2,1,0:T(8,128)S(1)}, u32[]{:S(2)}, u32[]{:S(2)}) collective-permute-start(f32[8,16,256]{2,1,0:T(8,128)} %velocity.1), channel_id=1, source_target_pairs={{0,12},{4,8},{8,4},{12,0},{1,13},{5,9},{9,5},{13,1},{2,14},{6,10},... | collective-permute-start | bytes 393224 | tf_op jit(solution)/shard_map/ppermute | solution.py:424
  4.8 0.0 collective-permute-start.4
  4.8 0.4 %collective-permute-start.3 = (f32[8,16,256]{2,1,0:T(8,128)}, f32[8,16,256]{2,1,0:T(8,128)S(1)}, u32[]{:S(2)}, u32[]{:S(2)}) collective-permute-start(f32[8,16,256]{2,1,0:T(8,128)} %velocity.1), channel_id=1, source_target_pairs={{0,4},{4,0},{8,12},{12,8},{1,5},{5,1},{9,13},{13,9},{2,6},{6,2},{1... | collective-permute-start | bytes 393224 | tf_op jit(solution)/shard_map/ppermute | solution.py:424
  5.2 1.3 %rims.1 = (f32[32,8,256]{2,1,0:T(8,128)S(1)}, f32[32,8,256]{2,1,0:T(8,128)S(1)}, f32[32,16,256]{2,1,0:T(8,128)S(1)}, f32[32,16,256]{2,1,0:T(8,128)S(1)}, f32[8,1...) custom-call(f32[1,2,32,16,256]{4,3,2,1,0:T(8,128)} %forward.3, f32[1,2,32,16,256]{4,3,2,1,0:T(8,128)} %adjoint.3, ...), custom_call_target="tpu_custom_call" | custom-call | tf_op jit(solution)/shard_map/rims/pallas_call | solution.py:46
  6.6 1.3 %collective-permute-start = (f32[32,8,256]{2,1,0:T(8,128)S(1)}, f32[32,8,256]{2,1,0:T(8,128)S(1)}, u32[]{:S(2)}, u32[]{:S(2)}) collective-permute-start(f32[32,8,256]{2,1,0:T(8,128)S(1)} %get-tuple-element.45), channel_id=1, source_target_pairs={{0,1},{2,3},{1,0},{3,2},{4,5},{6,7},{5,4},{7,6},{8,9},{10,11},{9,8... | collective-permute-start | bytes 786440 | tf_op jit(solution)/shard_map/ppermute | solution.py:410
  7.9 3.2 %collective-permute-start.1 = (f32[32,8,256]{2,1,0:T(8,128)S(1)}, f32[32,8,256]{2,1,0:T(8,128)S(1)}, u32[]{:S(2)}, u32[]{:S(2)}) collective-permute-start(f32[32,8,256]{2,1,0:T(8,128)S(1)} %get-tuple-element.46), channel_id=1, source_target_pairs={{1,2},{2,1},{5,6},{6,5},{9,10},{10,9},{13,14},{14,13},{17,18},{18,... | collective-permute-start | bytes 786440 | tf_op jit(solution)/shard_map/ppermute | solution.py:410
  11.0 2.5 %first.1 = (f32[32,16,256]{2,1,0:T(8,128)S(1)}, f32[32,16,256]{2,1,0:T(8,128)S(1)}, f32[32,16,256]{2,1,0:T(8,128)S(1)}, f32[32,16,256]{2,1,0:T(8,128)S(1)}, f32[...) custom-call(s32[3,1,256]{2,1,0:T(1,128)} %bitcast.1, ...), custom_call_target="tpu_custom_call" | custom-call | flops 10000000000 | bytes 100000000 | tf_op jit(solution)/shard_map/first/pallas_call | solution.py:46
  14.1 0.0 collective-permute-done.pair
  14.2 1.7 %collective-permute-done.1.other = f32[32,8,256]{2,1,0:T(8,128)S(1)} collective-permute-done((f32[32,8,256]{2,1,0:T(8,128)S(1)}, f32[32,8,256]{2,1,0:T(8,128)S(1)}, u32[]{:S(2)}, u32[]{:S(2)}) %collective-permute-start.1) | collective-permute-done | bytes 262176 | tf_op jit(solution)/shard_map/ppermute | solution.py:410
  15.8 0.5 %full.1 = (f32[32,16,256]{2,1,0:T(8,128)S(1)}, f32[32,16,256]{2,1,0:T(8,128)S(1)}, f32[32,16,256]{2,1,0:T(8,128)S(1)}) custom-call(f32[32,16,256]{2,1,0:T(8,128)S(1)} %get-tuple-element.42.lap_p, f32[32,16,256]{2,1,0:T(8,128)S(1)} %get-tuple-element.43.lap_q, ...), custom_call_target="tpu_custom_call", output_to_operand_aliasing={{0}: (0, {}), {1}: (1, {}), {2}: (2, {})} | custom-call | tf_op jit(solution)/shard_map/full/pallas_call | solution.py:46
  16.3 0.0 collective-permute-done.2.refs_1_
  16.3 0.0 collective-permute-done.4.refs_3_
  16.3 0.0 collective-permute-done.3.refs_2_
  16.3 0.3 step.1
  16.7 0.8 %collective-permute-start.5 = (f32[32,8,256]{2,1,0:T(8,128)S(1)}, f32[32,8,256]{2,1,0:T(8,128)S(1)}, u32[]{:S(2)}, u32[]{:S(2)}) collective-permute-start(f32[32,8,256]{2,1,0:T(8,128)S(1)} %get-tuple-element.56), channel_id=1, source_target_pairs={{0,1},{2,3},{1,0},{3,2},{4,5},{6,7},{5,4},{7,6},{8,9},{10,11},{9,8... | collective-permute-start | bytes 786440 | tf_op jit(solution)/shard_map/ppermute | solution.py:410
  17.5 3.0 %collective-permute-start.6 = (f32[16,8,256]{2,1,0:T(8,128)S(1)}, f32[16,8,256]{2,1,0:T(8,128)S(1)}, u32[]{:S(2)}, u32[]{:S(2)}) collective-permute-start(f32[16,8,256]{2,1,0:T(8,128)S(1)} %get-tuple-element.57), channel_id=1, source_target_pairs={{1,2},{2,1},{5,6},{6,5},{9,10},{10,9},{13,14},{14,13},{17,18},{18,... | collective-permute-start | bytes 393224 | tf_op jit(solution)/shard_map/ppermute | solution.py:410
  20.5 2.5 %collective-permute-start.10 = (f32[16,8,256]{2,1,0:T(8,128)S(1)}, f32[16,8,256]{2,1,0:T(8,128)S(1)}, u32[]{:S(2)}, u32[]{:S(2)}) collective-permute-start(f32[16,8,256]{2,1,0:T(8,128)S(1)} %get-tuple-element.64), channel_id=1, source_target_pairs={{1,2},{2,1},{5,6},{6,5},{9,10},{10,9},{13,14},{14,13},{17,18},{18,... | collective-permute-start | bytes 393224 | tf_op jit(solution)/shard_map/ppermute | solution.py:410
  23.0 0.5 %inner.1._ = f32[32,16,256]{2,1,0:T(8,128)S(1)} custom-call(f32[32,16,256]{2,1,0:T(8,128)S(1)} %get-tuple-element.52.p1, bf16[512,256]{1,0:T(8,128)(2,1)S(1)} %get-tuple-element.53.along_y, bf16[256,512]{1,0:T(8,128)(2,1)S(1)} %get-tuple-element.54.along_xz, bf16[2,256,128]{2,1,0:T(8,128)(2,1)S(1)} %get-tuple-element.55.across), custom_call_target="tpu_custom_call" | custom-call | tf_op jit(solution)/shard_map/inner/pallas_call | solution.py:46
  23.5 0.5 %collective-permute-done.6.other = f32[16,8,256]{2,1,0:T(8,128)S(1)} collective-permute-done((f32[16,8,256]{2,1,0:T(8,128)S(1)}, f32[16,8,256]{2,1,0:T(8,128)S(1)}, u32[]{:S(2)}, u32[]{:S(2)}) %collective-permute-start.6) | collective-permute-done | bytes 131104 | tf_op jit(solution)/shard_map/ppermute | solution.py:410
  24.0 0.0 collective-permute-done.5.pair
  24.0 0.4 %image.1 = (f32[32,16,256]{2,1,0:T(8,128)S(1)}, f32[8,16,256]{2,1,0:T(8,128)S(1)}, f32[8,16,256]{2,1,0:T(8,128)S(1)}, f32[8,16,256]{2,1,0:T(8,128)S(1)}, f32[8,16,256]{2,1,0:T(8,128)S(1)}) custom-call(s32[1]{0:T(128)S(6)} %copy.19.anchors, s32[1,3]{1,0:T(1,128)S(4)} %get-tuple-element.36.cells, ...), custom_call_target="tpu_custom_call", output_to_operand_aliasing={{0}: (7, {})} | custom-call | tf_op jit(solution)/shard_map/image/pallas_call | solution.py:46
  24.4 0.8 %collective-permute-start.7 = (f32[8,16,256]{2,1,0:T(8,128)S(1)}, f32[8,16,256]{2,1,0:T(8,128)S(1)}, u32[]{:S(2)}, u32[]{:S(2)}) collective-permute-start(f32[8,16,256]{2,1,0:T(8,128)S(1)} %get-tuple-element.59), channel_id=1, source_target_pairs={{0,8},{4,12},{8,0},{12,4},{1,9},{5,13},{9,1},{13,5},{2,10},{6,14},... | collective-permute-start | bytes 393224 | tf_op jit(solution)/shard_map/ppermute | solution.py:498
  25.2 1.5 %collective-permute-start.8 = (f32[8,16,256]{2,1,0:T(8,128)S(1)}, f32[8,16,256]{2,1,0:T(8,128)S(1)}, u32[]{:S(2)}, u32[]{:S(2)}) collective-permute-start(f32[8,16,256]{2,1,0:T(8,128)S(1)} %get-tuple-element.60), channel_id=1, source_target_pairs={{0,12},{4,8},{8,4},{12,0},{1,13},{5,9},{9,5},{13,1},{2,14},{6,10},... | collective-permute-start | bytes 393224 | tf_op jit(solution)/shard_map/ppermute | solution.py:498
  26.7 0.4 %collective-permute-start.9 = (f32[8,16,256]{2,1,0:T(8,128)S(1)}, f32[8,16,256]{2,1,0:T(8,128)S(1)}, u32[]{:S(2)}, u32[]{:S(2)}) collective-permute-start(f32[8,16,256]{2,1,0:T(8,128)S(1)} %get-tuple-element.61), channel_id=1, source_target_pairs={{0,4},{4,0},{8,12},{12,8},{1,5},{5,1},{9,13},{13,9},{2,6},{6,2},{1... | collective-permute-start | bytes 393224 | tf_op jit(solution)/shard_map/ppermute | solution.py:498
  27.1 0.0 collective-permute-done.10.other
  27.1 1.8 %last.1 = (f32[1,2,32,16,256]{4,3,2,1,0:T(8,128)}, f32[1,2,32,16,256]{4,3,2,1,0:T(8,128)}) custom-call(s32[1,3]{1,0:T(1,128)S(4)} %get-tuple-element.36.cells, f32[1,2]{1,0:T(1,128)S(4)} %get-tuple-element.37.amounts, f32[32,16,256]{2,1,0:T(8,128)S(1)} %get-tuple-element.39.p.p0, f32[32,16,256]{2,1,0:T(8,128)S(1)} %get-tuple-element.52.p1, ...), custom_call_target="tpu_custom_call" | custom-call | flops 10000000000 | bytes 100000000 | tf_op jit(solution)/shard_map/last/pallas_call | solution.py:46
  28.9 4.6 %collective-permute-done.7.refs_1_ = f32[8,16,256]{2,1,0:T(8,128)S(1)} collective-permute-done((f32[8,16,256]{2,1,0:T(8,128)S(1)}, f32[8,16,256]{2,1,0:T(8,128)S(1)}, u32[]{:S(2)}, u32[]{:S(2)}) %collective-permute-start.7) | collective-permute-done | bytes 131104 | tf_op jit(solution)/shard_map/ppermute | solution.py:498
  33.4 0.0 collective-permute-done.8.refs_2_
  33.4 0.0 collective-permute-done.9.refs_3_
  33.4 0.7 %gradient.1 = f32[8,16,256]{2,1,0:T(8,128)} custom-call(f32[8,16,256]{2,1,0:T(8,128)S(1)} %get-tuple-element.35.refs_0_.velocity, f32[8,16,256]{2,1,0:T(8,128)S(1)} %get-tuple-element.58.refs_0_, f32[8,16,256]{2,1,0:T(8,128)S(1)} %collective-permute-done.7.refs_1_, f32[8,16,256]{2,1,0:T(8,128)S(1)} %collective-permute-done.8.refs_2_, ...), custom_call_target="tpu_custom_call" | custom-call | tf_op jit(solution)/shard_map/gradient/pallas_call | solution.py:46
Async XLA Ops:
  0.6 15.7 %collective-permute-start.2 = (f32[8,16,256]{2,1,0:T(8,128)}, f32[8,16,256]{2,1,0:T(8,128)S(1)}, u32[]{:S(2)}, u32[]{:S(2)}) collective-permute-start(f32[8,16,256]{2,1,0:T(8,128)} %velocity.1), channel_id=1, source_target_pairs={{0,12},{4,8},{8,4},{12,0},{1,13},{5,9},{9,5},{13,1},{2,14},{6,10},... | collective-permute-start | bytes 393224 | tf_op jit(solution)/shard_map/ppermute | solution.py:424
  4.8 11.5 %collective-permute-start.4 = (f32[8,16,256]{2,1,0:T(8,128)}, f32[8,16,256]{2,1,0:T(8,128)S(1)}, u32[]{:S(2)}, u32[]{:S(2)}) collective-permute-start(f32[8,16,256]{2,1,0:T(8,128)} %velocity.1), channel_id=1, source_target_pairs={{0,8},{4,12},{8,0},{12,4},{1,9},{5,13},{9,1},{13,5},{2,10},{6,14},... | collective-permute-start | bytes 393224 | tf_op jit(solution)/shard_map/ppermute | solution.py:424
  4.8 11.5 %collective-permute-start.3 = (f32[8,16,256]{2,1,0:T(8,128)}, f32[8,16,256]{2,1,0:T(8,128)S(1)}, u32[]{:S(2)}, u32[]{:S(2)}) collective-permute-start(f32[8,16,256]{2,1,0:T(8,128)} %velocity.1), channel_id=1, source_target_pairs={{0,4},{4,0},{8,12},{12,8},{1,5},{5,1},{9,13},{13,9},{2,6},{6,2},{1... | collective-permute-start | bytes 393224 | tf_op jit(solution)/shard_map/ppermute | solution.py:424
  6.6 7.6 %collective-permute-start = (f32[32,8,256]{2,1,0:T(8,128)S(1)}, f32[32,8,256]{2,1,0:T(8,128)S(1)}, u32[]{:S(2)}, u32[]{:S(2)}) collective-permute-start(f32[32,8,256]{2,1,0:T(8,128)S(1)} %get-tuple-element.45), channel_id=1, source_target_pairs={{0,1},{2,3},{1,0},{3,2},{4,5},{6,7},{5,4},{7,6},{8,9},{10,11},{9,8... | collective-permute-start | bytes 786440 | tf_op jit(solution)/shard_map/ppermute | solution.py:410
  7.9 8.0 %collective-permute-start.1 = (f32[32,8,256]{2,1,0:T(8,128)S(1)}, f32[32,8,256]{2,1,0:T(8,128)S(1)}, u32[]{:S(2)}, u32[]{:S(2)}) collective-permute-start(f32[32,8,256]{2,1,0:T(8,128)S(1)} %get-tuple-element.46), channel_id=1, source_target_pairs={{1,2},{2,1},{5,6},{6,5},{9,10},{10,9},{13,14},{14,13},{17,18},{18,... | collective-permute-start | bytes 786440 | tf_op jit(solution)/shard_map/ppermute | solution.py:410
  16.7 7.4 %collective-permute-start.5 = (f32[32,8,256]{2,1,0:T(8,128)S(1)}, f32[32,8,256]{2,1,0:T(8,128)S(1)}, u32[]{:S(2)}, u32[]{:S(2)}) collective-permute-start(f32[32,8,256]{2,1,0:T(8,128)S(1)} %get-tuple-element.56), channel_id=1, source_target_pairs={{0,1},{2,3},{1,0},{3,2},{4,5},{6,7},{5,4},{7,6},{8,9},{10,11},{9,8... | collective-permute-start | bytes 786440 | tf_op jit(solution)/shard_map/ppermute | solution.py:410
  17.5 6.6 %collective-permute-start.6 = (f32[16,8,256]{2,1,0:T(8,128)S(1)}, f32[16,8,256]{2,1,0:T(8,128)S(1)}, u32[]{:S(2)}, u32[]{:S(2)}) collective-permute-start(f32[16,8,256]{2,1,0:T(8,128)S(1)} %get-tuple-element.57), channel_id=1, source_target_pairs={{1,2},{2,1},{5,6},{6,5},{9,10},{10,9},{13,14},{14,13},{17,18},{18,... | collective-permute-start | bytes 393224 | tf_op jit(solution)/shard_map/ppermute | solution.py:410
  20.5 6.6 %collective-permute-start.10 = (f32[16,8,256]{2,1,0:T(8,128)S(1)}, f32[16,8,256]{2,1,0:T(8,128)S(1)}, u32[]{:S(2)}, u32[]{:S(2)}) collective-permute-start(f32[16,8,256]{2,1,0:T(8,128)S(1)} %get-tuple-element.64), channel_id=1, source_target_pairs={{1,2},{2,1},{5,6},{6,5},{9,10},{10,9},{13,14},{14,13},{17,18},{18,... | collective-permute-start | bytes 393224 | tf_op jit(solution)/shard_map/ppermute | solution.py:410
  24.4 9.0 %collective-permute-start.7 = (f32[8,16,256]{2,1,0:T(8,128)S(1)}, f32[8,16,256]{2,1,0:T(8,128)S(1)}, u32[]{:S(2)}, u32[]{:S(2)}) collective-permute-start(f32[8,16,256]{2,1,0:T(8,128)S(1)} %get-tuple-element.59), channel_id=1, source_target_pairs={{0,8},{4,12},{8,0},{12,4},{1,9},{5,13},{9,1},{13,5},{2,10},{6,14},... | collective-permute-start | bytes 393224 | tf_op jit(solution)/shard_map/ppermute | solution.py:498
  25.2 8.3 %collective-permute-start.8 = (f32[8,16,256]{2,1,0:T(8,128)S(1)}, f32[8,16,256]{2,1,0:T(8,128)S(1)}, u32[]{:S(2)}, u32[]{:S(2)}) collective-permute-start(f32[8,16,256]{2,1,0:T(8,128)S(1)} %get-tuple-element.60), channel_id=1, source_target_pairs={{0,12},{4,8},{8,4},{12,0},{1,13},{5,9},{9,5},{13,1},{2,14},{6,10},... | collective-permute-start | bytes 393224 | tf_op jit(solution)/shard_map/ppermute | solution.py:498
  26.7 6.7 %collective-permute-start.9 = (f32[8,16,256]{2,1,0:T(8,128)S(1)}, f32[8,16,256]{2,1,0:T(8,128)S(1)}, u32[]{:S(2)}, u32[]{:S(2)}) collective-permute-start(f32[8,16,256]{2,1,0:T(8,128)S(1)} %get-tuple-element.61), channel_id=1, source_target_pairs={{0,4},{4,0},{8,12},{12,8},{1,5},{5,1},{9,13},{13,9},{2,6},{6,2},{1... | collective-permute-start | bytes 393224 | tf_op jit(solution)/shard_map/ppermute | solution.py:498
